TPU v7x, 128 devices: a whole 4x4x4 slice. The times are simulated.
128 devices in a mesh: fy: 8 (over y, core), fx: 16 (over x, z).
Axes of the slice: x: 4, y: 4, z: 4, core: 2. Of those that a mesh axis runs over, the one named last changes fastest.
Arguments:
- sky_image: float32 [8, 2048, 4096], P(None, 'fy', 'fx'), may hold values from 0 to 2
- vis_tiles: bfloat16 [2048, 2, 256, 256], P(('fy', 'fx')), may hold values from -6 to 6
- tile_dest: int32 [2048, 1], P(('fy', 'fx')), may hold values from 0 to 15; in each aligned block of 16 rows (0 to 15, 16 to 31, ...) at most 2 rows name the same one
- tile_chan: int32 [2048], P(('fy', 'fx')), may hold values from 0 to 7
- tile_count: int32 [2048], P(('fy', 'fx')), may hold values from 1 to 255
- thresholds: bfloat16 [8, 8, 2048, 4096], P(None, None, 'fy', 'fx'), may hold values from 0.0099487305 to 1
Outputs:
- new_image: float32 [8, 2048, 4096], P(None, 'fy', 'fx')
Inputs may be any that keep to these rules, and one draw needn't show every extreme that they name: `tile_dest`: of the tiles of one device, at most 2 name one facet column, and some device has exactly 2 naming one.
All inputs are finite; a program needn't handle non-finite values.
Results may differ from a plain program's by a relative error of at most 0.0073.
Values may be sent and summed in bfloat16 or wider, within the bound.
A program may use at most 192 MiB of HBM per device.

v0:
```python
import math

import jax
import jax.numpy as jnp
import numpy as np
from jax import lax
from jax.sharding import PartitionSpec as P

daubechies_taps = [
    [0.7071067811865476, 0.7071067811865476],
    [0.48296291314469025, 0.836516303737469, 0.22414386804185735, -0.12940952255092145],
    [
        0.3326705529509569,
        0.8068915093133388,
        0.4598775021193313,
        -0.13501102001039084,
        -0.08544127388224149,
        0.035226291882100656,
    ],
    [
        0.23037781330885523,
        0.7148465705525415,
        0.6308807679295904,
        -0.02798376941698385,
        -0.18703481171888114,
        0.030841381835986965,
        0.032883011666982945,
        -0.010597401784997278,
    ],
    [
        0.160102397974125,
        0.6038292697974729,
        0.7243085284385744,
        0.13842814590110342,
        -0.24229488706619015,
        -0.03224486958502952,
        0.07757149384006515,
        -0.006241490213011705,
        -0.012580751999015526,
        0.003335725285001549,
    ],
    [
        0.11154074335008017,
        0.4946238903983854,
        0.7511339080215775,
        0.3152503517092432,
        -0.22626469396516913,
        -0.12976686756709563,
        0.09750160558707936,
        0.02752286553001629,
        -0.031582039318031156,
        0.0005538422009938016,
        0.004777257511010651,
        -0.00107730108499558,
    ],
    [
        0.07785205408506236,
        0.39653931948230575,
        0.7291320908465551,
        0.4697822874053586,
        -0.14390600392910627,
        -0.22403618499416572,
        0.07130921926705004,
        0.0806126091510659,
        -0.03802993693503463,
        -0.01657454163101562,
        0.012550998556013784,
        0.00042957797300470274,
        -0.0018016407039998328,
        0.0003537138000010399,
    ],
    [
        0.05441584224308161,
        0.3128715909144659,
        0.6756307362980128,
        0.5853546836548691,
        -0.015829105256023893,
        -0.2840155429624281,
        0.00047248457399797254,
        0.128747426620186,
        -0.01736930100202211,
        -0.04408825393106472,
        0.013981027917015516,
        0.008746094047015655,
        -0.00487035299301066,
        -0.0003917403729959771,
        0.0006754494059985568,
        -0.00011747678400228192,
    ],
]


def passed_along(value, axis, by):
    devices = lax.axis_size(axis)
    return lax.ppermute(value, axis, [(i, (i + by) % devices) for i in range(devices)])


def daubechies_bank():
    low_rows = np.zeros((8, 16))
    high_rows = np.zeros((8, 16))
    for degree in range(1, 9):
        filter_taps = np.array(daubechies_taps[degree - 1])
        filter_taps = filter_taps * math.sqrt(2.0) / np.sum(filter_taps)
        length = 2 * degree
        low_rows[degree - 1, :length] = filter_taps
        high_rows[degree - 1, :length] = [
            (-1.0) ** position * filter_taps[length - 1 - position] for position in range(length)
        ]
    return (low_rows, high_rows)


def band_table(filter_taps, offsets):
    picks = (offsets[:, :, None] == jnp.arange(16, dtype=jnp.int32)[None, None, :]).astype(
        jnp.float32
    )
    return jnp.einsum("bj,rcj->brc", filter_taps, picks, precision=lax.Precision.HIGHEST)


def wavelet_tables(facet_side):
    low_bank, high_bank = daubechies_bank()
    lows = jnp.asarray(low_bank, jnp.float32).astype(jnp.bfloat16).astype(jnp.float32)
    highs = jnp.asarray(high_bank, jnp.float32).astype(jnp.bfloat16).astype(jnp.float32)
    half_side = facet_side // 2
    quarter = facet_side // 4
    cells_ext = jnp.arange(facet_side + 48, dtype=jnp.int32)
    coarse_ext = jnp.arange(half_side + 16, dtype=jnp.int32)
    approx_rows = jnp.arange(half_side + 16, dtype=jnp.int32)
    detail_rows = jnp.arange(half_side, dtype=jnp.int32)
    second_rows = jnp.arange(quarter, dtype=jnp.int32)
    analysis_one = jnp.concatenate(
        [
            band_table(lows, cells_ext[None, :] - 2 * approx_rows[:, None]),
            band_table(highs, cells_ext[None, :] - 2 * detail_rows[:, None]),
        ],
        axis=1,
    )
    analysis_two = jnp.concatenate(
        [
            band_table(lows, coarse_ext[None, :] - 2 * second_rows[:, None]),
            band_table(highs, coarse_ext[None, :] - 2 * second_rows[:, None]),
        ],
        axis=1,
    )
    up_rows = jnp.arange(half_side + 8, dtype=jnp.int32)
    up_cols = jnp.arange(quarter + 16, dtype=jnp.int32)
    offset_two = up_rows[:, None] - 2 * up_cols[None, :] + 24
    synthesis_two = jnp.concatenate(
        [band_table(lows, offset_two), band_table(highs, offset_two)], axis=2
    )
    cell_rows = jnp.arange(facet_side, dtype=jnp.int32)
    offset_one = cell_rows[:, None] - 2 * up_rows[None, :] + 16
    synthesis_one = jnp.concatenate(
        [band_table(lows, offset_one), band_table(highs, offset_one)], axis=2
    )
    return (
        analysis_one.astype(jnp.bfloat16),
        analysis_two.astype(jnp.bfloat16),
        synthesis_two.astype(jnp.bfloat16),
        synthesis_one.astype(jnp.bfloat16),
    )


def fourier_tables(facet_side):
    grid = (
        jnp.arange(facet_side, dtype=jnp.int32)[:, None]
        * jnp.arange(facet_side, dtype=jnp.int32)[None, :]
        % facet_side
    )
    angle = grid.astype(jnp.float32) * (2.0 * math.pi / facet_side)
    scale = 1.0 / math.sqrt(facet_side)
    return (
        (jnp.cos(angle) * scale).astype(jnp.bfloat16),
        (jnp.sin(angle) * scale).astype(jnp.bfloat16),
    )


def analyze_rows(tall_block, analysis_one, analysis_two, split_at):
    level_one = jnp.einsum(
        "brn,cnw->bcrw", analysis_one, tall_block, preferred_element_type=jnp.float32
    )
    approx = level_one[:, :, :split_at].astype(jnp.bfloat16)
    level_two = jnp.einsum(
        "brm,bcmw->bcrw", analysis_two, approx, preferred_element_type=jnp.float32
    )
    return jnp.concatenate([level_two, level_one[:, :, split_at:]], axis=2).astype(jnp.bfloat16)


def per_device(sky_image, vis_tiles, tile_dest, tile_chan, tile_count, thresholds):
    columns_fx = lax.axis_size("fx")
    tiles_here = vis_tiles.shape[0]
    capacity = 2 * tiles_here // columns_fx
    channels = sky_image.shape[0]
    facet_side = sky_image.shape[1]
    slot_total = columns_fx * capacity
    target = tile_dest[:, 0]
    order_row = lax.broadcasted_iota(jnp.int32, (tiles_here, tiles_here), 0)
    order_col = lax.broadcasted_iota(jnp.int32, (tiles_here, tiles_here), 1)
    same_target = target[:, None] == target[None, :]
    slot_rank = jnp.sum(jnp.where(same_target & (order_col < order_row), 1, 0), axis=1)
    slot_of = target * capacity + slot_rank
    picked = jnp.arange(slot_total, dtype=jnp.int32)[:, None] == slot_of[None, :]
    outgoing = jnp.einsum(
        "si,ixuv->sxuv", picked.astype(jnp.bfloat16), vis_tiles, preferred_element_type=jnp.float32
    ).astype(jnp.bfloat16)
    outgoing = outgoing.reshape(columns_fx, capacity, 2, facet_side, facet_side)
    sent_count = jnp.sum(jnp.where(picked, tile_count[None, :], 0), axis=1).reshape(
        columns_fx, capacity
    )
    sent_chan = jnp.sum(jnp.where(picked, tile_chan[None, :], 0), axis=1).reshape(
        columns_fx, capacity
    )
    arrived, got_count, got_chan = (
        lax.all_to_all(outgoing, "fx", split_axis=0, concat_axis=0, tiled=True),
        lax.all_to_all(sent_count, "fx", split_axis=0, concat_axis=0, tiled=True),
        lax.all_to_all(sent_chan, "fx", split_axis=0, concat_axis=0, tiled=True),
    )
    weight = got_count.reshape(slot_total).astype(jnp.float32) / 64.0
    member = got_chan.reshape(slot_total)[:, None] == jnp.arange(channels, dtype=jnp.int32)[None, :]
    slot_share = jnp.where(member, weight[:, None], 0.0)
    totals = jnp.sum(slot_share, axis=0)
    gathered = jnp.einsum(
        "sc,sxuv->cxuv",
        slot_share.astype(jnp.bfloat16),
        arrived.reshape(slot_total, 2, facet_side, facet_side),
        preferred_element_type=jnp.float32,
    )
    cosine, sine_table = fourier_tables(facet_side)
    pixels = sky_image.astype(jnp.bfloat16)
    half_re = jnp.einsum("cyx,xv->cyv", pixels, cosine, preferred_element_type=jnp.float32).astype(
        jnp.bfloat16
    )
    half_im = (
        -jnp.einsum("cyx,xv->cyv", pixels, sine_table, preferred_element_type=jnp.float32)
    ).astype(jnp.bfloat16)
    model_re = jnp.einsum(
        "uy,cyv->cuv", cosine, half_re, preferred_element_type=jnp.float32
    ) + jnp.einsum("uy,cyv->cuv", sine_table, half_im, preferred_element_type=jnp.float32)
    model_im = jnp.einsum(
        "uy,cyv->cuv", cosine, half_im, preferred_element_type=jnp.float32
    ) - jnp.einsum("uy,cyv->cuv", sine_table, half_re, preferred_element_type=jnp.float32)
    resid_re = (totals[:, None, None] * model_re - gathered[:, 0]).astype(jnp.bfloat16)
    resid_im = (totals[:, None, None] * model_im - gathered[:, 1]).astype(jnp.bfloat16)
    back_re = (
        jnp.einsum("uy,cuv->cyv", cosine, resid_re, preferred_element_type=jnp.float32)
        - jnp.einsum("uy,cuv->cyv", sine_table, resid_im, preferred_element_type=jnp.float32)
    ).astype(jnp.bfloat16)
    back_im = (
        jnp.einsum("uy,cuv->cyv", cosine, resid_im, preferred_element_type=jnp.float32)
        + jnp.einsum("uy,cuv->cyv", sine_table, resid_re, preferred_element_type=jnp.float32)
    ).astype(jnp.bfloat16)
    gradient = jnp.einsum(
        "cyv,xv->cyx", back_re, cosine, preferred_element_type=jnp.float32
    ) - jnp.einsum("cyv,xv->cyx", back_im, sine_table, preferred_element_type=jnp.float32)
    stepped = (sky_image - gradient / (1.0 + totals[:, None, None])).astype(jnp.bfloat16)
    analysis_one, analysis_two, synthesis_two, synthesis_one = wavelet_tables(facet_side)
    split_at = facet_side // 2 + 16
    rows_below = passed_along(stepped[:, :48, :], "fy", -1)
    tall_block = jnp.concatenate([stepped, rows_below], axis=1)
    row_section = analyze_rows(tall_block, analysis_one, analysis_two, split_at)
    beside = passed_along(row_section[..., :48], "fx", -1)
    framed = jnp.concatenate([row_section, beside], axis=3)
    level_one = jnp.einsum(
        "bcyn,brn->bcyr", framed, analysis_one, preferred_element_type=jnp.float32
    )
    approx = level_one[..., :split_at].astype(jnp.bfloat16)
    level_two = jnp.einsum(
        "bcym,brm->bcyr", approx, analysis_two, preferred_element_type=jnp.float32
    )
    coefficient = jnp.concatenate([level_two, level_one[..., split_at:]], axis=3)
    limits = thresholds.astype(jnp.float32)
    shrunk = (jnp.sign(coefficient) * jnp.maximum(jnp.abs(coefficient) - limits, 0.0)).astype(
        jnp.bfloat16
    )
    quarter = facet_side // 4
    half_side = facet_side // 2
    edge_cols = jnp.concatenate(
        [
            shrunk[..., quarter - 16 : quarter],
            shrunk[..., half_side - 16 : half_side],
            shrunk[..., facet_side - 8 :],
        ],
        axis=3,
    )
    behind = passed_along(edge_cols, "fx", 1)
    coarse = jnp.concatenate(
        [
            behind[..., :16],
            shrunk[..., :quarter],
            behind[..., 16:32],
            shrunk[..., quarter:half_side],
        ],
        axis=3,
    )
    approx_up = jnp.einsum(
        "bcym,bkm->bcyk", coarse, synthesis_two, preferred_element_type=jnp.float32
    ).astype(jnp.bfloat16)
    fine_part = jnp.concatenate([approx_up, behind[..., 32:], shrunk[..., half_side:]], axis=3)
    col_section = jnp.einsum(
        "bcyk,bnk->bcyn", fine_part, synthesis_one, preferred_element_type=jnp.float32
    ).astype(jnp.bfloat16)
    edge_rows = jnp.concatenate(
        [
            col_section[:, :, quarter - 16 : quarter],
            col_section[:, :, half_side - 16 : half_side],
            col_section[:, :, facet_side - 8 :],
        ],
        axis=2,
    )
    rows_above = passed_along(edge_rows, "fy", 1)
    coarse_rows = jnp.concatenate(
        [
            rows_above[:, :, :16],
            col_section[:, :, :quarter],
            rows_above[:, :, 16:32],
            col_section[:, :, quarter:half_side],
        ],
        axis=2,
    )
    approx_rows = jnp.einsum(
        "bkm,bcmx->bckx", synthesis_two, coarse_rows, preferred_element_type=jnp.float32
    ).astype(jnp.bfloat16)
    fine_rows = jnp.concatenate(
        [approx_rows, rows_above[:, :, 32:], col_section[:, :, half_side:]], axis=2
    )
    cell_terms = jnp.einsum(
        "bnk,bckx->bcnx", synthesis_one, fine_rows, preferred_element_type=jnp.float32
    )
    bases_count = analysis_one.shape[0]
    return jnp.maximum(jnp.sum(cell_terms, axis=0) / bases_count, 0.0)


def solution(mesh):
    in_specs = (
        P(None, "fy", "fx"),
        P(("fy", "fx"), None, None, None),
        P(("fy", "fx"), None),
        P(("fy", "fx")),
        P(("fy", "fx")),
        P(None, None, "fy", "fx"),
    )
    out_specs = P(None, "fy", "fx")
    return jax.shard_map(
        per_device, mesh=mesh, in_specs=in_specs, out_specs=out_specs, check_vma=False
    )
```

profile of v0, /device:TPU:1, one launch (start us, length us, event | category | flops | bytes accessed | tf_op | source)
XLA Modules:
  0.0 423.1 jit_solution(3010874234675520960)
XLA Ops:
  3.0 8.4 %all-to-all-start = ((s32[16,1,2]{2,1,0:T(1,128)}), s32[16,1,2]{2,1,0:T(1,128)S(1)}, u32[]{:S(2)}, u32[]{:S(2)}) async-start(s32[16,1,2]{2,1,0:T(1,128)} %bitcast.1), calls=%async_computation | async-start | bytes 16384 | tf_op jit(solution)/shard_map/all_to_all | solution.py:215
  11.5 8.4 %convolution_convert_fusion = bf16[32,2,256,256]{3,0,2,1:T(8,128)(2,1)} fusion(bf16[16,2,256,256]{3,2,1,0:T(8,128)(2,1)} %param.9, s32[16]{0:T(128)S(1)} %multiply_add_fusion), kind=kOutput, calls=%fused_computation.20 | convolution fusion | flops 138412544 | bytes 12582976 | tf_op jit(solution)/shard_map/si,ixuv->sxuv/dot_general | solution.py:202
  20.5 6.7 %all-to-all-start.1 = ((s32[16,1,2]{2,1,0:T(1,128)}), s32[16,1,2]{2,1,0:T(1,128)S(1)}, u32[]{:S(2)}, u32[]{:S(2)}) async-start(s32[16,1,2]{2,1,0:T(1,128)} %bitcast.2), calls=%async_computation.1 | async-start | bytes 16384 | tf_op jit(solution)/shard_map/all_to_all | solution.py:214
  27.2 13.1 %reshape.168 = bf16[16,2,2,256,256]{4,1,0,3,2:T(2,128)(2,1)} reshape(bf16[32,2,256,256]{3,0,2,1:T(8,128)(2,1)} %convolution_convert_fusion) | data formatting | bytes 16777216 | tf_op jit(solution)/shard_map/reshape | solution.py:205
  40.3 8.0 %copy.112 = bf16[16,2,2,256,256]{4,1,3,2,0:T(2,128)(2,1)} copy(bf16[16,2,2,256,256]{4,1,0,3,2:T(2,128)(2,1)} %reshape.168) | data formatting | bytes 16777216 | tf_op jit(solution)/shard_map/reshape | solution.py:205
  48.3 6.9 %all-to-all-start.2 = ((bf16[16,2,2,256,256]{4,1,3,2,0:T(2,128)(2,1)}), bf16[16,2,2,256,256]{4,1,3,2,0:T(2,128)(2,1)}, u32[]{:S(2)}, u32[]{:S(2)}) async-start(bf16[16,2,2,256,256]{4,1,3,2,0:T(2,128)(2,1)} %copy.112), calls=%async_computation.2 | async-start | bytes 16777216 | tf_op jit(solution)/shard_map/all_to_all | solution.py:213
  70.2 116.0 %all-to-all-done.2 = bf16[16,2,2,256,256]{4,1,3,2,0:T(2,128)(2,1)} async-done(((bf16[16,2,2,256,256]{4,1,3,2,0:T(2,128)(2,1)}), bf16[16,2,2,256,256]{4,1,3,2,0:T(2,128)(2,1)}, u32[]{:S(2)}, u32[]{:S(2)}) %all-to-all-start.2) | async-done | bytes 8388640 | tf_op jit(solution)/shard_map/all_to_all | solution.py:213
  186.2 11.0 %copy.113 = bf16[16,2,2,256,256]{4,1,0,3,2:T(2,128)(2,1)} copy(bf16[16,2,2,256,256]{4,1,3,2,0:T(2,128)(2,1)} %all-to-all-done.2) | data formatting | bytes 16777216 | tf_op jit(solution)/shard_map/all_to_all | solution.py:213
  197.1 13.1 %reshape.169 = bf16[32,2,256,256]{3,0,2,1:T(8,128)(2,1)} reshape(bf16[16,2,2,256,256]{4,1,0,3,2:T(2,128)(2,1)} %copy.113) | data formatting | bytes 16777216 | tf_op jit(solution)/shard_map/reshape | solution.py:224
  235.9 4.8 %fusion.57 = f32[8,256,256]{2,1,0:T(8,128)} fusion(f32[8,256,256]{2,1,0:T(8,128)} %fusion.101, bf16[8,256,256]{1,2,0:T(8,128)(2,1)S(1)} %fusion.44), kind=kOutput, calls=%fused_computation.69 | convolution fusion | flops 540016640 | bytes 5242880 | tf_op jit(solution)/shard_map/cyv,xv->cyx/dot_general | solution.py:251
  240.7 5.0 %subtract_convert_fusion = bf16[8,256,256]{2,1,0:T(8,128)(2,1)S(1)} fusion(f32[8,256,256]{2,1,0:T(8,128)} %param.8, f32[8,256,256]{2,1,0:T(8,128)} %fusion.57, f32[8,256,256]{2,1,0:T(8,128)} %fusion.96, bf16[8,256,256]{1,2,0:T(8,128)(2,1)S(1)} %copy-done.6, f32[8]{0:T(128)S(1)} %broadcast_add_fusion), kind=kOutput, calls=%fused_computation.54 | convolution fusion | flops 542113792 | bytes 8388640 | tf_op jit(solution)/shard_map/cyv,xv->cyx/dot_general | solution.py:253
  246.7 4.6 %collective-permute-start = (bf16[8,48,256]{2,1,0:T(8,128)(2,1)S(1)}, bf16[8,48,256]{2,1,0:T(8,128)(2,1)}, u32[]{:S(2)}, u32[]{:S(2)}) collective-permute-start(bf16[8,48,256]{2,1,0:T(8,128)(2,1)S(1)} %slice.109), channel_id=1, source_target_pairs={{0,112},{16,0},{32,16},{48,32},{64,48},{80,64},{96,80},{112,96},{1... | collective-permute-start | bytes 589832 | tf_op jit(solution)/shard_map/ppermute | solution.py:95
  256.0 6.1 %convert_bitcast_fusion = bf16[8,8,272,256]{3,2,0,1:T(8,128)(2,1)S(1)} fusion(bf16[8,272,304]{2,0,1:T(8,128)(2,1)S(1)} %get-tuple-element.18, bf16[8,48,256]{2,1,0:T(8,128)(2,1)} %collective-permute-done, bf16[8,256,256]{2,1,0:T(8,128)(2,1)S(1)} %copy-done.14), kind=kOutput, calls=%fused_computation.18 | convolution fusion | flops 2716467200 | bytes 11481088 | tf_op jit(solution)/shard_map/brn,cnw->bcrw/dot_general | solution.py:178
  269.5 4.7 %copy.123 = bf16[8,8,256,48]{2,3,1,0:T(8,128)(2,1)} copy(bf16[8,8,256,48]{3,2,0,1:T(8,128)(2,1)} %pad_maximum_fusion.3) | data formatting | bytes 3145728 | tf_op jit(solution)/shard_map/slice | solution.py:260
  274.2 11.4 %copy.128 = bf16[8,8,256,256]{2,3,1,0:T(8,128)(2,1)} copy(bf16[8,8,256,256]{3,2,1,0:T(8,128)(2,1)} %param.13) | data formatting | bytes 16777216 | tf_op args[5]
  287.3 22.3 %collective-permute-done.1 = bf16[8,8,256,48]{2,3,1,0:T(8,128)(2,1)} collective-permute-done((bf16[8,8,256,48]{2,3,1,0:T(8,128)(2,1)}, bf16[8,8,256,48]{2,3,1,0:T(8,128)(2,1)}, u32[]{:S(2)}, u32[]{:S(2)}) %collective-permute-start.1) | collective-permute-done | bytes 1572896 | tf_op jit(solution)/shard_map/ppermute | solution.py:95
  309.6 4.7 %copy.124 = bf16[8,8,256,48]{3,2,0,1:T(8,128)(2,1)} copy(bf16[8,8,256,48]{2,3,1,0:T(8,128)(2,1)} %collective-permute-done.1) | data formatting | bytes 3145728 | tf_op jit(solution)/shard_map/ppermute | solution.py:95
  314.3 11.5 %fusion = f32[8,8,256,272]{2,3,1,0:T(8,128)} fusion(bf16[8,272,304,1]{2,0,1,3:T(8,128)(2,1)S(1)} %copy-done.9, bf16[8,8,256,48]{3,2,0,1:T(8,128)(2,1)} %copy.124, bf16[8,8,128,256]{3,2,0,1:T(8,128)(2,1)} %copy-done.1, bf16[8,8,128,256]{3,2,0,1:T(8,128)(2,1)} %copy-done.4), kind=kOutput, calls=%fused_computation.3 | convolution fusion | flops 2739404800 | bytes 29110272 | tf_op jit(solution)/shard_map/bcyn,brn->bcyr/dot_general | solution.py:262
  325.8 7.8 %slice.113 = f32[8,8,256,128]{2,3,1,0:T(8,128)} slice(f32[8,8,256,272]{2,3,1,0:T(8,128)} %fusion), slice={[0:8], [0:8], [0:256], [144:272]} | slice | bytes 16777216 | tf_op jit(solution)/shard_map/slice | solution.py:269
  333.6 8.4 %fusion.27 = f32[8,8,256,128]{2,3,1,0:T(8,128)} fusion(f32[8,8,256,272]{2,3,1,0:T(8,128)} %fusion, bf16[8,128,144,1]{2,0,1,3:T(8,128)(2,1)S(1)} %get-tuple-element.27), kind=kOutput, calls=%fused_computation.32 | convolution fusion | flops 603979776 | bytes 13402112 | tf_op jit(solution)/shard_map/bcym,brm->bcyr/dot_general | solution.py:266
  342.0 9.7 %multiply_convert_fusion = bf16[8,8,256,256]{2,3,1,0:T(8,128)(2,1)S(1)} fusion(bf16[8,8,256,256]{2,3,1,0:T(8,128)(2,1)S(1)} %bitcast.139, f32[8,8,256,128]{2,3,1,0:T(8,128)} %slice.113, f32[8,8,256,128]{2,3,1,0:T(8,128)} %fusion.27), kind=kLoop, calls=%fused_computation.1 | loop fusion | flops 33554432 | bytes 33554432 | tf_op jit(solution)/shard_map/convert_element_type | solution.py:271
  355.9 30.2 %collective-permute-done.2 = bf16[8,8,256,40]{2,3,1,0:T(8,128)(2,1)S(1)} collective-permute-done((bf16[8,8,256,40]{2,3,1,0:T(8,128)(2,1)S(1)}, bf16[8,8,256,40]{2,3,1,0:T(8,128)(2,1)S(1)}, u32[]{:S(2)}, u32[]{:S(2)}) %collective-permute-start.2) | collective-permute-done | bytes 1310752 | tf_op jit(solution)/shard_map/ppermute | solution.py:95
  390.2 7.5 %fusion.14 = bf16[8,8,256,256]{3,2,1,0:T(8,128)(2,1)S(1)} fusion(bf16[8,8,256,128]{2,3,1,0:T(8,128)(2,1)S(1)} %slice-done, bf16[8,8,256,8]{2,3,1,0:T(8,128)(2,1)} %slice.121, bf16[8,8,256,136]{2,3,1,0:T(8,128)(2,1)} %fusion.32, bf16[8,256,272,1]{1,0,2,3:T(8,128)(2,1)} %get-tuple-element.24), kind=kOutput, calls=%fused_computation.19 | convolution fusion | flops 2312634368 | bytes 18415616 | tf_op jit(solution)/shard_map/bcyk,bnk->bcyn/dot_general | solution.py:298
  400.2 14.0 %collective-permute-done.3 = bf16[8,8,40,256]{3,2,1,0:T(8,128)(2,1)S(1)} collective-permute-done((bf16[8,8,40,256]{3,2,1,0:T(8,128)(2,1)S(1)}, bf16[8,8,40,256]{3,2,1,0:T(8,128)(2,1)S(1)}, u32[]{:S(2)}, u32[]{:S(2)}) %collective-permute-start.3) | collective-permute-done | bytes 1310752 | tf_op jit(solution)/shard_map/ppermute | solution.py:95
  (114 shorter events, 78.1 us)
Async XLA Ops:
  3.0 17.5 %all-to-all-start = ((s32[16,1,2]{2,1,0:T(1,128)}), s32[16,1,2]{2,1,0:T(1,128)S(1)}, u32[]{:S(2)}, u32[]{:S(2)}) async-start(s32[16,1,2]{2,1,0:T(1,128)} %bitcast.1), calls=%async_computation | async-start | bytes 16384 | tf_op jit(solution)/shard_map/all_to_all | solution.py:215
  20.5 27.8 %all-to-all-start.1 = ((s32[16,1,2]{2,1,0:T(1,128)}), s32[16,1,2]{2,1,0:T(1,128)S(1)}, u32[]{:S(2)}, u32[]{:S(2)}) async-start(s32[16,1,2]{2,1,0:T(1,128)} %bitcast.2), calls=%async_computation.1 | async-start | bytes 16384 | tf_op jit(solution)/shard_map/all_to_all | solution.py:214
  48.3 7.2 %copy-start.15 = (bf16[8,16,1]{1,0,2:T(8,128)(2,1)S(1)}, bf16[8,16,1]{1,0,2:T(8,128)(2,1)}, u32[]{:S(2)}) copy-start(bf16[8,16,1]{1,0,2:T(8,128)(2,1)} %constant.57) | copy-start | bytes 772
  48.3 8.1 %copy-start.16 = (bf16[8,16,1]{1,0,2:T(8,128)(2,1)S(1)}, bf16[8,16,1]{1,0,2:T(8,128)(2,1)}, u32[]{:S(2)}) copy-start(bf16[8,16,1]{1,0,2:T(8,128)(2,1)} %constant.58) | copy-start | bytes 772
  48.3 137.9 %all-to-all-start.2 = ((bf16[16,2,2,256,256]{4,1,3,2,0:T(2,128)(2,1)}), bf16[16,2,2,256,256]{4,1,3,2,0:T(2,128)(2,1)}, u32[]{:S(2)}, u32[]{:S(2)}) async-start(bf16[16,2,2,256,256]{4,1,3,2,0:T(2,128)(2,1)} %copy.112), calls=%async_computation.2 | async-start | bytes 16777216 | tf_op jit(solution)/shard_map/all_to_all | solution.py:213
  55.2 5.1 %copy-start.2 = (f32[8,256,256]{2,1,0:T(8,128)S(1)}, f32[8,256,256]{2,1,0:T(8,128)}, u32[]{:S(2)}) copy-start(f32[8,256,256]{2,1,0:T(8,128)} %param.8) | copy-start | bytes 6291460
  225.0 2.7 copy-start.3
  233.2 7.5 %copy-start.6 = (bf16[8,256,256]{1,2,0:T(8,128)(2,1)S(1)}, bf16[8,256,256]{1,2,0:T(8,128)(2,1)}, u32[]{:S(2)}) copy-start(bf16[8,256,256]{1,2,0:T(8,128)(2,1)} %copy-done.5) | copy-start | bytes 3145732
  240.7 10.6 %copy-start.10 = (bf16[8,64,144]{2,0,1:T(8,128)(2,1)S(1)}, bf16[8,64,144]{2,0,1:T(8,128)(2,1)}, u32[]{:S(2)}) copy-start(bf16[8,64,144]{2,0,1:T(8,128)(2,1)} %fusion.70) | copy-start | bytes 442372
  240.7 10.6 %copy-start.11 = (bf16[8,64,144]{2,0,1:T(8,128)(2,1)S(1)}, bf16[8,64,144]{2,0,1:T(8,128)(2,1)}, u32[]{:S(2)}) copy-start(bf16[8,64,144]{2,0,1:T(8,128)(2,1)} %fusion.71) | copy-start | bytes 442372
  240.7 10.7 %copy-start.8 = (bf16[8,128,304]{1,0,2:T(8,128)(2,1)S(1)}, bf16[8,128,304]{1,0,2:T(8,128)(2,1)}, u32[]{:S(2)}) copy-start(bf16[8,128,304]{1,0,2:T(8,128)(2,1)} %fusion.62) | copy-start | bytes 1867780
  245.7 6.8 %copy-start.7 = (bf16[8,144,304]{2,0,1:T(8,128)(2,1)S(1)}, bf16[8,144,304]{2,0,1:T(8,128)(2,1)}, u32[]{:S(2)}) copy-start(bf16[8,144,304]{2,0,1:T(8,128)(2,1)} %fusion.59) | copy-start | bytes 2101252
  246.7 9.3 %collective-permute-start = (bf16[8,48,256]{2,1,0:T(8,128)(2,1)S(1)}, bf16[8,48,256]{2,1,0:T(8,128)(2,1)}, u32[]{:S(2)}, u32[]{:S(2)}) collective-permute-start(bf16[8,48,256]{2,1,0:T(8,128)(2,1)S(1)} %slice.109), channel_id=1, source_target_pairs={{0,112},{16,0},{32,16},{48,32},{64,48},{80,64},{96,80},{112,96},{1... | collective-permute-start | bytes 589832 | tf_op jit(solution)/shard_map/ppermute | solution.py:95
  252.5 3.5 copy-start.14
  262.7 2.1 copy-start.1
  274.2 35.4 %collective-permute-start.1 = (bf16[8,8,256,48]{2,3,1,0:T(8,128)(2,1)}, bf16[8,8,256,48]{2,3,1,0:T(8,128)(2,1)}, u32[]{:S(2)}, u32[]{:S(2)}) collective-permute-start(bf16[8,8,256,48]{2,3,1,0:T(8,128)(2,1)} %copy.123), channel_id=1, source_target_pairs={{0,15},{1,0},{2,1},{3,2},{4,3},{5,4},{6,5},{7,6},{8,7},{9,8},{10,9... | collective-permute-start | bytes 4718600 | tf_op jit(solution)/shard_map/ppermute | solution.py:95
  285.6 28.7 %copy-start.9 = (bf16[8,272,304,1]{2,0,1,3:T(8,128)(2,1)S(1)}, bf16[8,272,304,1]{2,0,1,3:T(8,128)(2,1)}, u32[]{:S(2)}) copy-start(bf16[8,272,304,1]{2,0,1,3:T(8,128)(2,1)} %get-tuple-element.17) | copy-start | bytes 3969028
  325.8 16.2 %slice-start.1 = ((s8[8388608]{0:T(1024)(128)(4,1)}), s8[4194304]{0:T(1024)(128)(4,1)S(1)}, s32[]{:S(2)}) async-start(s8[8388608]{0:T(1024)(128)(4,1)} %bitcast.138), calls=%async_computation.4 | async-start | bytes 8388608
  333.6 8.4 %slice-start.2 = ((s8[8388608]{0:T(1024)(128)(4,1)}), s8[4194304]{0:T(1024)(128)(4,1)S(1)}, s32[]{:S(2)}) async-start(s8[8388608]{0:T(1024)(128)(4,1)} %bitcast.138), calls=%async_computation.5 | async-start | bytes 8388608
  351.8 3.6 copy-start
  352.0 34.1 %collective-permute-start.2 = (bf16[8,8,256,40]{2,3,1,0:T(8,128)(2,1)S(1)}, bf16[8,8,256,40]{2,3,1,0:T(8,128)(2,1)S(1)}, u32[]{:S(2)}, u32[]{:S(2)}) collective-permute-start(bf16[8,8,256,40]{2,3,1,0:T(8,128)(2,1)S(1)} %pad_maximum_fusion.5), channel_id=1, source_target_pairs={{0,1},{1,2},{2,3},{3,4},{4,5},{5,6},{6,7},{7,8},{8,9},{9,10},{10,1... | collective-permute-start | bytes 3932168 | tf_op jit(solution)/shard_map/ppermute | solution.py:95
  355.4 30.9 %copy-start.12 = (bf16[8,136,160,1]{2,0,1,3:T(8,128)(2,1)S(1)}, bf16[8,136,160,1]{2,0,1,3:T(8,128)(2,1)}, u32[]{:S(2)}) copy-start(bf16[8,136,160,1]{2,0,1,3:T(8,128)(2,1)} %get-tuple-element.26) | copy-start | bytes 1044484
  386.3 3.9 slice-start
  398.0 16.3 %collective-permute-start.3 = (bf16[8,8,40,256]{3,2,1,0:T(8,128)(2,1)S(1)}, bf16[8,8,40,256]{3,2,1,0:T(8,128)(2,1)S(1)}, u32[]{:S(2)}, u32[]{:S(2)}) collective-permute-start(bf16[8,8,40,256]{3,2,1,0:T(8,128)(2,1)S(1)} %pad_maximum_fusion.6), channel_id=1, source_target_pairs={{0,16},{16,32},{32,48},{48,64},{64,80},{80,96},{96,112},{112,0},{1... | collective-permute-start | bytes 3932168 | tf_op jit(solution)/shard_map/ppermute | solution.py:95
  (3 other events, 4.0 us)
where the time goes:
time: 432 us; the launch traced here: 423 us
  waiting for transfers between devices  185 us (43%)
  local copies, waits for them, and re-layouts  95.3 us (22%)
  matrix products  93.7 us (22%)
  starting transfers between devices  28.4 us (7%)
  other arithmetic  20.4 us (5%)
    all_to_all x1, waiting for transfers between devices, per_device(): lax.all_to_all(outgoing, 'fx', split_axis=0, concat_axis=0, tiled=True)  116 us
    ppermute x4, waiting for transfers between devices, passed_along(): lax.ppermute(value, axis, [(i, (i + by) % devices) for i in range(devices)])  68.6 us
    unnamed x41, local copies, waits for them, and re-layouts  21.8 us
    reshape x2, local copies, waits for them, and re-layouts, per_device(): outgoing = outgoing.reshape(columns_fx, capacity, 2, facet_side, facet_side)  21.1 us
    reshape x1, local copies, waits for them, and re-layouts, per_device(): arrived.reshape(slot_total, 2, facet_side, facet_side)  13.1 us
    dot_general x1, matrix products, per_device(): jnp.einsum('bcyn,brn->bcyr', framed, analysis_one, preferred_element_type...  11.5 us
    all_to_all x1, local copies, waits for them, and re-layouts, per_device(): lax.all_to_all(outgoing, 'fx', split_axis=0, concat_axis=0, tiled=True)  11 us
    convert_element_type x1, other arithmetic, per_device(): (jnp.sign(coefficient) * jnp.maximum(jnp.abs(coefficient) - limits, 0.0))...  9.72 us
  transfers between devices with their start and end apart: 7, of which 5 were waited for; matrix products, arithmetic and copies ran while one was open for 15% of the time, Pallas kernels for 0%

commit v1 on v0

v1 whole, which is shorter than its diff:
```python
import functools
import math

import jax
import jax.numpy as jnp
import ml_dtypes
import numpy as np
from jax import lax
from jax.experimental import pallas as pl
from jax.experimental.pallas import tpu as pltpu
from jax.sharding import PartitionSpec as P

daubechies_taps = [
    [0.7071067811865476, 0.7071067811865476],
    [0.48296291314469025, 0.836516303737469, 0.22414386804185735, -0.12940952255092145],
    [
        0.3326705529509569,
        0.8068915093133388,
        0.4598775021193313,
        -0.13501102001039084,
        -0.08544127388224149,
        0.035226291882100656,
    ],
    [
        0.23037781330885523,
        0.7148465705525415,
        0.6308807679295904,
        -0.02798376941698385,
        -0.18703481171888114,
        0.030841381835986965,
        0.032883011666982945,
        -0.010597401784997278,
    ],
    [
        0.160102397974125,
        0.6038292697974729,
        0.7243085284385744,
        0.13842814590110342,
        -0.24229488706619015,
        -0.03224486958502952,
        0.07757149384006515,
        -0.006241490213011705,
        -0.012580751999015526,
        0.003335725285001549,
    ],
    [
        0.11154074335008017,
        0.4946238903983854,
        0.7511339080215775,
        0.3152503517092432,
        -0.22626469396516913,
        -0.12976686756709563,
        0.09750160558707936,
        0.02752286553001629,
        -0.031582039318031156,
        0.0005538422009938016,
        0.004777257511010651,
        -0.00107730108499558,
    ],
    [
        0.07785205408506236,
        0.39653931948230575,
        0.7291320908465551,
        0.4697822874053586,
        -0.14390600392910627,
        -0.22403618499416572,
        0.07130921926705004,
        0.0806126091510659,
        -0.03802993693503463,
        -0.01657454163101562,
        0.012550998556013784,
        0.00042957797300470274,
        -0.0018016407039998328,
        0.0003537138000010399,
    ],
    [
        0.05441584224308161,
        0.3128715909144659,
        0.6756307362980128,
        0.5853546836548691,
        -0.015829105256023893,
        -0.2840155429624281,
        0.00047248457399797254,
        0.128747426620186,
        -0.01736930100202211,
        -0.04408825393106472,
        0.013981027917015516,
        0.008746094047015655,
        -0.00487035299301066,
        -0.0003917403729959771,
        0.0006754494059985568,
        -0.00011747678400228192,
    ],
]


SIDE = 256
CH = 8
BASES = 8
HALO = 48
BF = jnp.bfloat16
F32 = jnp.float32
SEGMENTS = ((48, 64), (112, 128), (240, 256))
SEG_ROWS = 48


def rounded(table):
    return np.asarray(table, np.float32).astype(ml_dtypes.bfloat16)


def composite_tables():
    full = np.zeros((BASES, SIDE, SIDE + HALO))
    for degree in range(1, 9):
        taps = np.array(daubechies_taps[degree - 1])
        taps = taps * math.sqrt(2.0) / np.sum(taps)
        length = 2 * degree
        low = np.zeros(16)
        high = np.zeros(16)
        low[:length] = taps
        high[:length] = [(-1.0) ** j * taps[length - 1 - j] for j in range(length)]
        low = rounded(low).astype(np.float64)
        high = rounded(high).astype(np.float64)
        level_low = np.zeros((144, SIDE + HALO))
        level_high = np.zeros((128, SIDE + HALO))
        for k in range(144):
            level_low[k, 2 * k : 2 * k + 16] = low[: min(16, SIDE + HALO - 2 * k)]
        for k in range(128):
            level_high[k, 2 * k : 2 * k + 16] = high
        second = np.zeros((128, 144))
        for m in range(64):
            second[m, 2 * m : 2 * m + 16] = low
            second[64 + m, 2 * m : 2 * m + 16] = high
        full[degree - 1, :128] = second @ level_low
        full[degree - 1, 128:] = level_high
    return rounded(full).astype(np.float32)


@functools.lru_cache(maxsize=1)
def tables():
    full = composite_tables()
    main = full[:, :, :SIDE]
    over = full[:, :, SIDE:]
    seg = np.concatenate([np.arange(a, b) for a, b in SEGMENTS])
    assert not np.any(np.delete(over, seg, axis=1))
    flat = main.reshape(BASES * SIDE, SIDE)
    out = {"t_cols": flat.T}
    keep = np.setdiff1d(np.arange(SIDE), seg)
    out["inner_rows"] = main[:, keep].reshape(BASES * len(keep), SIDE)
    out["outer_rows"] = full[:, seg].reshape(BASES * SEG_ROWS, SIDE + HALO)
    analyse = np.zeros((BASES, SIDE + 128, SIDE), np.float32)
    analyse[:, : SIDE + HALO] = full.transpose(0, 2, 1)
    out["analyse"] = analyse
    select = np.zeros((BASES * SIDE, 128), np.float32)
    synthesise = np.zeros((BASES, SIDE + 128, SIDE), np.float32)
    synthesise[:, :SIDE] = main
    at = 0
    for b in range(BASES):
        for k in np.nonzero(np.any(over[b] != 0, axis=1))[0]:
            select[b * SIDE + k, at] = 1.0
            synthesise[b, SIDE + at, :HALO] = over[b, k]
            at += 1
    assert at <= 128 and not np.any(over[0])
    out["select"] = select
    out["synthesise"] = synthesise
    top = np.zeros((HALO, 3, BASES - 1, 16), np.float32)
    for i, (a, b) in enumerate(SEGMENTS):
        top[:, i] = over[1:, a:b].transpose(2, 0, 1)
    out["top"] = top.reshape(HALO, 3 * (BASES - 1) * 16)
    grid = np.arange(SIDE)[:, None] * np.arange(SIDE)[None, :] % SIDE
    angle = grid * (2.0 * math.pi / SIDE)
    cosine = rounded(np.cos(angle) / math.sqrt(SIDE)).astype(np.float64)
    sine = rounded(np.sin(angle) / math.sqrt(SIDE)).astype(np.float64)
    out["fourier"] = np.block([[cosine, sine], [-sine, cosine]])
    out["back"] = np.concatenate([cosine, -sine], axis=1)
    out["excess"] = cosine @ cosine + sine @ sine - np.eye(SIDE)
    return {name: rounded(table) for name, table in out.items()}


TABLES = ("t_cols", "inner_rows", "outer_rows", "analyse", "select", "synthesise", "top")


NEAR = ((1, 0), (3, 0), (0, 1), (0, 3), (1, 1), (1, 3), (3, 1), (3, 3))
FAR = ((2, 0), (0, 2), (2, 1), (2, 3), (1, 2), (3, 2), (2, 2))
THROUGH = (
    ((1, 0), (3, 0)),
    ((0, 1), (0, 3)),
    ((1, 1), (3, 1)),
    ((1, 3), (3, 3)),
    ((1, 1), (1, 3)),
    ((3, 1), (3, 3)),
    ((1, 1), (3, 3)),
)


def choose(j, values):
    out = jnp.int32(values[0])
    for i, value in enumerate(values):
        out = jnp.where(j == i, jnp.int32(value), out)
    return out


def dot(a, b):
    return jnp.dot(a, b, preferred_element_type=F32)


def exchange_kernel(
    n_fx,
    dest_ref,
    chan_ref,
    count_ref,
    fourier,
    back,
    excess,
    sky_hbm,
    vis_hbm,
    stepped,
    columns,
    vis,
    sky,
    model,
    sending,
    arrived,
    relay,
    share_ref,
    shares,
    kron,
    load_sem,
    tile_send,
    tile_recv,
    relay_send,
    relay_recv,
    share_send,
    share_recv,
):
    fx = lax.axis_index("fx")
    n_z = 4
    n_x = n_fx // n_z
    my_x, my_z = fx // n_z, fx % n_z

    def at(dx, dz):
        return (my_x + dx) % n_x * n_z + (my_z + dz) % n_z

    def peer(k):
        return at(k // n_z, k % n_z)

    load_vis = pltpu.make_async_copy(vis_hbm, vis, load_sem.at[0])
    load_sky = pltpu.make_async_copy(sky_hbm, sky, load_sem.at[1])
    load_vis.start()
    load_sky.start()

    barrier = pltpu.get_barrier_semaphore()

    def greet(k, carry):
        pl.semaphore_signal(
            barrier, inc=1, device_id={"fx": peer(k)}, device_id_type=pl.DeviceIdType.MESH
        )
        return carry

    lax.fori_loop(1, n_fx, greet, 0)
    pl.semaphore_wait(barrier, n_fx - 1)

    def share_copy(to, source):
        return pltpu.make_async_remote_copy(
            src_ref=share_ref.at[to],
            dst_ref=shares.at[source],
            send_sem=share_send.at[to],
            recv_sem=share_recv.at[source],
            device_id={"fx": to},
            device_id_type=pl.DeviceIdType.MESH,
        )

    def near(j):
        return choose(j, [o[0] for o in NEAR]), choose(j, [o[1] for o in NEAR])

    def far(j):
        return choose(j, [o[0] for o in FAR]), choose(j, [o[1] for o in FAR])

    def through(j, r):
        return (
            choose(j, [o[r][0] for o in THROUGH]),
            choose(j, [o[r][1] for o in THROUGH]),
        )

    def near_copy(j):
        return pltpu.make_async_remote_copy(
            src_ref=sending.at[len(FAR) + j],
            dst_ref=arrived.at[fx],
            send_sem=tile_send.at[len(FAR) + j, 0],
            recv_sem=tile_recv.at[fx, 0],
            device_id={"fx": at(*near(j))},
            device_id_type=pl.DeviceIdType.MESH,
        )

    def far_copy(j, r):
        return pltpu.make_async_remote_copy(
            src_ref=sending.at[j, r],
            dst_ref=relay.at[j, r],
            send_sem=tile_send.at[j, r],
            recv_sem=relay_recv.at[j, r],
            device_id={"fx": at(*through(j, r))},
            device_id_type=pl.DeviceIdType.MESH,
        )

    def relay_copy(j, r):
        end, mid = far(j), through(j, r)
        source = at(4 - mid[0], 4 - mid[1])
        return pltpu.make_async_remote_copy(
            src_ref=relay.at[j, r],
            dst_ref=arrived.at[source, r],
            send_sem=relay_send.at[j, r],
            recv_sem=tile_recv.at[source, r],
            device_id={"fx": at(end[0] + 4 - mid[0], end[1] + 4 - mid[1])},
            device_id_type=pl.DeviceIdType.MESH,
        )

    def near_arrival(j):
        dx, dz = near(j)
        source = at(4 - dx, 4 - dz)
        return pltpu.make_async_remote_copy(
            src_ref=arrived.at[source],
            dst_ref=arrived.at[source],
            send_sem=tile_send.at[0, 0],
            recv_sem=tile_recv.at[source, 0],
            device_id={"fx": source},
            device_id_type=pl.DeviceIdType.MESH,
        )

    def far_arrival(j, r):
        dx, dz = far(j)
        source = at(4 - dx, 4 - dz)
        return pltpu.make_async_remote_copy(
            src_ref=arrived.at[source, r],
            dst_ref=arrived.at[source, r],
            send_sem=tile_send.at[0, 0],
            recv_sem=tile_recv.at[source, r],
            device_id={"fx": source},
            device_id_type=pl.DeviceIdType.MESH,
        )

    tiles = vis_hbm.shape[0]
    row = lax.broadcasted_iota(jnp.int32, (8, 128), 0)
    lane = lax.broadcasted_iota(jnp.int32, (8, 128), 1)

    def slots_for(to):
        found = jnp.int32(0)
        picked = [(jnp.int32(0), jnp.int32(0), jnp.int32(0))] * 2
        for i in range(tiles):
            match = dest_ref[i, 0] == to
            for r in range(2):
                here = match & (found == r)
                new = (jnp.int32(i), count_ref[i], chan_ref[i])
                picked[r] = tuple(jnp.where(here, a, b) for a, b in zip(new, picked[r]))
            found = found + jnp.where(match, 1, 0)
        return [(tile, count.astype(F32) * (1.0 / 64.0), chan) for tile, count, chan in picked]

    def share_rows(slots):
        total = jnp.zeros((8, 128), F32)
        for r, (_, weight, chan) in enumerate(slots):
            total = total + jnp.where((row == r) & (lane == chan), weight, 0.0)
        return total

    load_vis.wait()

    def planes(slots):
        spectra = [jnp.concatenate([vis[t, 0], vis[t, 1]], axis=1) for t, _, _ in slots]
        both = dot(jnp.concatenate(spectra, axis=0), fourier[...]).astype(BF)
        stacked = [
            jnp.concatenate(
                [both[i * SIDE : (i + 1) * SIDE, :SIDE], both[i * SIDE : (i + 1) * SIDE, SIDE:]],
                axis=0,
            )
            for i in range(2)
        ]
        flat = dot(back[...], jnp.concatenate(stacked, axis=1))
        return [
            (flat[:, i * SIDE : (i + 1) * SIDE] * slots[i][1]).astype(BF) for i in range(2)
        ]

    def prepare(to, place):
        slots = slots_for(to)
        share_ref[to] = share_rows(slots)
        share_copy(to, fx).start()
        sending[place, 0], sending[place, 1] = planes(slots)

    def send_far(j, carry):
        prepare(at(*far(j)), j)
        far_copy(j, 0).start()
        far_copy(j, 1).start()
        return carry

    lax.fori_loop(0, len(FAR), send_far, 0)

    def send_near(j, carry):
        prepare(at(*near(j)), len(FAR) + j)
        near_copy(j).start()

        @pl.when(j >= 1)
        def _():
            for r in range(2):
                far_copy(j - 1, r).wait_recv()
                relay_copy(j - 1, r).start()

        return carry

    lax.fori_loop(0, len(NEAR), send_near, 0)
    own = slots_for(fx)
    shares[fx] = share_rows(own)
    arrived[fx, 0], arrived[fx, 1] = planes(own)

    load_sky.wait()

    def there_and_back(c, carry):
        pixels = sky[c].astype(BF)
        half = pixels.astype(F32) + dot(excess[...], pixels)
        model[c] = half + dot(half.astype(BF), excess[...])
        return carry

    lax.fori_loop(0, CH, there_and_back, 0)

    def wait_share(k, carry):
        share_copy(peer(k), peer(k)).wait_recv()
        return carry

    lax.fori_loop(1, n_fx, wait_share, 0)
    slots = n_fx * 2
    wide = slots * 16
    all_shares = shares[...].reshape(n_fx * 8, 128)
    members = jnp.where(all_shares > 0, 1.0, 0.0).astype(BF)
    spread = (
        lax.broadcasted_iota(jnp.int32, (CH * 16, 128), 0) // 16
        == lax.broadcasted_iota(jnp.int32, (CH * 16, 128), 1)
    )
    spread = jnp.where(spread, 1.0, 0.0).astype(BF)
    by_source = lax.dot_general(
        spread, members, (((1,), (1,)), ((), ())), preferred_element_type=F32
    ).astype(BF)
    weights = lax.dot_general(
        spread, all_shares.astype(BF), (((1,), (1,)), ((), ())), preferred_element_type=F32
    )
    totals = jnp.sum(weights, axis=1, keepdims=True)
    src_row = lax.broadcasted_iota(jnp.int32, (n_fx * 8, wide), 0)
    dst_col = lax.broadcasted_iota(jnp.int32, (n_fx * 8, wide), 1)
    widen = (src_row // 8 == dst_col // 32) & (src_row % 8 == dst_col // 16 % 2)
    widened = dot(by_source, jnp.where(widen, 1.0, 0.0).astype(BF))
    diagonal = (
        lax.broadcasted_iota(jnp.int32, (CH * 16, wide), 0) % 16
        == lax.broadcasted_iota(jnp.int32, (CH * 16, wide), 1) % 16
    )
    kron[...] = jnp.where(diagonal, widened, 0.0).astype(BF)
    scale = 1.0 / (1.0 + totals)

    def wait_near(j, carry):
        near_arrival(j).wait_recv()
        return carry

    def wait_far(j, carry):
        for r in range(2):
            far_arrival(j, r).wait_recv()
        return carry

    lax.fori_loop(0, len(NEAR), wait_near, 0)
    lax.fori_loop(0, len(FAR), wait_far, 0)

    def combine(g, carry):
        rows = pl.ds(pl.multiple_of(g * 16, 16), 16)
        gathered = dot(kron[...], arrived[:, :, rows, :].reshape(wide, SIDE))
        pixels = sky[:, rows, :].reshape(CH * 16, SIDE)
        there = model[:, rows, :].reshape(CH * 16, SIDE)
        new = pixels - (totals * there - gathered) * scale
        new = new.reshape(CH // 2, 2, 16, SIDE)
        stepped[:, rows, :] = new.reshape(CH, 16, SIDE).astype(BF)
        low = lax.broadcasted_iota(jnp.int32, (CH // 2, 16, 128), 2) < 64
        second = pltpu.roll(new[:, 1, :, :128].reshape(CH // 2 * 16, 128), 64, 1)
        pair = jnp.where(low, new[:, 0, :, :128], second.reshape(CH // 2, 16, 128))
        columns[:, rows, :] = pair.astype(BF)
        return carry

    lax.fori_loop(0, SIDE // 16, combine, 0)

    def finish_shares(k, carry):
        share_copy(peer(k), fx).wait_send()
        return carry

    def finish_near(j, carry):
        near_copy(j).wait_send()
        return carry

    def finish_far(j, carry):
        for r in range(2):
            far_copy(j, r).wait_send()
            relay_copy(j, r).wait_send()
        return carry

    lax.fori_loop(1, n_fx, finish_shares, 0)
    lax.fori_loop(0, len(NEAR), finish_near, 0)
    lax.fori_loop(0, len(FAR), finish_far, 0)


def wavelet_kernel(
    n_fy,
    n_fx,
    t_cols,
    inner_rows,
    outer_rows,
    analysis,
    select,
    synthesis,
    top,
    stepped,
    columns,
    thr_hbm,
    out_hbm,
    thr,
    below,
    beside,
    corner,
    side,
    row_sec,
    shrunk,
    edge,
    edge_left,
    col_sec,
    edge_top,
    result,
    load_sem,
    halo_send,
    halo_recv,
    edge_send,
    edge_recv,
    rows_send,
    rows_recv,
    out_sem,
):
    fy = lax.axis_index("fy")
    fx = lax.axis_index("fx")
    up, down = (fy + n_fy - 1) % n_fy, (fy + 1) % n_fy
    prev, nxt = (fx + n_fx - 1) % n_fx, (fx + 1) % n_fx

    load_thr = pltpu.make_async_copy(thr_hbm, thr, load_sem.at[0])
    load_thr.start()
    barrier = pltpu.get_barrier_semaphore()
    for where in (
        {"fy": up},
        {"fy": down},
        {"fx": prev},
        {"fx": nxt},
        {"fy": up, "fx": prev},
        {"fy": down, "fx": nxt},
    ):
        pl.semaphore_signal(barrier, inc=1, device_id=where, device_id_type=pl.DeviceIdType.MESH)
    pl.semaphore_wait(barrier, 6)

    def halo_copy(i):
        source = (stepped.at[:, :HALO, :], columns, columns.at[:, :HALO, :])[i]
        target = (below, beside, corner)[i]
        where = ({"fy": up}, {"fx": prev}, {"fy": up, "fx": prev})[i]
        return pltpu.make_async_remote_copy(
            src_ref=source,
            dst_ref=target,
            send_sem=halo_send.at[i],
            recv_sem=halo_recv.at[i],
            device_id=where,
            device_id_type=pl.DeviceIdType.MESH,
        )

    for i in range(3):
        halo_copy(i).start()
    load_thr.wait()
    for i in range(3):
        halo_copy(i).wait_recv()

    def edge_copy(p):
        return pltpu.make_async_remote_copy(
            src_ref=edge.at[p],
            dst_ref=edge_left.at[p],
            send_sem=edge_send.at[p],
            recv_sem=edge_recv.at[p],
            device_id={"fx": nxt},
            device_id_type=pl.DeviceIdType.MESH,
        )

    def rows_copy(p, i):
        return pltpu.make_async_remote_copy(
            src_ref=col_sec.at[p, 1:, SEGMENTS[i][0] : SEGMENTS[i][1], :],
            dst_ref=edge_top.at[p, i],
            send_sem=rows_send.at[p, i],
            recv_sem=rows_recv.at[p, i],
            device_id={"fy": down},
            device_id_type=pl.DeviceIdType.MESH,
        )

    def out_copy(p):
        pair = pl.ds(2 * p, 2)
        return pltpu.make_async_copy(result.at[pair], out_hbm.at[pair], out_sem.at[p])

    for p in range(CH // 2):
        whole = jnp.concatenate([beside[p], corner[p]], axis=0)
        turned = pltpu.roll(whole.astype(F32), 64, 1).astype(BF)
        side[p] = jnp.concatenate([whole, turned], axis=1)

    inner = SIDE - SEG_ROWS

    def analyse(p):
        first = 2 * p
        near = jnp.concatenate([stepped[first], stepped[first + 1], side[p, :SIDE]], axis=1)
        far = jnp.concatenate([below[first], below[first + 1], side[p, SIDE:]], axis=1)
        tall = jnp.concatenate([near, far], axis=0)

        def keep(b, begin, end, values):
            values = values.astype(BF)
            for h in range(2):
                row_sec[b, h, begin:end, :SIDE] = values[:, h * SIDE : (h + 1) * SIDE]
                row_sec[b, h, begin:end, SIDE:] = values[
                    :, 2 * SIDE + h * 128 : 2 * SIDE + (h + 1) * 128
                ]

        for b in range(BASES):
            r = dot(inner_rows[b * inner : (b + 1) * inner], near)
            at = 0
            begin = 0
            for a, e in SEGMENTS:
                keep(b, begin, a, r[at : at + a - begin])
                at += a - begin
                begin = e
        r = dot(outer_rows[...], tall)
        for b in range(BASES):
            for i, (a, e) in enumerate(SEGMENTS):
                at = b * SEG_ROWS + i * 16
                keep(b, a, e, r[at : at + 16])
        for b in range(BASES):
            lanes = slice(b * SIDE, (b + 1) * SIDE)
            coefficient = dot(row_sec[b].reshape(2 * SIDE, SIDE + 128), analysis[b])
            limit = thr[b, pl.ds(first, 2)].reshape(2 * SIDE, SIDE).astype(F32)
            kept = coefficient - jnp.clip(coefficient, -limit, limit)
            shrunk[:, lanes] = kept.astype(BF)
        edge[p] = dot(shrunk[...], select[...]).astype(BF)
        edge_copy(p).start()

    def synthesise_columns(p):
        edge_copy(p).wait_recv()
        for b in range(BASES):
            lanes = slice(b * SIDE, (b + 1) * SIDE)
            with_edge = jnp.concatenate([shrunk[:, lanes], edge_left[p]], axis=1)
            r = dot(with_edge, synthesis[b]).astype(BF)
            col_sec[p, b, :, :SIDE] = r[:SIDE]
            col_sec[p, b, :, SIDE:] = r[SIDE:]
        for i in range(3):
            rows_copy(p, i).start()

    def synthesise_rows(p, carry):
        for i in range(3):
            rows_copy(p, i).wait_recv()
        r = dot(t_cols[...], col_sec[p].reshape(BASES * SIDE, 2 * SIDE))
        t = dot(top[...], edge_top[p].reshape(3 * (BASES - 1) * 16, 2 * SIDE))
        for h in range(2):
            lanes = slice(h * SIDE, (h + 1) * SIDE)
            result[2 * p + h, :HALO] = r[:HALO, lanes] + t[:, lanes]
            result[2 * p + h, HALO:] = r[HALO:, lanes]
        out_copy(p).start()
        return carry

    def step(p, carry):
        @pl.when(p >= 1)
        def _():
            synthesise_columns(p - 1)

        @pl.when(p < CH // 2)
        def _():
            analyse(p)

        return carry

    lax.fori_loop(0, CH // 2 + 1, step, 0)
    lax.fori_loop(0, CH // 2, synthesise_rows, 0)

    for i in range(3):
        halo_copy(i).wait_send()

    def finish(p, carry):
        edge_copy(p).wait_send()
        for i in range(3):
            rows_copy(p, i).wait_send()
        out_copy(p).wait()
        return carry

    lax.fori_loop(0, CH // 2, finish, 0)


def per_device(n_fy, n_fx, sky_image, vis_tiles, tile_dest, tile_chan, tile_count, thresholds):
    made = {name: jnp.asarray(table) for name, table in tables().items()}
    smem = pl.BlockSpec(memory_space=pltpu.SMEM)
    vmem = pl.BlockSpec(memory_space=pltpu.VMEM)
    anywhere = pl.BlockSpec(memory_space=pl.ANY)
    dma = pltpu.SemaphoreType.DMA
    tiles = vis_tiles.shape[0]
    stepped, columns = pl.pallas_call(
        functools.partial(exchange_kernel, n_fx),
        out_shape=(
            jax.ShapeDtypeStruct((CH, SIDE, SIDE), BF),
            jax.ShapeDtypeStruct((CH // 2, SIDE, 128), BF),
        ),
        in_specs=[smem] * 3 + [vmem] * 3 + [anywhere] * 2,
        out_specs=[vmem] * 2,
        scratch_shapes=[
            pltpu.VMEM((tiles, 2, SIDE, SIDE), BF),
            pltpu.VMEM((CH, SIDE, SIDE), F32),
            pltpu.VMEM((CH, SIDE, SIDE), F32),
            pltpu.VMEM((n_fx, 2, SIDE, SIDE), BF),
            pltpu.VMEM((n_fx, 2, SIDE, SIDE), BF),
            pltpu.VMEM((len(FAR), 2, SIDE, SIDE), BF),
            pltpu.VMEM((n_fx, 8, 128), F32),
            pltpu.VMEM((n_fx, 8, 128), F32),
            pltpu.VMEM((CH * 16, n_fx * 32), BF),
            dma((2,)),
            dma((n_fx, 2)),
            dma((n_fx, 2)),
            dma((len(FAR), 2)),
            dma((len(FAR), 2)),
            dma((n_fx,)),
            dma((n_fx,)),
        ],
        compiler_params=pltpu.CompilerParams(
            collective_id=0, has_side_effects=True, vmem_limit_bytes=58 * 1024 * 1024
        ),
    )(
        tile_dest,
        tile_chan,
        tile_count,
        made["fourier"],
        made["back"],
        made["excess"],
        sky_image,
        vis_tiles,
    )
    summed = pl.pallas_call(
        functools.partial(wavelet_kernel, n_fy, n_fx),
        out_shape=jax.ShapeDtypeStruct((CH, SIDE, SIDE), F32),
        in_specs=[vmem] * (len(TABLES) + 2) + [anywhere],
        out_specs=anywhere,
        scratch_shapes=[
            pltpu.VMEM((BASES, CH, SIDE, SIDE), BF),
            pltpu.VMEM((CH, HALO, SIDE), BF),
            pltpu.VMEM((CH // 2, SIDE, 128), BF),
            pltpu.VMEM((CH // 2, HALO, 128), BF),
            pltpu.VMEM((CH // 2, SIDE + HALO, SIDE), BF),
            pltpu.VMEM((BASES, 2, SIDE, SIDE + 128), BF),
            pltpu.VMEM((2 * SIDE, BASES * SIDE), BF),
            pltpu.VMEM((CH // 2, 2 * SIDE, 128), BF),
            pltpu.VMEM((CH // 2, 2 * SIDE, 128), BF),
            pltpu.VMEM((CH // 2, BASES, SIDE, 2 * SIDE), BF),
            pltpu.VMEM((CH // 2, 3, BASES - 1, 16, 2 * SIDE), BF),
            pltpu.VMEM((CH, SIDE, SIDE), F32),
            dma((1,)),
            dma((3,)),
            dma((3,)),
            dma((CH // 2,)),
            dma((CH // 2,)),
            dma((CH // 2, 3)),
            dma((CH // 2, 3)),
            dma((CH // 2,)),
        ],
        compiler_params=pltpu.CompilerParams(
            collective_id=1, has_side_effects=True, vmem_limit_bytes=58 * 1024 * 1024
        ),
    )(*[made[name] for name in TABLES], stepped, columns, thresholds)
    return jnp.maximum(summed * (1.0 / BASES), 0.0)


def solution(mesh):
    in_specs = (
        P(None, "fy", "fx"),
        P(("fy", "fx"), None, None, None),
        P(("fy", "fx"), None),
        P(("fy", "fx")),
        P(("fy", "fx")),
        P(None, None, "fy", "fx"),
    )
    out_specs = P(None, "fy", "fx")
    return jax.shard_map(
        functools.partial(per_device, mesh.shape["fy"], mesh.shape["fx"]),
        mesh=mesh,
        in_specs=in_specs,
        out_specs=out_specs,
        check_vma=False,
    )
```

time: 432 us -> 129 us (0.30); the launches traced: 423 us -> 127 us
  waiting for transfers between devices: 185 us -> 0 us
  Pallas kernels: 0 us -> 123 us
  local copies, waits for them, and re-layouts: 95.3 us -> 1.33 us
  matrix products: 93.7 us -> 0 us
  starting transfers between devices: 28.4 us -> 0 us
  other arithmetic: 20.4 us -> 3.1 us
    pallas_call x0 -> x2, Pallas kernels: none -> 123 us  [the longest x1 68.6 us: per_device(): pl.pallas_call(functools.partial(exchange_kernel, n_fx), out_shape=(jax.S...]
    all_to_all x3 -> x0, waiting for transfers between devices: 116 us -> none  [the longest x1 116 us: per_device(): lax.all_to_all(outgoing, 'fx', split_axis=0, concat_axis=0, tiled=True)]
    dot_general x28 -> x0, matrix products: 93.7 us -> none  [the longest x1 11.5 us: per_device(): jnp.einsum('bcyn,brn->bcyr', framed, analysis_one, preferred_element_type...]
    ppermute x4 -> x0, waiting for transfers between devices: 68.6 us -> none  [passed_along(): lax.ppermute(value, axis, [(i, (i + by) % devices) for i in range(devices)])]
    reshape x3 -> x0, local copies, waits for them, and re-layouts: 34.2 us -> none  [the longest x2 21.1 us: per_device(): outgoing = outgoing.reshape(columns_fx, capacity, 2, facet_side, facet_side)]
    all_to_all x3 -> x0, starting transfers between devices: 22 us -> none  [the longest x1 8.43 us: per_device(): lax.all_to_all(sent_chan, 'fx', split_axis=0, concat_axis=0, tiled=True)]
    unnamed x41 -> x1, local copies, waits for them, and re-layouts: 21.8 us -> 1.33 us
    slice x16 -> x0, local copies, waits for them, and re-layouts: 17.6 us -> none  [the longest x1 7.81 us: per_device(): level_one[..., split_at:]]
  transfers between devices with their start and end apart: 7 -> 0, of which waited for: 5 -> 0; matrix products, arithmetic and copies ran while one was open for 15% -> 0% of each run, Pallas kernels for 0% -> 0%
where the time goes in v1:
time: 129 us; the launch traced here: 127 us
  Pallas kernels  123 us (95%)
  other arithmetic  3.1 us (2%)
  local copies, waits for them, and re-layouts  1.33 us (1%)
    pallas_call x1, Pallas kernels, per_device(): pl.pallas_call(functools.partial(exchange_kernel, n_fx), out_shape=(jax.S...  68.6 us
    pallas_call x1, Pallas kernels, per_device(): pl.pallas_call(functools.partial(wavelet_kernel, n_fy, n_fx), out_shape=j...  54.4 us
    max x1, other arithmetic, per_device(): return jnp.maximum(summed * (1.0 / BASES), 0.0)  3.1 us

profile of v1, /device:TPU:1, one launch (start us, length us, event | category | flops | bytes accessed | tf_op | source)
XLA Modules:
  0.0 127.4 jit_solution(1177637685771224523)
XLA Ops:
  0.0 1.3 %copy.17.dest_ref = s32[16,1]{1,0:T(8,128)} copy(s32[16,1]{0,1:T(1,128)} %param.18) | data formatting | bytes 128 | tf_op args[2]
  1.3 68.6 %shard_map.154 = (bf16[8,256,256]{2,1,0:T(8,128)(2,1)}, bf16[4,256,128]{2,1,0:T(8,128)(2,1)}) custom-call(s32[16,1]{1,0:T(8,128)} %copy.17.dest_ref, s32[16]{0:T(128)} %chan_ref.1, s32[16]{0:T(128)} %count_ref.1, bf16[512,512]{1,0:T(8,128)(2,1)} %constant.31.clone.fourier, bf16[256,512]{1,0:T(8,128)(2,1)} %constant.32.clone.back, ...), custom_call_target="tpu_custom_call" | custom-call | tf_op jit(solution)/shard_map/pallas_call | solution.py:696
  69.9 54.4 %shard_map.155 = f32[8,256,256]{2,1,0:T(8,128)} custom-call(bf16[256,2048]{1,0:T(8,128)(2,1)} %constant.24.clone.t_cols, bf16[1664,256]{1,0:T(8,128)(2,1)} %constant.25.clone.inner_rows, bf16[384,304]{1,0:T(8,128)(2,1)} %constant.26.clone.outer_rows, bf16[8,384,256]{2,1,0:T(8,128)(2,1)} %constant.27.clone.analysis, bf16[2048,128]{1,0:T(8,128)(2,1)} %constant.28.clone.select, ...), custom_call_target="tpu_custom_call" | custom-call | tf_op jit(solution)/shard_map/pallas_call | solution.py:735
  124.3 3.1 %multiply_maximum_fusion = f32[8,256,256]{2,1,0:T(8,128)} fusion(f32[8,256,256]{2,1,0:T(8,128)} %shard_map.155), kind=kLoop, calls=%fused_computation | loop fusion | flops 1048576 | bytes 4194304 | tf_op jit(solution)/shard_map/max | solution.py:766

commit v2 on v1

--- a/solution.py
+++ b/solution.py
@@ -144,9 +144,8 @@
     assert not np.any(np.delete(over, seg, axis=1))
     flat = main.reshape(BASES * SIDE, SIDE)
     out = {"t_cols": flat.T}
-    keep = np.setdiff1d(np.arange(SIDE), seg)
-    out["inner_rows"] = main[:, keep].reshape(BASES * len(keep), SIDE)
-    out["outer_rows"] = full[:, seg].reshape(BASES * SEG_ROWS, SIDE + HALO)
+    out["inner_rows"] = main[:, np.setdiff1d(np.arange(SIDE), seg)]
+    out["outer_rows"] = full[:, seg]
     analyse = np.zeros((BASES, SIDE + 128, SIDE), np.float32)
     analyse[:, : SIDE + HALO] = full.transpose(0, 2, 1)
     out["analyse"] = analyse
@@ -221,6 +220,7 @@
     sending,
     arrived,
     relay,
+    half,
     share_ref,
     shares,
     kron,
@@ -345,7 +345,7 @@
         found = jnp.int32(0)
         picked = [(jnp.int32(0), jnp.int32(0), jnp.int32(0))] * 2
         for i in range(tiles):
-            match = dest_ref[i, 0] == to
+            match = dest_ref[i] == to
             for r in range(2):
                 here = match & (found == r)
                 new = (jnp.int32(i), count_ref[i], chan_ref[i])
@@ -362,19 +362,13 @@
     load_vis.wait()
 
     def planes(slots):
-        spectra = [jnp.concatenate([vis[t, 0], vis[t, 1]], axis=1) for t, _, _ in slots]
-        both = dot(jnp.concatenate(spectra, axis=0), fourier[...]).astype(BF)
-        stacked = [
-            jnp.concatenate(
-                [both[i * SIDE : (i + 1) * SIDE, :SIDE], both[i * SIDE : (i + 1) * SIDE, SIDE:]],
-                axis=0,
-            )
-            for i in range(2)
-        ]
-        flat = dot(back[...], jnp.concatenate(stacked, axis=1))
-        return [
-            (flat[:, i * SIDE : (i + 1) * SIDE] * slots[i][1]).astype(BF) for i in range(2)
-        ]
+        for i, (t, _, _) in enumerate(slots):
+            spectrum = jnp.concatenate([vis[t, 0], vis[t, 1]], axis=1)
+            for part in range(2):
+                half[i, part * SIDE : (part + 1) * SIDE] = dot(
+                    spectrum, fourier[:, part * SIDE : (part + 1) * SIDE]
+                ).astype(BF)
+        return [(dot(back[...], half[i]) * slots[i][1]).astype(BF) for i in range(2)]
 
     def prepare(to, place):
         slots = slots_for(to)
@@ -411,8 +405,8 @@
 
     def there_and_back(c, carry):
         pixels = sky[c].astype(BF)
-        half = pixels.astype(F32) + dot(excess[...], pixels)
-        model[c] = half + dot(half.astype(BF), excess[...])
+        once = pixels.astype(F32) + dot(excess[...], pixels)
+        model[c] = once + dot(once.astype(BF), excess[...])
         return carry
 
     lax.fori_loop(0, CH, there_and_back, 0)
@@ -509,7 +503,7 @@
     stepped,
     columns,
     thr_hbm,
-    out_hbm,
+    result,
     thr,
     below,
     beside,
@@ -521,7 +515,6 @@
     edge_left,
     col_sec,
     edge_top,
-    result,
     load_sem,
     halo_send,
     halo_recv,
@@ -529,7 +522,6 @@
     edge_recv,
     rows_send,
     rows_recv,
-    out_sem,
 ):
     fy = lax.axis_index("fy")
     fx = lax.axis_index("fx")
@@ -589,16 +581,10 @@
             device_id_type=pl.DeviceIdType.MESH,
         )
 
-    def out_copy(p):
-        pair = pl.ds(2 * p, 2)
-        return pltpu.make_async_copy(result.at[pair], out_hbm.at[pair], out_sem.at[p])
-
     for p in range(CH // 2):
         whole = jnp.concatenate([beside[p], corner[p]], axis=0)
         turned = pltpu.roll(whole.astype(F32), 64, 1).astype(BF)
         side[p] = jnp.concatenate([whole, turned], axis=1)
-
-    inner = SIDE - SEG_ROWS
 
     def analyse(p):
         first = 2 * p
@@ -614,36 +600,46 @@
                     :, 2 * SIDE + h * 128 : 2 * SIDE + (h + 1) * 128
                 ]
 
-        for b in range(BASES):
-            r = dot(inner_rows[b * inner : (b + 1) * inner], near)
+        def rows_of(b, carry):
+            r = dot(inner_rows[b], near)
             at = 0
             begin = 0
             for a, e in SEGMENTS:
                 keep(b, begin, a, r[at : at + a - begin])
                 at += a - begin
                 begin = e
-        r = dot(outer_rows[...], tall)
-        for b in range(BASES):
+            r = dot(outer_rows[b], tall)
             for i, (a, e) in enumerate(SEGMENTS):
-                at = b * SEG_ROWS + i * 16
-                keep(b, a, e, r[at : at + 16])
-        for b in range(BASES):
-            lanes = slice(b * SIDE, (b + 1) * SIDE)
+                keep(b, a, e, r[i * 16 : (i + 1) * 16])
+            return carry
+
+        lax.fori_loop(0, BASES, rows_of, 0)
+
+        def columns_of(b, carry):
+            lanes = pl.ds(pl.multiple_of(b * SIDE, SIDE), SIDE)
             coefficient = dot(row_sec[b].reshape(2 * SIDE, SIDE + 128), analysis[b])
             limit = thr[b, pl.ds(first, 2)].reshape(2 * SIDE, SIDE).astype(F32)
             kept = coefficient - jnp.clip(coefficient, -limit, limit)
             shrunk[:, lanes] = kept.astype(BF)
+            return carry
+
+        lax.fori_loop(0, BASES, columns_of, 0)
         edge[p] = dot(shrunk[...], select[...]).astype(BF)
         edge_copy(p).start()
 
     def synthesise_columns(p):
         edge_copy(p).wait_recv()
-        for b in range(BASES):
-            lanes = slice(b * SIDE, (b + 1) * SIDE)
-            with_edge = jnp.concatenate([shrunk[:, lanes], edge_left[p]], axis=1)
+        edges = edge_left[p]
+
+        def columns_of(b, carry):
+            lanes = pl.ds(pl.multiple_of(b * SIDE, SIDE), SIDE)
+            with_edge = jnp.concatenate([shrunk[:, lanes], edges], axis=1)
             r = dot(with_edge, synthesis[b]).astype(BF)
             col_sec[p, b, :, :SIDE] = r[:SIDE]
             col_sec[p, b, :, SIDE:] = r[SIDE:]
+            return carry
+
+        lax.fori_loop(0, BASES, columns_of, 0)
         for i in range(3):
             rows_copy(p, i).start()
 
@@ -656,7 +652,6 @@
             lanes = slice(h * SIDE, (h + 1) * SIDE)
             result[2 * p + h, :HALO] = r[:HALO, lanes] + t[:, lanes]
             result[2 * p + h, HALO:] = r[HALO:, lanes]
-        out_copy(p).start()
         return carry
 
     def step(p, carry):
@@ -680,7 +675,6 @@
         edge_copy(p).wait_send()
         for i in range(3):
             rows_copy(p, i).wait_send()
-        out_copy(p).wait()
         return carry
 
     lax.fori_loop(0, CH // 2, finish, 0)
@@ -708,6 +702,7 @@
             pltpu.VMEM((n_fx, 2, SIDE, SIDE), BF),
             pltpu.VMEM((n_fx, 2, SIDE, SIDE), BF),
             pltpu.VMEM((len(FAR), 2, SIDE, SIDE), BF),
+            pltpu.VMEM((2, 2 * SIDE, SIDE), BF),
             pltpu.VMEM((n_fx, 8, 128), F32),
             pltpu.VMEM((n_fx, 8, 128), F32),
             pltpu.VMEM((CH * 16, n_fx * 32), BF),
@@ -723,7 +718,7 @@
             collective_id=0, has_side_effects=True, vmem_limit_bytes=58 * 1024 * 1024
         ),
     )(
-        tile_dest,
+        tile_dest.reshape(tiles),
         tile_chan,
         tile_count,
         made["fourier"],
@@ -734,9 +729,8 @@
     )
     summed = pl.pallas_call(
         functools.partial(wavelet_kernel, n_fy, n_fx),
-        out_shape=jax.ShapeDtypeStruct((CH, SIDE, SIDE), F32),
+        out_shape=pltpu.VMEM((CH, SIDE, SIDE), F32),
         in_specs=[vmem] * (len(TABLES) + 2) + [anywhere],
-        out_specs=anywhere,
         scratch_shapes=[
             pltpu.VMEM((BASES, CH, SIDE, SIDE), BF),
             pltpu.VMEM((CH, HALO, SIDE), BF),
@@ -749,7 +743,6 @@
             pltpu.VMEM((CH // 2, 2 * SIDE, 128), BF),
             pltpu.VMEM((CH // 2, BASES, SIDE, 2 * SIDE), BF),
             pltpu.VMEM((CH // 2, 3, BASES - 1, 16, 2 * SIDE), BF),
-            pltpu.VMEM((CH, SIDE, SIDE), F32),
             dma((1,)),
             dma((3,)),
             dma((3,)),
@@ -757,7 +750,6 @@
             dma((CH // 2,)),
             dma((CH // 2, 3)),
             dma((CH // 2, 3)),
-            dma((CH // 2,)),
         ],
         compiler_params=pltpu.CompilerParams(
             collective_id=1, has_side_effects=True, vmem_limit_bytes=58 * 1024 * 1024

time: 129 us -> 140 us (1.085)
  Pallas kernels: 123 us -> 136 us
  other arithmetic: 3.1 us -> 1.52 us
    pallas_call x1, Pallas kernels: 54.4 us -> 67.6 us  [per_device(): pl.pallas_call(functools.partial(wavelet_kernel, n_fy, n_fx), out_shape=p...]
    max x1, other arithmetic: 3.1 us -> 1.52 us  [per_device(): return jnp.maximum(summed * (1.0 / BASES), 0.0)]
where the time goes in v2:
time: 140 us; the launch traced here: 138 us
  Pallas kernels  136 us (97%)
  other arithmetic  1.52 us (1%)
    pallas_call x1, Pallas kernels, per_device(): pl.pallas_call(functools.partial(exchange_kernel, n_fx), out_shape=(jax.S...  68.6 us
    pallas_call x1, Pallas kernels, per_device(): pl.pallas_call(functools.partial(wavelet_kernel, n_fy, n_fx), out_shape=p...  67.6 us

profile of v2, /device:TPU:1, one launch (start us, length us, event | category | flops | bytes accessed | tf_op | source)
XLA Modules:
  0.0 137.7 jit_solution(4152306902090380669)
XLA Ops:
  0.0 68.6 %shard_map.154 = (bf16[8,256,256]{2,1,0:T(8,128)(2,1)}, bf16[4,256,128]{2,1,0:T(8,128)(2,1)}) custom-call(s32[16]{0:T(128)} %bitcast.1, s32[16]{0:T(128)} %chan_ref.1, s32[16]{0:T(128)} %count_ref.1, bf16[512,512]{1,0:T(8,128)(2,1)} %constant.31.clone.fourier, bf16[256,512]{1,0:T(8,128)(2,1)} %constant.32.clone.back, ...), custom_call_target="tpu_custom_call" | custom-call | tf_op jit(solution)/shard_map/pallas_call | solution.py:690
  68.6 67.6 %shard_map.155 = f32[8,256,256]{2,1,0:T(8,128)S(1)} custom-call(bf16[256,2048]{1,0:T(8,128)(2,1)} %constant.24.clone.t_cols, bf16[8,208,256]{2,1,0:T(8,128)(2,1)} %constant.25.clone.inner_rows, bf16[8,48,304]{2,1,0:T(8,128)(2,1)} %constant.26.clone.outer_rows, bf16[8,384,256]{2,1,0:T(8,128)(2,1)} %constant.27.clone.analysis, ...), custom_call_target="tpu_custom_call" | custom-call | tf_op jit(solution)/shard_map/pallas_call | solution.py:730
  136.2 1.5 %multiply_maximum_fusion = f32[8,256,256]{2,1,0:T(8,128)} fusion(f32[8,256,256]{2,1,0:T(8,128)S(1)} %shard_map.155), kind=kLoop, calls=%fused_computation | loop fusion | flops 1048576 | bytes 4194304 | tf_op jit(solution)/shard_map/max | solution.py:758

commit v3 on v2

--- a/solution.py
+++ b/solution.py
@@ -100,8 +100,8 @@
 HALO = 48
 BF = jnp.bfloat16
 F32 = jnp.float32
-SEGMENTS = ((48, 64), (112, 128), (240, 256))
-SEG_ROWS = 48
+WIDE = SIDE + 128
+TALL = SIDE + HALO
 
 
 def rounded(table):
@@ -138,33 +138,8 @@
 @functools.lru_cache(maxsize=1)
 def tables():
     full = composite_tables()
-    main = full[:, :, :SIDE]
-    over = full[:, :, SIDE:]
-    seg = np.concatenate([np.arange(a, b) for a, b in SEGMENTS])
-    assert not np.any(np.delete(over, seg, axis=1))
-    flat = main.reshape(BASES * SIDE, SIDE)
-    out = {"t_cols": flat.T}
-    out["inner_rows"] = main[:, np.setdiff1d(np.arange(SIDE), seg)]
-    out["outer_rows"] = full[:, seg]
-    analyse = np.zeros((BASES, SIDE + 128, SIDE), np.float32)
-    analyse[:, : SIDE + HALO] = full.transpose(0, 2, 1)
-    out["analyse"] = analyse
-    select = np.zeros((BASES * SIDE, 128), np.float32)
-    synthesise = np.zeros((BASES, SIDE + 128, SIDE), np.float32)
-    synthesise[:, :SIDE] = main
-    at = 0
-    for b in range(BASES):
-        for k in np.nonzero(np.any(over[b] != 0, axis=1))[0]:
-            select[b * SIDE + k, at] = 1.0
-            synthesise[b, SIDE + at, :HALO] = over[b, k]
-            at += 1
-    assert at <= 128 and not np.any(over[0])
-    out["select"] = select
-    out["synthesise"] = synthesise
-    top = np.zeros((HALO, 3, BASES - 1, 16), np.float32)
-    for i, (a, b) in enumerate(SEGMENTS):
-        top[:, i] = over[1:, a:b].transpose(2, 0, 1)
-    out["top"] = top.reshape(HALO, 3 * (BASES - 1) * 16)
+    wide = np.concatenate([full, np.zeros((BASES, SIDE, 128 - HALO), np.float32)], axis=2)
+    out = {"rows": full, "columns": wide}
     grid = np.arange(SIDE)[:, None] * np.arange(SIDE)[None, :] % SIDE
     angle = grid * (2.0 * math.pi / SIDE)
     cosine = rounded(np.cos(angle) / math.sqrt(SIDE)).astype(np.float64)
@@ -173,9 +148,6 @@
     out["back"] = np.concatenate([cosine, -sine], axis=1)
     out["excess"] = cosine @ cosine + sine @ sine - np.eye(SIDE)
     return {name: rounded(table) for name, table in out.items()}
-
-
-TABLES = ("t_cols", "inner_rows", "outer_rows", "analyse", "select", "synthesise", "top")
 
 
 NEAR = ((1, 0), (3, 0), (0, 1), (0, 3), (1, 1), (1, 3), (3, 1), (3, 3))
@@ -203,6 +175,7 @@
 
 
 def exchange_kernel(
+    n_fy,
     n_fx,
     dest_ref,
     chan_ref,
@@ -212,8 +185,7 @@
     excess,
     sky_hbm,
     vis_hbm,
-    stepped,
-    columns,
+    extended,
     vis,
     sky,
     model,
@@ -224,6 +196,9 @@
     share_ref,
     shares,
     kron,
+    columns,
+    beside,
+    corner,
     load_sem,
     tile_send,
     tile_recv,
@@ -231,7 +206,10 @@
     relay_recv,
     share_send,
     share_recv,
+    halo_send,
+    halo_recv,
 ):
+    fy = lax.axis_index("fy")
     fx = lax.axis_index("fx")
     n_z = 4
     n_x = n_fx // n_z
@@ -257,7 +235,11 @@
         return carry
 
     lax.fori_loop(1, n_fx, greet, 0)
-    pl.semaphore_wait(barrier, n_fx - 1)
+    up, down = (fy + n_fy - 1) % n_fy, (fy + 1) % n_fy
+    prev, nxt = (fx + n_fx - 1) % n_fx, (fx + 1) % n_fx
+    for where in ({"fy": up}, {"fy": down}, {"fy": up, "fx": prev}, {"fy": down, "fx": nxt}):
+        pl.semaphore_signal(barrier, inc=1, device_id=where, device_id_type=pl.DeviceIdType.MESH)
+    pl.semaphore_wait(barrier, n_fx - 1 + 4)
 
     def share_copy(to, source):
         return pltpu.make_async_remote_copy(
@@ -462,7 +444,7 @@
         there = model[:, rows, :].reshape(CH * 16, SIDE)
         new = pixels - (totals * there - gathered) * scale
         new = new.reshape(CH // 2, 2, 16, SIDE)
-        stepped[:, rows, :] = new.reshape(CH, 16, SIDE).astype(BF)
+        extended[:, rows, :SIDE] = new.reshape(CH, 16, SIDE).astype(BF)
         low = lax.broadcasted_iota(jnp.int32, (CH // 2, 16, 128), 2) < 64
         second = pltpu.roll(new[:, 1, :, :128].reshape(CH // 2 * 16, 128), 64, 1)
         pair = jnp.where(low, new[:, 0, :, :128], second.reshape(CH // 2, 16, 128))
@@ -471,80 +453,9 @@
 
     lax.fori_loop(0, SIDE // 16, combine, 0)
 
-    def finish_shares(k, carry):
-        share_copy(peer(k), fx).wait_send()
-        return carry
-
-    def finish_near(j, carry):
-        near_copy(j).wait_send()
-        return carry
-
-    def finish_far(j, carry):
-        for r in range(2):
-            far_copy(j, r).wait_send()
-            relay_copy(j, r).wait_send()
-        return carry
-
-    lax.fori_loop(1, n_fx, finish_shares, 0)
-    lax.fori_loop(0, len(NEAR), finish_near, 0)
-    lax.fori_loop(0, len(FAR), finish_far, 0)
-
-
-def wavelet_kernel(
-    n_fy,
-    n_fx,
-    t_cols,
-    inner_rows,
-    outer_rows,
-    analysis,
-    select,
-    synthesis,
-    top,
-    stepped,
-    columns,
-    thr_hbm,
-    result,
-    thr,
-    below,
-    beside,
-    corner,
-    side,
-    row_sec,
-    shrunk,
-    edge,
-    edge_left,
-    col_sec,
-    edge_top,
-    load_sem,
-    halo_send,
-    halo_recv,
-    edge_send,
-    edge_recv,
-    rows_send,
-    rows_recv,
-):
-    fy = lax.axis_index("fy")
-    fx = lax.axis_index("fx")
-    up, down = (fy + n_fy - 1) % n_fy, (fy + 1) % n_fy
-    prev, nxt = (fx + n_fx - 1) % n_fx, (fx + 1) % n_fx
-
-    load_thr = pltpu.make_async_copy(thr_hbm, thr, load_sem.at[0])
-    load_thr.start()
-    barrier = pltpu.get_barrier_semaphore()
-    for where in (
-        {"fy": up},
-        {"fy": down},
-        {"fx": prev},
-        {"fx": nxt},
-        {"fy": up, "fx": prev},
-        {"fy": down, "fx": nxt},
-    ):
-        pl.semaphore_signal(barrier, inc=1, device_id=where, device_id_type=pl.DeviceIdType.MESH)
-    pl.semaphore_wait(barrier, 6)
-
     def halo_copy(i):
-        source = (stepped.at[:, :HALO, :], columns, columns.at[:, :HALO, :])[i]
-        target = (below, beside, corner)[i]
+        source = (extended.at[:, :HALO, :SIDE], columns, columns.at[:, :HALO, :])[i]
+        target = (extended.at[:, SIDE:, :SIDE], beside, corner)[i]
         where = ({"fy": up}, {"fx": prev}, {"fy": up, "fx": prev})[i]
         return pltpu.make_async_remote_copy(
             src_ref=source,
@@ -557,127 +468,47 @@
 
     for i in range(3):
         halo_copy(i).start()
-    load_thr.wait()
-    for i in range(3):
+    for i in range(1, 3):
         halo_copy(i).wait_recv()
 
-    def edge_copy(p):
-        return pltpu.make_async_remote_copy(
-            src_ref=edge.at[p],
-            dst_ref=edge_left.at[p],
-            send_sem=edge_send.at[p],
-            recv_sem=edge_recv.at[p],
-            device_id={"fx": nxt},
-            device_id_type=pl.DeviceIdType.MESH,
-        )
-
-    def rows_copy(p, i):
-        return pltpu.make_async_remote_copy(
-            src_ref=col_sec.at[p, 1:, SEGMENTS[i][0] : SEGMENTS[i][1], :],
-            dst_ref=edge_top.at[p, i],
-            send_sem=rows_send.at[p, i],
-            recv_sem=rows_recv.at[p, i],
-            device_id={"fy": down},
-            device_id_type=pl.DeviceIdType.MESH,
-        )
-
-    for p in range(CH // 2):
-        whole = jnp.concatenate([beside[p], corner[p]], axis=0)
-        turned = pltpu.roll(whole.astype(F32), 64, 1).astype(BF)
-        side[p] = jnp.concatenate([whole, turned], axis=1)
-
-    def analyse(p):
-        first = 2 * p
-        near = jnp.concatenate([stepped[first], stepped[first + 1], side[p, :SIDE]], axis=1)
-        far = jnp.concatenate([below[first], below[first + 1], side[p, SIDE:]], axis=1)
-        tall = jnp.concatenate([near, far], axis=0)
-
-        def keep(b, begin, end, values):
-            values = values.astype(BF)
-            for h in range(2):
-                row_sec[b, h, begin:end, :SIDE] = values[:, h * SIDE : (h + 1) * SIDE]
-                row_sec[b, h, begin:end, SIDE:] = values[
-                    :, 2 * SIDE + h * 128 : 2 * SIDE + (h + 1) * 128
-                ]
-
-        def rows_of(b, carry):
-            r = dot(inner_rows[b], near)
-            at = 0
-            begin = 0
-            for a, e in SEGMENTS:
-                keep(b, begin, a, r[at : at + a - begin])
-                at += a - begin
-                begin = e
-            r = dot(outer_rows[b], tall)
-            for i, (a, e) in enumerate(SEGMENTS):
-                keep(b, a, e, r[i * 16 : (i + 1) * 16])
-            return carry
-
-        lax.fori_loop(0, BASES, rows_of, 0)
-
-        def columns_of(b, carry):
-            lanes = pl.ds(pl.multiple_of(b * SIDE, SIDE), SIDE)
-            coefficient = dot(row_sec[b].reshape(2 * SIDE, SIDE + 128), analysis[b])
-            limit = thr[b, pl.ds(first, 2)].reshape(2 * SIDE, SIDE).astype(F32)
-            kept = coefficient - jnp.clip(coefficient, -limit, limit)
-            shrunk[:, lanes] = kept.astype(BF)
-            return carry
-
-        lax.fori_loop(0, BASES, columns_of, 0)
-        edge[p] = dot(shrunk[...], select[...]).astype(BF)
-        edge_copy(p).start()
-
-    def synthesise_columns(p):
-        edge_copy(p).wait_recv()
-        edges = edge_left[p]
-
-        def columns_of(b, carry):
-            lanes = pl.ds(pl.multiple_of(b * SIDE, SIDE), SIDE)
-            with_edge = jnp.concatenate([shrunk[:, lanes], edges], axis=1)
-            r = dot(with_edge, synthesis[b]).astype(BF)
-            col_sec[p, b, :, :SIDE] = r[:SIDE]
-            col_sec[p, b, :, SIDE:] = r[SIDE:]
-            return carry
-
-        lax.fori_loop(0, BASES, columns_of, 0)
-        for i in range(3):
-            rows_copy(p, i).start()
-
-    def synthesise_rows(p, carry):
-        for i in range(3):
-            rows_copy(p, i).wait_recv()
-        r = dot(t_cols[...], col_sec[p].reshape(BASES * SIDE, 2 * SIDE))
-        t = dot(top[...], edge_top[p].reshape(3 * (BASES - 1) * 16, 2 * SIDE))
-        for h in range(2):
-            lanes = slice(h * SIDE, (h + 1) * SIDE)
-            result[2 * p + h, :HALO] = r[:HALO, lanes] + t[:, lanes]
-            result[2 * p + h, HALO:] = r[HALO:, lanes]
-        return carry
-
-    def step(p, carry):
-        @pl.when(p >= 1)
-        def _():
-            synthesise_columns(p - 1)
-
-        @pl.when(p < CH // 2)
-        def _():
-            analyse(p)
-
-        return carry
-
-    lax.fori_loop(0, CH // 2 + 1, step, 0)
-    lax.fori_loop(0, CH // 2, synthesise_rows, 0)
-
+    def place(p, carry):
+        for source, begin, end in ((beside, 0, SIDE), (corner, SIDE, TALL)):
+            first = source[p]
+            extended[2 * p, begin:end, SIDE:] = first
+            extended[2 * p + 1, begin:end, SIDE:] = pltpu.roll(first.astype(F32), 64, 1).astype(BF)
+        return carry
+
+    lax.fori_loop(0, CH // 2, place, 0)
+    halo_copy(0).wait_recv()
+
+    def finish_shares(k, carry):
+        share_copy(peer(k), fx).wait_send()
+        return carry
+
+    def finish_near(j, carry):
+        near_copy(j).wait_send()
+        return carry
+
+    def finish_far(j, carry):
+        for r in range(2):
+            far_copy(j, r).wait_send()
+            relay_copy(j, r).wait_send()
+        return carry
+
+    lax.fori_loop(1, n_fx, finish_shares, 0)
+    lax.fori_loop(0, len(NEAR), finish_near, 0)
+    lax.fori_loop(0, len(FAR), finish_far, 0)
     for i in range(3):
         halo_copy(i).wait_send()
 
-    def finish(p, carry):
-        edge_copy(p).wait_send()
-        for i in range(3):
-            rows_copy(p, i).wait_send()
-        return carry
-
-    lax.fori_loop(0, CH // 2, finish, 0)
+
+def passed(value, axes, to):
+    sizes = [lax.axis_size(a) for a in axes]
+    pairs = []
+    for i in np.ndindex(*sizes):
+        j = [(a + b) % n for a, b, n in zip(i, to, sizes)]
+        pairs.append((int(np.ravel_multi_index(i, sizes)), int(np.ravel_multi_index(j, sizes))))
+    return lax.ppermute(value, axes if len(axes) > 1 else axes[0], pairs)
 
 
 def per_device(n_fy, n_fx, sky_image, vis_tiles, tile_dest, tile_chan, tile_count, thresholds):
@@ -687,14 +518,11 @@
     anywhere = pl.BlockSpec(memory_space=pl.ANY)
     dma = pltpu.SemaphoreType.DMA
     tiles = vis_tiles.shape[0]
-    stepped, columns = pl.pallas_call(
-        functools.partial(exchange_kernel, n_fx),
-        out_shape=(
-            jax.ShapeDtypeStruct((CH, SIDE, SIDE), BF),
-            jax.ShapeDtypeStruct((CH // 2, SIDE, 128), BF),
-        ),
+    extended = pl.pallas_call(
+        functools.partial(exchange_kernel, n_fy, n_fx),
+        out_shape=jax.ShapeDtypeStruct((CH, TALL, WIDE), BF),
         in_specs=[smem] * 3 + [vmem] * 3 + [anywhere] * 2,
-        out_specs=[vmem] * 2,
+        out_specs=vmem,
         scratch_shapes=[
             pltpu.VMEM((tiles, 2, SIDE, SIDE), BF),
             pltpu.VMEM((CH, SIDE, SIDE), F32),
@@ -706,6 +534,9 @@
             pltpu.VMEM((n_fx, 8, 128), F32),
             pltpu.VMEM((n_fx, 8, 128), F32),
             pltpu.VMEM((CH * 16, n_fx * 32), BF),
+            pltpu.VMEM((CH // 2, SIDE, 128), BF),
+            pltpu.VMEM((CH // 2, SIDE, 128), BF),
+            pltpu.VMEM((CH // 2, HALO, 128), BF),
             dma((2,)),
             dma((n_fx, 2)),
             dma((n_fx, 2)),
@@ -713,6 +544,8 @@
             dma((len(FAR), 2)),
             dma((n_fx,)),
             dma((n_fx,)),
+            dma((3,)),
+            dma((3,)),
         ],
         compiler_params=pltpu.CompilerParams(
             collective_id=0, has_side_effects=True, vmem_limit_bytes=58 * 1024 * 1024
@@ -727,34 +560,21 @@
         sky_image,
         vis_tiles,
     )
-    summed = pl.pallas_call(
-        functools.partial(wavelet_kernel, n_fy, n_fx),
-        out_shape=pltpu.VMEM((CH, SIDE, SIDE), F32),
-        in_specs=[vmem] * (len(TABLES) + 2) + [anywhere],
-        scratch_shapes=[
-            pltpu.VMEM((BASES, CH, SIDE, SIDE), BF),
-            pltpu.VMEM((CH, HALO, SIDE), BF),
-            pltpu.VMEM((CH // 2, SIDE, 128), BF),
-            pltpu.VMEM((CH // 2, HALO, 128), BF),
-            pltpu.VMEM((CH // 2, SIDE + HALO, SIDE), BF),
-            pltpu.VMEM((BASES, 2, SIDE, SIDE + 128), BF),
-            pltpu.VMEM((2 * SIDE, BASES * SIDE), BF),
-            pltpu.VMEM((CH // 2, 2 * SIDE, 128), BF),
-            pltpu.VMEM((CH // 2, 2 * SIDE, 128), BF),
-            pltpu.VMEM((CH // 2, BASES, SIDE, 2 * SIDE), BF),
-            pltpu.VMEM((CH // 2, 3, BASES - 1, 16, 2 * SIDE), BF),
-            dma((1,)),
-            dma((3,)),
-            dma((3,)),
-            dma((CH // 2,)),
-            dma((CH // 2,)),
-            dma((CH // 2, 3)),
-            dma((CH // 2, 3)),
-        ],
-        compiler_params=pltpu.CompilerParams(
-            collective_id=1, has_side_effects=True, vmem_limit_bytes=58 * 1024 * 1024
-        ),
-    )(*[made[name] for name in TABLES], stepped, columns, thresholds)
+    rows, columns = made["rows"], made["columns"]
+    row_sec = jnp.einsum("bkn,cnx->bckx", rows, extended, preferred_element_type=F32).astype(BF)
+    coefficient = jnp.einsum("bcyx,bkx->bcyk", row_sec, columns, preferred_element_type=F32)
+    limits = thresholds.astype(F32)
+    shrunk = (coefficient - jnp.clip(coefficient, -limits, limits)).astype(BF)
+    col_sec = jnp.einsum("bcyk,bkx->bcyx", shrunk, columns, preferred_element_type=F32).astype(BF)
+    cells = jnp.einsum("bkn,bckx->cnx", rows, col_sec, preferred_element_type=F32)
+    spill = cells.astype(BF)
+    from_left = passed(spill[:, :SIDE, SIDE:TALL], ("fx",), (1,)).astype(F32)
+    from_above = passed(spill[:, SIDE:, :SIDE], ("fy",), (1,)).astype(F32)
+    from_corner = passed(spill[:, SIDE:, SIDE:TALL], ("fy", "fx"), (1, 1)).astype(F32)
+    left = jnp.pad(from_left, ((0, 0), (0, 0), (0, SIDE - HALO)))
+    above = jnp.pad(from_above, ((0, 0), (0, SIDE - HALO), (0, 0)))
+    corner = jnp.pad(from_corner, ((0, 0), (0, SIDE - HALO), (0, SIDE - HALO)))
+    summed = cells[:, :SIDE, :SIDE] + left + above + corner
     return jnp.maximum(summed * (1.0 / BASES), 0.0)
 
 

time: 140 us -> 134 us (0.957)
  Pallas kernels: 136 us -> 79 us
  matrix products: 0 us -> 29.1 us
  waiting for transfers between devices: 0 us -> 18 us
  starting transfers between devices: 0 us -> 3.38 us
  other arithmetic: 1.52 us -> 3.29 us
    pallas_call x2 -> x1, Pallas kernels: 136 us -> 79 us  [per_device(): pl.pallas_call(functools.partial(exchange_kernel, n_fy, n_fx), out_shape=...]
    dot_general x0 -> x2, matrix products: none -> 29.1 us  [the longest x1 16.7 us: per_device(): jnp.einsum('bcyx,bkx->bcyk', row_sec, columns, preferred_element_type=F32)]
    ppermute x0 -> x3, waiting for transfers between devices: none -> 18 us  [passed(): return lax.ppermute(value, axes if len(axes) > 1 else axes[0], pairs)]
    ppermute x0 -> x3, starting transfers between devices: none -> 3.38 us  [passed(): return lax.ppermute(value, axes if len(axes) > 1 else axes[0], pairs)]
    max x1, other arithmetic: 1.52 us -> 3.29 us  [per_device(): return jnp.maximum(summed * (1.0 / BASES), 0.0)]
  transfers between devices with their start and end apart: 0 -> 3, of which waited for: 0 -> 1; matrix products, arithmetic and copies ran while one was open for 0% -> 0% of each run, Pallas kernels for 0% -> 0%
where the time goes in v3:
time: 134 us; the launch traced here: 133 us
  Pallas kernels  79 us (59%)
  matrix products  29.1 us (22%)
  waiting for transfers between devices  18 us (13%)
  starting transfers between devices  3.38 us (3%)
  other arithmetic  3.29 us (2%)
    pallas_call x1, Pallas kernels, per_device(): pl.pallas_call(functools.partial(exchange_kernel, n_fy, n_fx), out_shape=...  79 us
    ppermute x3, waiting for transfers between devices, passed(): return lax.ppermute(value, axes if len(axes) > 1 else axes[0], pairs)  18 us
    dot_general x1, matrix products, per_device(): jnp.einsum('bcyx,bkx->bcyk', row_sec, columns, preferred_element_type=F32)  16.7 us
    dot_general x1, matrix products, per_device(): jnp.einsum('bkn,bckx->cnx', rows, col_sec, preferred_element_type=F32)  12.4 us
    ppermute x3, starting transfers between devices, passed(): return lax.ppermute(value, axes if len(axes) > 1 else axes[0], pairs)  3.38 us
    max x1, other arithmetic, per_device(): return jnp.maximum(summed * (1.0 / BASES), 0.0)  3.29 us
  transfers between devices with their start and end apart: 3, of which 1 were waited for; matrix products, arithmetic and copies ran while one was open for 0% of the time, Pallas kernels for 0%

profile of v3, /device:TPU:1, one launch (start us, length us, event | category | flops | bytes accessed | tf_op | source)
XLA Modules:
  0.0 133.0 jit_solution(13825326390578530770)
XLA Ops:
  0.0 0.0 copy-start.1
  0.0 79.0 %shard_map.109 = bf16[8,304,384]{2,1,0:T(8,128)(2,1)} custom-call(s32[16]{0:T(128)} %bitcast.25, s32[16]{0:T(128)} %chan_ref.1, s32[16]{0:T(128)} %count_ref.1, bf16[512,512]{1,0:T(8,128)(2,1)} %constant.20.clone.fourier, bf16[256,512]{1,0:T(8,128)(2,1)} %constant.21.clone.back, bf16[256,256]{1,0:T(8,128)(2,1)} %constant.22.clone.excess, ...), custom_call_target="tpu_custom_call" | custom-call | tf_op jit(solution)/shard_map/pallas_call | solution.py:521
  79.0 0.0 copy-done.1
  79.0 0.0 copy-start
  79.1 16.7 %fusion.2 = bf16[8,8,256,256]{3,2,1,0:T(8,128)(2,1)} fusion(bf16[8,8,256,256]{3,2,1,0:T(8,128)(2,1)} %param.16, bf16[8,256,384,1]{2,1,3,0:T(8,128)(2,1)S(1)} %copy-done.1, bf16[8,256,304,1]{1,2,3,0:T(8,128)(2,1)} %constant.33, bf16[8,304,384]{2,1,0:T(8,128)(2,1)} %shard_map.109), kind=kOutput, calls=%fused_computation.4 | convolution fusion | flops 7077888000 | bytes 21463040 | tf_op jit(solution)/shard_map/bcyx,bkx->bcyk/dot_general | solution.py:565
  95.8 0.0 copy-done
  95.8 12.4 %fusion.27 = (bf16[8,304,384]{2,1,0:T(8,128)(2,1)S(1)}, f32[8,304,384]{2,1,0:T(8,128)}) fusion(bf16[8,256,304,1]{1,2,0,3:T(8,128)(2,1)} %constant.36, bf16[8,256,384,1]{2,1,0,3:T(8,128)(2,1)S(1)} %copy-done, bf16[8,8,256,256]{3,2,1,0:T(8,128)(2,1)} %fusion.2), kind=kOutput, calls=%fused_computation.20 | convolution fusion | flops 7053656064 | bytes 16809984 | tf_op jit(solution)/shard_map/bkn,bckx->cnx/dot_general | solution.py:569
  108.2 3.2 %collective-permute-start.1 = (bf16[8,48,256]{2,1,0:T(8,128)(2,1)S(1)}, bf16[8,48,256]{2,1,0:T(8,128)(2,1)S(1)}, u32[]{:S(2)}, u32[]{:S(2)}) collective-permute-start(bf16[8,48,256]{2,1,0:T(8,128)(2,1)S(1)} %slice.18), channel_id=1, source_target_pairs={{0,16},{16,32},{32,48},{48,64},{64,80},{80,96},{96,112},{112,0},{1... | collective-permute-start | bytes 589832 | tf_op jit(solution)/shard_map/ppermute | solution.py:511
  111.4 0.1 slice.17
  111.5 0.1 collective-permute-start
  111.6 0.1 collective-permute-start.2
  111.7 18.0 %collective-permute-done.2 = bf16[8,48,48]{2,1,0:T(8,128)(2,1)S(1)} collective-permute-done((bf16[8,48,48]{2,1,0:T(8,128)(2,1)S(1)}, bf16[8,48,48]{2,1,0:T(8,128)(2,1)S(1)}, u32[]{:S(2)}, u32[]{:S(2)}) %collective-permute-start.2) | collective-permute-done | bytes 36896 | tf_op jit(solution)/shard_map/ppermute | solution.py:511
  129.7 0.0 collective-permute-done.1
  129.7 0.0 collective-permute-done
  129.7 3.3 %fusion.19 = f32[8,256,256]{2,1,0:T(8,128)} fusion(f32[8,304,384]{2,1,0:T(8,128)} %get-tuple-element.6, bf16[8,48,48]{2,1,0:T(8,128)(2,1)S(1)} %collective-permute-done.2, bf16[8,48,256]{2,1,0:T(8,128)(2,1)S(1)} %collective-permute-done.1, bf16[8,256,48]{2,1,0:T(8,128)(2,1)S(1)} %collective-permute-done), kind=kLoop, calls=%fused_computation.17 | loop fusion | flops 4194304 | bytes 4624384 | tf_op jit(solution)/shard_map/max | solution.py:578
  (2 shorter events, 0.0 us)
Async XLA Ops:
  0.0 79.0 %copy-start.1 = (bf16[8,256,384,1]{2,1,3,0:T(8,128)(2,1)S(1)}, bf16[8,256,384,1]{2,1,3,0:T(8,128)(2,1)}, u32[]{:S(2)}) copy-start(bf16[8,256,384,1]{2,1,3,0:T(8,128)(2,1)} %constant.34) | copy-start | bytes 4718596
  79.0 16.7 %copy-start = (bf16[8,256,384,1]{2,1,0,3:T(8,128)(2,1)S(1)}, bf16[8,256,384,1]{2,1,0,3:T(8,128)(2,1)}, u32[]{:S(2)}) copy-start(bf16[8,256,384,1]{2,1,0,3:T(8,128)(2,1)} %constant.35) | copy-start | bytes 4718596
  108.2 21.5 %collective-permute-start.1 = (bf16[8,48,256]{2,1,0:T(8,128)(2,1)S(1)}, bf16[8,48,256]{2,1,0:T(8,128)(2,1)S(1)}, u32[]{:S(2)}, u32[]{:S(2)}) collective-permute-start(bf16[8,48,256]{2,1,0:T(8,128)(2,1)S(1)} %slice.18), channel_id=1, source_target_pairs={{0,16},{16,32},{32,48},{48,64},{64,80},{80,96},{96,112},{112,0},{1... | collective-permute-start | bytes 589832 | tf_op jit(solution)/shard_map/ppermute | solution.py:511
  111.5 18.2 %collective-permute-start = (bf16[8,256,48]{2,1,0:T(8,128)(2,1)S(1)}, bf16[8,256,48]{2,1,0:T(8,128)(2,1)S(1)}, u32[]{:S(2)}, u32[]{:S(2)}) collective-permute-start(bf16[8,256,48]{2,1,0:T(8,128)(2,1)S(1)} %slice.17), channel_id=1, source_target_pairs={{0,1},{1,2},{2,3},{3,4},{4,5},{5,6},{6,7},{7,8},{8,9},{9,10},{10,1... | collective-permute-start | bytes 589832 | tf_op jit(solution)/shard_map/ppermute | solution.py:511
  111.6 18.1 %collective-permute-start.2 = (bf16[8,48,48]{2,1,0:T(8,128)(2,1)S(1)}, bf16[8,48,48]{2,1,0:T(8,128)(2,1)S(1)}, u32[]{:S(2)}, u32[]{:S(2)}) collective-permute-start(bf16[8,48,48]{2,1,0:T(8,128)(2,1)S(1)} %slice.19), channel_id=1, source_target_pairs={{0,17},{1,18},{2,19},{3,20},{4,21},{5,22},{6,23},{7,24},{8,25},{9,... | collective-permute-start | bytes 110600 | tf_op jit(solution)/shard_map/ppermute | solution.py:511

commit v4 on v3

--- a/solution.py
+++ b/solution.py
@@ -144,8 +144,10 @@
     angle = grid * (2.0 * math.pi / SIDE)
     cosine = rounded(np.cos(angle) / math.sqrt(SIDE)).astype(np.float64)
     sine = rounded(np.sin(angle) / math.sqrt(SIDE)).astype(np.float64)
-    out["fourier"] = np.block([[cosine, sine], [-sine, cosine]])
-    out["back"] = np.concatenate([cosine, -sine], axis=1)
+    out["fourier"] = np.stack(
+        [np.stack([cosine, sine], axis=1), np.stack([-sine, cosine], axis=1)]
+    )
+    out["back"] = np.stack([cosine, -sine], axis=1)
     out["excess"] = cosine @ cosine + sine @ sine - np.eye(SIDE)
     return {name: rounded(table) for name, table in out.items()}
 
@@ -180,19 +182,15 @@
     dest_ref,
     chan_ref,
     count_ref,
-    fourier,
-    back,
     excess,
+    planes,
     sky_hbm,
-    vis_hbm,
     extended,
-    vis,
     sky,
     model,
     sending,
     arrived,
     relay,
-    half,
     share_ref,
     shares,
     kron,
@@ -208,6 +206,8 @@
     share_recv,
     halo_send,
     halo_recv,
+    columns_send,
+    columns_recv,
 ):
     fy = lax.axis_index("fy")
     fx = lax.axis_index("fx")
@@ -221,9 +221,7 @@
     def peer(k):
         return at(k // n_z, k % n_z)
 
-    load_vis = pltpu.make_async_copy(vis_hbm, vis, load_sem.at[0])
-    load_sky = pltpu.make_async_copy(sky_hbm, sky, load_sem.at[1])
-    load_vis.start()
+    load_sky = pltpu.make_async_copy(sky_hbm, sky, load_sem.at[0])
     load_sky.start()
 
     barrier = pltpu.get_barrier_semaphore()
@@ -319,7 +317,7 @@
             device_id_type=pl.DeviceIdType.MESH,
         )
 
-    tiles = vis_hbm.shape[0]
+    tiles = planes.shape[0]
     row = lax.broadcasted_iota(jnp.int32, (8, 128), 0)
     lane = lax.broadcasted_iota(jnp.int32, (8, 128), 1)
 
@@ -341,22 +339,12 @@
             total = total + jnp.where((row == r) & (lane == chan), weight, 0.0)
         return total
 
-    load_vis.wait()
-
-    def planes(slots):
-        for i, (t, _, _) in enumerate(slots):
-            spectrum = jnp.concatenate([vis[t, 0], vis[t, 1]], axis=1)
-            for part in range(2):
-                half[i, part * SIDE : (part + 1) * SIDE] = dot(
-                    spectrum, fourier[:, part * SIDE : (part + 1) * SIDE]
-                ).astype(BF)
-        return [(dot(back[...], half[i]) * slots[i][1]).astype(BF) for i in range(2)]
-
     def prepare(to, place):
         slots = slots_for(to)
         share_ref[to] = share_rows(slots)
         share_copy(to, fx).start()
-        sending[place, 0], sending[place, 1] = planes(slots)
+        for r in range(2):
+            sending[place, r] = planes[slots[r][0]]
 
     def send_far(j, carry):
         prepare(at(*far(j)), j)
@@ -369,19 +357,13 @@
     def send_near(j, carry):
         prepare(at(*near(j)), len(FAR) + j)
         near_copy(j).start()
-
-        @pl.when(j >= 1)
-        def _():
-            for r in range(2):
-                far_copy(j - 1, r).wait_recv()
-                relay_copy(j - 1, r).start()
-
         return carry
 
     lax.fori_loop(0, len(NEAR), send_near, 0)
     own = slots_for(fx)
     shares[fx] = share_rows(own)
-    arrived[fx, 0], arrived[fx, 1] = planes(own)
+    for r in range(2):
+        arrived[fx, r] = planes[own[r][0]]
 
     load_sky.wait()
 
@@ -392,6 +374,14 @@
         return carry
 
     lax.fori_loop(0, CH, there_and_back, 0)
+
+    def pass_on(j, carry):
+        for r in range(2):
+            far_copy(j, r).wait_recv()
+            relay_copy(j, r).start()
+        return carry
+
+    lax.fori_loop(0, len(FAR), pass_on, 0)
 
     def wait_share(k, carry):
         share_copy(peer(k), peer(k)).wait_recv()
@@ -437,7 +427,7 @@
     lax.fori_loop(0, len(NEAR), wait_near, 0)
     lax.fori_loop(0, len(FAR), wait_far, 0)
 
-    def combine(g, carry):
+    def combine(g):
         rows = pl.ds(pl.multiple_of(g * 16, 16), 16)
         gathered = dot(kron[...], arrived[:, :, rows, :].reshape(wide, SIDE))
         pixels = sky[:, rows, :].reshape(CH * 16, SIDE)
@@ -449,14 +439,25 @@
         second = pltpu.roll(new[:, 1, :, :128].reshape(CH // 2 * 16, 128), 64, 1)
         pair = jnp.where(low, new[:, 0, :, :128], second.reshape(CH // 2, 16, 128))
         columns[:, rows, :] = pair.astype(BF)
-        return carry
-
-    lax.fori_loop(0, SIDE // 16, combine, 0)
+
+    chunks = 4
+    deep = SIDE // chunks
+
+    def columns_copy(q):
+        rows = pl.ds(pl.multiple_of(q * deep, deep), deep)
+        return pltpu.make_async_remote_copy(
+            src_ref=columns.at[:, rows, :],
+            dst_ref=beside.at[:, rows, :],
+            send_sem=columns_send.at[q],
+            recv_sem=columns_recv.at[q],
+            device_id={"fx": prev},
+            device_id_type=pl.DeviceIdType.MESH,
+        )
 
     def halo_copy(i):
-        source = (extended.at[:, :HALO, :SIDE], columns, columns.at[:, :HALO, :])[i]
-        target = (extended.at[:, SIDE:, :SIDE], beside, corner)[i]
-        where = ({"fy": up}, {"fx": prev}, {"fy": up, "fx": prev})[i]
+        source = (extended.at[:, :HALO, :SIDE], columns.at[:, :HALO, :])[i]
+        target = (extended.at[:, SIDE:, :SIDE], corner)[i]
+        where = ({"fy": up}, {"fy": up, "fx": prev})[i]
         return pltpu.make_async_remote_copy(
             src_ref=source,
             dst_ref=target,
@@ -466,19 +467,31 @@
             device_id_type=pl.DeviceIdType.MESH,
         )
 
-    for i in range(3):
-        halo_copy(i).start()
-    for i in range(1, 3):
-        halo_copy(i).wait_recv()
-
-    def place(p, carry):
-        for source, begin, end in ((beside, 0, SIDE), (corner, SIDE, TALL)):
+    def make_chunk(q, carry):
+        for i in range(deep // 16):
+            combine(q * (deep // 16) + i)
+        columns_copy(q).start()
+
+        @pl.when(q == 0)
+        def _():
+            for i in range(2):
+                halo_copy(i).start()
+
+        return carry
+
+    lax.fori_loop(0, chunks, make_chunk, 0)
+
+    def place(source, begin, end):
+        for p in range(CH // 2):
             first = source[p]
             extended[2 * p, begin:end, SIDE:] = first
             extended[2 * p + 1, begin:end, SIDE:] = pltpu.roll(first.astype(F32), 64, 1).astype(BF)
-        return carry
-
-    lax.fori_loop(0, CH // 2, place, 0)
+
+    halo_copy(1).wait_recv()
+    place(corner, SIDE, TALL)
+    for q in range(chunks):
+        columns_copy(q).wait_recv()
+        place(beside.at[:, q * deep : (q + 1) * deep, :], q * deep, (q + 1) * deep)
     halo_copy(0).wait_recv()
 
     def finish_shares(k, carry):
@@ -498,8 +511,10 @@
     lax.fori_loop(1, n_fx, finish_shares, 0)
     lax.fori_loop(0, len(NEAR), finish_near, 0)
     lax.fori_loop(0, len(FAR), finish_far, 0)
-    for i in range(3):
+    for i in range(2):
         halo_copy(i).wait_send()
+    for q in range(chunks):
+        columns_copy(q).wait_send()
 
 
 def passed(value, axes, to):
@@ -518,34 +533,40 @@
     anywhere = pl.BlockSpec(memory_space=pl.ANY)
     dma = pltpu.SemaphoreType.DMA
     tiles = vis_tiles.shape[0]
+    half = jnp.einsum(
+        "ipuv,pvqx->iuqx", vis_tiles, made["fourier"], preferred_element_type=F32
+    ).astype(BF)
+    planes = jnp.einsum("yqu,iuqx->iyx", made["back"], half, preferred_element_type=F32)
+    weight = tile_count.astype(F32) / 64.0
+    planes = (planes * weight[:, None, None]).astype(BF)
     extended = pl.pallas_call(
         functools.partial(exchange_kernel, n_fy, n_fx),
         out_shape=jax.ShapeDtypeStruct((CH, TALL, WIDE), BF),
-        in_specs=[smem] * 3 + [vmem] * 3 + [anywhere] * 2,
+        in_specs=[smem] * 3 + [vmem] * 2 + [anywhere],
         out_specs=vmem,
         scratch_shapes=[
-            pltpu.VMEM((tiles, 2, SIDE, SIDE), BF),
             pltpu.VMEM((CH, SIDE, SIDE), F32),
             pltpu.VMEM((CH, SIDE, SIDE), F32),
             pltpu.VMEM((n_fx, 2, SIDE, SIDE), BF),
             pltpu.VMEM((n_fx, 2, SIDE, SIDE), BF),
             pltpu.VMEM((len(FAR), 2, SIDE, SIDE), BF),
-            pltpu.VMEM((2, 2 * SIDE, SIDE), BF),
             pltpu.VMEM((n_fx, 8, 128), F32),
             pltpu.VMEM((n_fx, 8, 128), F32),
             pltpu.VMEM((CH * 16, n_fx * 32), BF),
             pltpu.VMEM((CH // 2, SIDE, 128), BF),
             pltpu.VMEM((CH // 2, SIDE, 128), BF),
             pltpu.VMEM((CH // 2, HALO, 128), BF),
-            dma((2,)),
+            dma((1,)),
             dma((n_fx, 2)),
             dma((n_fx, 2)),
             dma((len(FAR), 2)),
             dma((len(FAR), 2)),
             dma((n_fx,)),
             dma((n_fx,)),
-            dma((3,)),
-            dma((3,)),
+            dma((2,)),
+            dma((2,)),
+            dma((4,)),
+            dma((4,)),
         ],
         compiler_params=pltpu.CompilerParams(
             collective_id=0, has_side_effects=True, vmem_limit_bytes=58 * 1024 * 1024
@@ -554,11 +575,9 @@
         tile_dest.reshape(tiles),
         tile_chan,
         tile_count,
-        made["fourier"],
-        made["back"],
         made["excess"],
+        planes,
         sky_image,
-        vis_tiles,
     )
     rows, columns = made["rows"], made["columns"]
     row_sec = jnp.einsum("bkn,cnx->bckx", rows, extended, preferred_element_type=F32).astype(BF)
@@ -568,12 +587,12 @@
     col_sec = jnp.einsum("bcyk,bkx->bcyx", shrunk, columns, preferred_element_type=F32).astype(BF)
     cells = jnp.einsum("bkn,bckx->cnx", rows, col_sec, preferred_element_type=F32)
     spill = cells.astype(BF)
-    from_left = passed(spill[:, :SIDE, SIDE:TALL], ("fx",), (1,)).astype(F32)
+    from_left = passed(spill[:, :SIDE, SIDE:], ("fx",), (1,)).astype(F32)
     from_above = passed(spill[:, SIDE:, :SIDE], ("fy",), (1,)).astype(F32)
-    from_corner = passed(spill[:, SIDE:, SIDE:TALL], ("fy", "fx"), (1, 1)).astype(F32)
-    left = jnp.pad(from_left, ((0, 0), (0, 0), (0, SIDE - HALO)))
+    from_corner = passed(spill[:, SIDE:, SIDE:], ("fy", "fx"), (1, 1)).astype(F32)
+    left = jnp.pad(from_left, ((0, 0), (0, 0), (0, 128)))
     above = jnp.pad(from_above, ((0, 0), (0, SIDE - HALO), (0, 0)))
-    corner = jnp.pad(from_corner, ((0, 0), (0, SIDE - HALO), (0, SIDE - HALO)))
+    corner = jnp.pad(from_corner, ((0, 0), (0, SIDE - HALO), (0, 128)))
     summed = cells[:, :SIDE, :SIDE] + left + above + corner
     return jnp.maximum(summed * (1.0 / BASES), 0.0)
 

time: 134 us -> 140 us (1.045)
  matrix products: 29.1 us -> 36.9 us
  local copies, waits for them, and re-layouts: 0.13 us -> 2.57 us
  Pallas kernels: 79 us -> 76.7 us
  waiting for transfers between devices: 18 us -> 16.2 us
    dot_general x0 -> x2, matrix products: none -> 7.79 us  [the longest x1 4.73 us: per_device(): jnp.einsum('ipuv,pvqx->iuqx', vis_tiles, made['fourier'], preferred_eleme...]
    dot_general x0 -> x1, local copies, waits for them, and re-layouts: none -> 2.43 us  [per_device(): jnp.einsum('ipuv,pvqx->iuqx', vis_tiles, made['fourier'], preferred_eleme...]
    pallas_call x1, Pallas kernels: 79 us -> 76.7 us  [per_device(): pl.pallas_call(functools.partial(exchange_kernel, n_fy, n_fx), out_shape=...]
    ppermute x3, waiting for transfers between devices: 18 us -> 16.2 us  [passed(): return lax.ppermute(value, axes if len(axes) > 1 else axes[0], pairs)]
where the time goes in v4:
time: 140 us
  Pallas kernels  76.7 us (55%)
  matrix products  36.9 us (26%)
  waiting for transfers between devices  16.2 us (12%)
  other arithmetic  3.89 us (3%)
  starting transfers between devices  3.62 us (3%)
  local copies, waits for them, and re-layouts  2.57 us (2%)
    pallas_call x1, Pallas kernels, per_device(): pl.pallas_call(functools.partial(exchange_kernel, n_fy, n_fx), out_shape=...  76.7 us
    dot_general x1, matrix products, per_device(): jnp.einsum('bcyx,bkx->bcyk', row_sec, columns, preferred_element_type=F32)  16.3 us
    ppermute x3, waiting for transfers between devices, passed(): return lax.ppermute(value, axes if len(axes) > 1 else axes[0], pairs)  16.2 us
    dot_general x1, matrix products, per_device(): jnp.einsum('bkn,bckx->cnx', rows, col_sec, preferred_element_type=F32)  12.9 us
    dot_general x1, matrix products, per_device(): jnp.einsum('ipuv,pvqx->iuqx', vis_tiles, made['fourier'], preferred_eleme...  4.73 us
    ppermute x3, starting transfers between devices, passed(): return lax.ppermute(value, axes if len(axes) > 1 else axes[0], pairs)  3.62 us
    max x1, other arithmetic, per_device(): return jnp.maximum(summed * (1.0 / BASES), 0.0)  3.23 us
    dot_general x1, matrix products, per_device(): jnp.einsum('yqu,iuqx->iyx', made['back'], half, preferred_element_type=F32)  3.07 us
  transfers between devices with their start and end apart: 3, of which 1 were waited for; matrix products, arithmetic and copies ran while one was open for 0% of the time, Pallas kernels for 0%

profile of v4, /device:TPU:1, one launch (start us, length us, event | category | flops | bytes accessed | tf_op | source)
XLA Modules:
  0.0 140.0 jit_solution(10092133565688302229)
XLA Ops:
  0.0 0.7 convert_multiply_fusion
  0.7 4.7 %fusion.18 = bf16[2,256,16,256,1]{3,1,4,2,0:T(8,128)(2,1)S(1)} fusion(bf16[2,256,2,256,1]{1,3,0,4,2:T(8,128)(2,1)} %constant.37, bf16[16,2,256,256]{3,2,1,0:T(8,128)(2,1)} %param.12), kind=kOutput, calls=%fused_computation.17 | convolution fusion | flops 2147483648 | bytes 8912896 | tf_op jit(solution)/shard_map/ipuv,pvqx->iuqx/dot_general | solution.py:536
  5.4 0.0 copy-start.2
  5.4 2.4 %copy.35 = bf16[2,256,16,256,1]{3,2,1,0,4:T(8,128)(2,1)S(1)} copy(bf16[2,256,16,256,1]{3,1,4,2,0:T(8,128)(2,1)S(1)} %fusion.18) | data formatting | bytes 8388608 | tf_op jit(solution)/shard_map/ipuv,pvqx->iuqx/dot_general | solution.py:536
  7.8 0.0 copy-done.2
  7.9 3.1 %fusion.22.planes = bf16[16,256,256]{2,1,0:T(8,128)(2,1)} fusion(f32[16]{0:T(128)S(1)} %convert_multiply_fusion, bf16[256,2,256,1]{0,2,1,3:T(8,128)(2,1)S(1)} %copy-done.2, bf16[16,256,2,256]{1,0,3,2:T(8,128)(2,1)S(1)} %bitcast.49), kind=kOutput, calls=%fused_computation.21 | convolution fusion | flops 1075838976 | bytes 6553664 | tf_op jit(solution)/shard_map/yqu,iuqx->iyx/dot_general | solution.py:539
  10.9 0.0 copy-start
  10.9 0.0 copy-start.1
  10.9 76.7 %shard_map.109 = bf16[8,304,384]{2,1,0:T(8,128)(2,1)} custom-call(s32[16]{0:T(128)} %bitcast.50, s32[16]{0:T(128)} %chan_ref.1, s32[16]{0:T(128)} %count_ref.1, bf16[256,256]{1,0:T(8,128)(2,1)} %constant.25.clone.excess, bf16[16,256,256]{2,1,0:T(8,128)(2,1)} %fusion.22.planes, f32[8,256,256]{2,1,0:T(8,128)} %sky_hbm.1), custom_call_target="tpu_custom_call" | custom-call | tf_op jit(solution)/shard_map/pallas_call | solution.py:542
  87.7 0.0 copy-done
  87.7 0.0 copy-done.1
  87.7 16.3 %fusion.2 = bf16[8,8,256,256]{3,2,1,0:T(8,128)(2,1)} fusion(bf16[8,8,256,256]{3,2,1,0:T(8,128)(2,1)} %param.16, bf16[8,256,384,1]{2,1,3,0:T(8,128)(2,1)S(1)} %copy-done, bf16[8,256,304,1]{1,2,3,0:T(8,128)(2,1)S(1)} %copy-done.1, bf16[8,304,384]{2,1,0:T(8,128)(2,1)} %shard_map.109), kind=kOutput, calls=%fused_computation.4 | convolution fusion | flops 7077888000 | bytes 21463040 | tf_op jit(solution)/shard_map/bcyx,bkx->bcyk/dot_general | solution.py:584
  103.9 12.9 %fusion.36 = (bf16[8,304,384]{2,1,0:T(8,128)(2,1)S(1)}, f32[8,304,384]{2,1,0:T(8,128)}) fusion(bf16[8,256,304,1]{1,2,0,3:T(8,128)(2,1)} %constant.43, bf16[8,256,384,1]{2,1,0,3:T(8,128)(2,1)} %constant.42, bf16[8,8,256,256]{3,2,1,0:T(8,128)(2,1)} %fusion.2), kind=kOutput, calls=%fused_computation.30 | convolution fusion | flops 7053656064 | bytes 16809984 | tf_op jit(solution)/shard_map/bkn,bckx->cnx/dot_general | solution.py:588
  116.8 0.1 slice.17
  116.9 0.3 collective-permute-start
  117.2 3.3 %collective-permute-start.1 = (bf16[8,48,256]{2,1,0:T(8,128)(2,1)S(1)}, bf16[8,48,256]{2,1,0:T(8,128)(2,1)S(1)}, u32[]{:S(2)}, u32[]{:S(2)}) collective-permute-start(bf16[8,48,256]{2,1,0:T(8,128)(2,1)S(1)} %slice.18), channel_id=1, source_target_pairs={{0,16},{16,32},{32,48},{48,64},{64,80},{80,96},{96,112},{112,0},{1... | collective-permute-start | bytes 589832 | tf_op jit(solution)/shard_map/ppermute | solution.py:526
  120.5 0.1 collective-permute-start.2
  120.6 16.2 %collective-permute-done.2 = bf16[8,48,128]{2,1,0:T(8,128)(2,1)S(1)} collective-permute-done((bf16[8,48,128]{2,1,0:T(8,128)(2,1)S(1)}, bf16[8,48,128]{2,1,0:T(8,128)(2,1)S(1)}, u32[]{:S(2)}, u32[]{:S(2)}) %collective-permute-start.2) | collective-permute-done | bytes 98336 | tf_op jit(solution)/shard_map/ppermute | solution.py:526
  136.8 0.0 collective-permute-done.1
  136.8 0.0 collective-permute-done
  136.8 3.2 %fusion.26 = f32[8,256,256]{2,1,0:T(8,128)} fusion(f32[8,304,384]{2,1,0:T(8,128)} %get-tuple-element.6, bf16[8,48,128]{2,1,0:T(8,128)(2,1)S(1)} %collective-permute-done.2, bf16[8,48,256]{2,1,0:T(8,128)(2,1)S(1)} %collective-permute-done.1, bf16[8,256,128]{2,1,0:T(8,128)(2,1)S(1)} %collective-permute-done), kind=kLoop, calls=%fused_computation.26 | loop fusion | flops 4194304 | bytes 5013504 | tf_op jit(solution)/shard_map/max | solution.py:597
  (2 shorter events, 0.0 us)
Async XLA Ops:
  5.4 2.4 %copy-start.2 = (bf16[256,2,256,1]{0,2,1,3:T(8,128)(2,1)S(1)}, bf16[256,2,256,1]{0,2,1,3:T(8,128)(2,1)}, u32[]{:S(2)}) copy-start(bf16[256,2,256,1]{0,2,1,3:T(8,128)(2,1)} %constant.39) | copy-start | bytes 786436
  10.9 76.7 %copy-start = (bf16[8,256,384,1]{2,1,3,0:T(8,128)(2,1)S(1)}, bf16[8,256,384,1]{2,1,3,0:T(8,128)(2,1)}, u32[]{:S(2)}) copy-start(bf16[8,256,384,1]{2,1,3,0:T(8,128)(2,1)} %constant.41) | copy-start | bytes 4718596
  10.9 76.8 %copy-start.1 = (bf16[8,256,304,1]{1,2,3,0:T(8,128)(2,1)S(1)}, bf16[8,256,304,1]{1,2,3,0:T(8,128)(2,1)}, u32[]{:S(2)}) copy-start(bf16[8,256,304,1]{1,2,3,0:T(8,128)(2,1)} %constant.40) | copy-start | bytes 3735556
  116.9 19.9 %collective-permute-start = (bf16[8,256,128]{2,1,0:T(8,128)(2,1)S(1)}, bf16[8,256,128]{2,1,0:T(8,128)(2,1)S(1)}, u32[]{:S(2)}, u32[]{:S(2)}) collective-permute-start(bf16[8,256,128]{2,1,0:T(8,128)(2,1)S(1)} %slice.17), channel_id=1, source_target_pairs={{0,1},{1,2},{2,3},{3,4},{4,5},{5,6},{6,7},{7,8},{8,9},{9,10},{10,1... | collective-permute-start | bytes 1572872 | tf_op jit(solution)/shard_map/ppermute | solution.py:526
  117.2 19.6 %collective-permute-start.1 = (bf16[8,48,256]{2,1,0:T(8,128)(2,1)S(1)}, bf16[8,48,256]{2,1,0:T(8,128)(2,1)S(1)}, u32[]{:S(2)}, u32[]{:S(2)}) collective-permute-start(bf16[8,48,256]{2,1,0:T(8,128)(2,1)S(1)} %slice.18), channel_id=1, source_target_pairs={{0,16},{16,32},{32,48},{48,64},{64,80},{80,96},{96,112},{112,0},{1... | collective-permute-start | bytes 589832 | tf_op jit(solution)/shard_map/ppermute | solution.py:526
  120.5 16.3 %collective-permute-start.2 = (bf16[8,48,128]{2,1,0:T(8,128)(2,1)S(1)}, bf16[8,48,128]{2,1,0:T(8,128)(2,1)S(1)}, u32[]{:S(2)}, u32[]{:S(2)}) collective-permute-start(bf16[8,48,128]{2,1,0:T(8,128)(2,1)S(1)} %slice.19), channel_id=1, source_target_pairs={{0,17},{1,18},{2,19},{3,20},{4,21},{5,22},{6,23},{7,24},{8,25},{9,... | collective-permute-start | bytes 294920 | tf_op jit(solution)/shard_map/ppermute | solution.py:526

commit v5 on v3

--- a/solution.py
+++ b/solution.py
@@ -150,17 +150,9 @@
     return {name: rounded(table) for name, table in out.items()}
 
 
-NEAR = ((1, 0), (3, 0), (0, 1), (0, 3), (1, 1), (1, 3), (3, 1), (3, 3))
+NEAR = ((1, 0), (0, 1), (3, 0), (0, 3), (1, 1), (3, 3), (1, 3), (3, 1))
 FAR = ((2, 0), (0, 2), (2, 1), (2, 3), (1, 2), (3, 2), (2, 2))
-THROUGH = (
-    ((1, 0), (3, 0)),
-    ((0, 1), (0, 3)),
-    ((1, 1), (3, 1)),
-    ((1, 3), (3, 3)),
-    ((1, 1), (1, 3)),
-    ((3, 1), (3, 3)),
-    ((1, 1), (3, 3)),
-)
+THROUGH = ((3, 0), (0, 3), (3, 1), (3, 3), (1, 3), (3, 3), (3, 3))
 
 
 def choose(j, values):
@@ -208,6 +200,8 @@
     share_recv,
     halo_send,
     halo_recv,
+    columns_send,
+    columns_recv,
 ):
     fy = lax.axis_index("fy")
     fx = lax.axis_index("fx")
@@ -257,11 +251,8 @@
     def far(j):
         return choose(j, [o[0] for o in FAR]), choose(j, [o[1] for o in FAR])
 
-    def through(j, r):
-        return (
-            choose(j, [o[r][0] for o in THROUGH]),
-            choose(j, [o[r][1] for o in THROUGH]),
-        )
+    def through(j):
+        return choose(j, [o[0] for o in THROUGH]), choose(j, [o[1] for o in THROUGH])
 
     def near_copy(j):
         return pltpu.make_async_remote_copy(
@@ -276,21 +267,21 @@
     def far_copy(j, r):
         return pltpu.make_async_remote_copy(
             src_ref=sending.at[j, r],
-            dst_ref=relay.at[j, r],
+            dst_ref=arrived.at[fx, 0] if r == 0 else relay.at[j],
             send_sem=tile_send.at[j, r],
-            recv_sem=relay_recv.at[j, r],
-            device_id={"fx": at(*through(j, r))},
-            device_id_type=pl.DeviceIdType.MESH,
-        )
-
-    def relay_copy(j, r):
-        end, mid = far(j), through(j, r)
+            recv_sem=tile_recv.at[fx, 0] if r == 0 else relay_recv.at[j],
+            device_id={"fx": at(*far(j)) if r == 0 else at(*through(j))},
+            device_id_type=pl.DeviceIdType.MESH,
+        )
+
+    def relay_copy(j):
+        end, mid = far(j), through(j)
         source = at(4 - mid[0], 4 - mid[1])
         return pltpu.make_async_remote_copy(
-            src_ref=relay.at[j, r],
-            dst_ref=arrived.at[source, r],
-            send_sem=relay_send.at[j, r],
-            recv_sem=tile_recv.at[source, r],
+            src_ref=relay.at[j],
+            dst_ref=arrived.at[source, 1],
+            send_sem=relay_send.at[j],
+            recv_sem=tile_recv.at[source, 1],
             device_id={"fx": at(end[0] + 4 - mid[0], end[1] + 4 - mid[1])},
             device_id_type=pl.DeviceIdType.MESH,
         )
@@ -360,8 +351,8 @@
 
     def send_far(j, carry):
         prepare(at(*far(j)), j)
+        far_copy(j, 1).start()
         far_copy(j, 0).start()
-        far_copy(j, 1).start()
         return carry
 
     lax.fori_loop(0, len(FAR), send_far, 0)
@@ -372,9 +363,8 @@
 
         @pl.when(j >= 1)
         def _():
-            for r in range(2):
-                far_copy(j - 1, r).wait_recv()
-                relay_copy(j - 1, r).start()
+            far_copy(j - 1, 1).wait_recv()
+            relay_copy(j - 1).start()
 
         return carry
 
@@ -437,7 +427,7 @@
     lax.fori_loop(0, len(NEAR), wait_near, 0)
     lax.fori_loop(0, len(FAR), wait_far, 0)
 
-    def combine(g, carry):
+    def combine(g):
         rows = pl.ds(pl.multiple_of(g * 16, 16), 16)
         gathered = dot(kron[...], arrived[:, :, rows, :].reshape(wide, SIDE))
         pixels = sky[:, rows, :].reshape(CH * 16, SIDE)
@@ -449,14 +439,25 @@
         second = pltpu.roll(new[:, 1, :, :128].reshape(CH // 2 * 16, 128), 64, 1)
         pair = jnp.where(low, new[:, 0, :, :128], second.reshape(CH // 2, 16, 128))
         columns[:, rows, :] = pair.astype(BF)
-        return carry
-
-    lax.fori_loop(0, SIDE // 16, combine, 0)
+
+    chunks = 4
+    deep = SIDE // chunks
+
+    def columns_copy(q):
+        rows = pl.ds(pl.multiple_of(q * deep, deep), deep)
+        return pltpu.make_async_remote_copy(
+            src_ref=columns.at[:, rows, :],
+            dst_ref=beside.at[:, rows, :],
+            send_sem=columns_send.at[q],
+            recv_sem=columns_recv.at[q],
+            device_id={"fx": prev},
+            device_id_type=pl.DeviceIdType.MESH,
+        )
 
     def halo_copy(i):
-        source = (extended.at[:, :HALO, :SIDE], columns, columns.at[:, :HALO, :])[i]
-        target = (extended.at[:, SIDE:, :SIDE], beside, corner)[i]
-        where = ({"fy": up}, {"fx": prev}, {"fy": up, "fx": prev})[i]
+        source = (extended.at[:, :HALO, :SIDE], columns.at[:, :HALO, :])[i]
+        target = (extended.at[:, SIDE:, :SIDE], corner)[i]
+        where = ({"fy": up}, {"fy": up, "fx": prev})[i]
         return pltpu.make_async_remote_copy(
             src_ref=source,
             dst_ref=target,
@@ -466,19 +467,31 @@
             device_id_type=pl.DeviceIdType.MESH,
         )
 
-    for i in range(3):
-        halo_copy(i).start()
-    for i in range(1, 3):
-        halo_copy(i).wait_recv()
-
-    def place(p, carry):
-        for source, begin, end in ((beside, 0, SIDE), (corner, SIDE, TALL)):
+    def make_chunk(q, carry):
+        for i in range(deep // 16):
+            combine(q * (deep // 16) + i)
+        columns_copy(q).start()
+
+        @pl.when(q == 0)
+        def _():
+            for i in range(2):
+                halo_copy(i).start()
+
+        return carry
+
+    lax.fori_loop(0, chunks, make_chunk, 0)
+
+    def place(source, begin, end):
+        for p in range(CH // 2):
             first = source[p]
             extended[2 * p, begin:end, SIDE:] = first
             extended[2 * p + 1, begin:end, SIDE:] = pltpu.roll(first.astype(F32), 64, 1).astype(BF)
-        return carry
-
-    lax.fori_loop(0, CH // 2, place, 0)
+
+    halo_copy(1).wait_recv()
+    place(corner, SIDE, TALL)
+    for q in range(chunks):
+        columns_copy(q).wait_recv()
+        place(beside.at[:, q * deep : (q + 1) * deep, :], q * deep, (q + 1) * deep)
     halo_copy(0).wait_recv()
 
     def finish_shares(k, carry):
@@ -492,14 +505,16 @@
     def finish_far(j, carry):
         for r in range(2):
             far_copy(j, r).wait_send()
-            relay_copy(j, r).wait_send()
+        relay_copy(j).wait_send()
         return carry
 
     lax.fori_loop(1, n_fx, finish_shares, 0)
     lax.fori_loop(0, len(NEAR), finish_near, 0)
     lax.fori_loop(0, len(FAR), finish_far, 0)
-    for i in range(3):
+    for i in range(2):
         halo_copy(i).wait_send()
+    for q in range(chunks):
+        columns_copy(q).wait_send()
 
 
 def passed(value, axes, to):
@@ -529,7 +544,7 @@
             pltpu.VMEM((CH, SIDE, SIDE), F32),
             pltpu.VMEM((n_fx, 2, SIDE, SIDE), BF),
             pltpu.VMEM((n_fx, 2, SIDE, SIDE), BF),
-            pltpu.VMEM((len(FAR), 2, SIDE, SIDE), BF),
+            pltpu.VMEM((len(FAR), SIDE, SIDE), BF),
             pltpu.VMEM((2, 2 * SIDE, SIDE), BF),
             pltpu.VMEM((n_fx, 8, 128), F32),
             pltpu.VMEM((n_fx, 8, 128), F32),
@@ -540,12 +555,14 @@
             dma((2,)),
             dma((n_fx, 2)),
             dma((n_fx, 2)),
-            dma((len(FAR), 2)),
-            dma((len(FAR), 2)),
+            dma((len(FAR),)),
+            dma((len(FAR),)),
             dma((n_fx,)),
             dma((n_fx,)),
-            dma((3,)),
-            dma((3,)),
+            dma((2,)),
+            dma((2,)),
+            dma((4,)),
+            dma((4,)),
         ],
         compiler_params=pltpu.CompilerParams(
             collective_id=0, has_side_effects=True, vmem_limit_bytes=58 * 1024 * 1024

time: 134 us -> 136 us (1.015)
  Pallas kernels: 79 us -> 81.3 us
  waiting for transfers between devices: 18 us -> 16 us
    pallas_call x1, Pallas kernels: 79 us -> 81.3 us  [per_device(): pl.pallas_call(functools.partial(exchange_kernel, n_fy, n_fx), out_shape=...]
    ppermute x3, waiting for transfers between devices: 18 us -> 16 us  [passed(): return lax.ppermute(value, axes if len(axes) > 1 else axes[0], pairs)]
where the time goes in v5:
time: 136 us; the launch traced here: 134 us
  Pallas kernels  81.3 us (60%)
  matrix products  29.3 us (22%)
  waiting for transfers between devices  16 us (12%)
  starting transfers between devices  4.07 us (3%)
  other arithmetic  3.29 us (2%)
    pallas_call x1, Pallas kernels, per_device(): pl.pallas_call(functools.partial(exchange_kernel, n_fy, n_fx), out_shape=...  81.3 us
    dot_general x1, matrix products, per_device(): jnp.einsum('bcyx,bkx->bcyk', row_sec, columns, preferred_element_type=F32)  16.7 us
    ppermute x3, waiting for transfers between devices, passed(): return lax.ppermute(value, axes if len(axes) > 1 else axes[0], pairs)  16 us
    dot_general x1, matrix products, per_device(): jnp.einsum('bkn,bckx->cnx', rows, col_sec, preferred_element_type=F32)  12.6 us
    ppermute x3, starting transfers between devices, passed(): return lax.ppermute(value, axes if len(axes) > 1 else axes[0], pairs)  4.07 us
    max x1, other arithmetic, per_device(): return jnp.maximum(summed * (1.0 / BASES), 0.0)  3.29 us
  transfers between devices with their start and end apart: 3, of which 1 were waited for; matrix products, arithmetic and copies ran while one was open for 0% of the time, Pallas kernels for 0%

profile of v5, /device:TPU:1, one launch (start us, length us, event | category | flops | bytes accessed | tf_op | source)
XLA Modules:
  0.0 134.1 jit_solution(10022495996467876079)
XLA Ops:
  0.0 0.0 copy-start.1
  0.0 81.3 %shard_map.109 = bf16[8,304,384]{2,1,0:T(8,128)(2,1)} custom-call(s32[16]{0:T(128)} %bitcast.25, s32[16]{0:T(128)} %chan_ref.1, s32[16]{0:T(128)} %count_ref.1, bf16[512,512]{1,0:T(8,128)(2,1)} %constant.20.clone.fourier, bf16[256,512]{1,0:T(8,128)(2,1)} %constant.21.clone.back, bf16[256,256]{1,0:T(8,128)(2,1)} %constant.22.clone.excess, ...), custom_call_target="tpu_custom_call" | custom-call | tf_op jit(solution)/shard_map/pallas_call | solution.py:536
  81.3 0.0 copy-done.1
  81.3 0.0 copy-start
  81.3 16.7 %fusion.2 = bf16[8,8,256,256]{3,2,1,0:T(8,128)(2,1)} fusion(bf16[8,8,256,256]{3,2,1,0:T(8,128)(2,1)} %param.16, bf16[8,256,384,1]{2,1,3,0:T(8,128)(2,1)S(1)} %copy-done.1, bf16[8,256,304,1]{1,2,3,0:T(8,128)(2,1)} %constant.33, bf16[8,304,384]{2,1,0:T(8,128)(2,1)} %shard_map.109), kind=kOutput, calls=%fused_computation.4 | convolution fusion | flops 7077888000 | bytes 21463040 | tf_op jit(solution)/shard_map/bcyx,bkx->bcyk/dot_general | solution.py:582
  98.0 0.0 copy-done
  98.0 12.6 %fusion.27 = (bf16[8,304,384]{2,1,0:T(8,128)(2,1)S(1)}, f32[8,304,384]{2,1,0:T(8,128)}) fusion(bf16[8,256,304,1]{1,2,0,3:T(8,128)(2,1)} %constant.36, bf16[8,256,384,1]{2,1,0,3:T(8,128)(2,1)S(1)} %copy-done, bf16[8,8,256,256]{3,2,1,0:T(8,128)(2,1)} %fusion.2), kind=kOutput, calls=%fused_computation.20 | convolution fusion | flops 7053656064 | bytes 16809984 | tf_op jit(solution)/shard_map/bkn,bckx->cnx/dot_general | solution.py:586
  110.6 2.9 %collective-permute-start.1 = (bf16[8,48,256]{2,1,0:T(8,128)(2,1)S(1)}, bf16[8,48,256]{2,1,0:T(8,128)(2,1)S(1)}, u32[]{:S(2)}, u32[]{:S(2)}) collective-permute-start(bf16[8,48,256]{2,1,0:T(8,128)(2,1)S(1)} %slice.18), channel_id=1, source_target_pairs={{0,16},{16,32},{32,48},{48,64},{64,80},{80,96},{96,112},{112,0},{1... | collective-permute-start | bytes 589832 | tf_op jit(solution)/shard_map/ppermute | solution.py:526
  113.6 0.1 slice.17
  113.7 1.1 collective-permute-start
  114.7 0.1 collective-permute-start.2
  114.8 16.0 %collective-permute-done.2 = bf16[8,48,48]{2,1,0:T(8,128)(2,1)S(1)} collective-permute-done((bf16[8,48,48]{2,1,0:T(8,128)(2,1)S(1)}, bf16[8,48,48]{2,1,0:T(8,128)(2,1)S(1)}, u32[]{:S(2)}, u32[]{:S(2)}) %collective-permute-start.2) | collective-permute-done | bytes 36896 | tf_op jit(solution)/shard_map/ppermute | solution.py:526
  130.9 0.0 collective-permute-done.1
  130.9 0.0 collective-permute-done
  130.9 3.3 %fusion.19 = f32[8,256,256]{2,1,0:T(8,128)} fusion(f32[8,304,384]{2,1,0:T(8,128)} %get-tuple-element.6, bf16[8,48,48]{2,1,0:T(8,128)(2,1)S(1)} %collective-permute-done.2, bf16[8,48,256]{2,1,0:T(8,128)(2,1)S(1)} %collective-permute-done.1, bf16[8,256,48]{2,1,0:T(8,128)(2,1)S(1)} %collective-permute-done), kind=kLoop, calls=%fused_computation.17 | loop fusion | flops 4194304 | bytes 4624384 | tf_op jit(solution)/shard_map/max | solution.py:595
  (2 shorter events, 0.0 us)
Async XLA Ops:
  0.0 81.3 %copy-start.1 = (bf16[8,256,384,1]{2,1,3,0:T(8,128)(2,1)S(1)}, bf16[8,256,384,1]{2,1,3,0:T(8,128)(2,1)}, u32[]{:S(2)}) copy-start(bf16[8,256,384,1]{2,1,3,0:T(8,128)(2,1)} %constant.34) | copy-start | bytes 4718596
  81.3 16.7 %copy-start = (bf16[8,256,384,1]{2,1,0,3:T(8,128)(2,1)S(1)}, bf16[8,256,384,1]{2,1,0,3:T(8,128)(2,1)}, u32[]{:S(2)}) copy-start(bf16[8,256,384,1]{2,1,0,3:T(8,128)(2,1)} %constant.35) | copy-start | bytes 4718596
  110.6 20.2 %collective-permute-start.1 = (bf16[8,48,256]{2,1,0:T(8,128)(2,1)S(1)}, bf16[8,48,256]{2,1,0:T(8,128)(2,1)S(1)}, u32[]{:S(2)}, u32[]{:S(2)}) collective-permute-start(bf16[8,48,256]{2,1,0:T(8,128)(2,1)S(1)} %slice.18), channel_id=1, source_target_pairs={{0,16},{16,32},{32,48},{48,64},{64,80},{80,96},{96,112},{112,0},{1... | collective-permute-start | bytes 589832 | tf_op jit(solution)/shard_map/ppermute | solution.py:526
  113.7 17.2 %collective-permute-start = (bf16[8,256,48]{2,1,0:T(8,128)(2,1)S(1)}, bf16[8,256,48]{2,1,0:T(8,128)(2,1)S(1)}, u32[]{:S(2)}, u32[]{:S(2)}) collective-permute-start(bf16[8,256,48]{2,1,0:T(8,128)(2,1)S(1)} %slice.17), channel_id=1, source_target_pairs={{0,1},{1,2},{2,3},{3,4},{4,5},{5,6},{6,7},{7,8},{8,9},{9,10},{10,1... | collective-permute-start | bytes 589832 | tf_op jit(solution)/shard_map/ppermute | solution.py:526
  114.7 16.1 %collective-permute-start.2 = (bf16[8,48,48]{2,1,0:T(8,128)(2,1)S(1)}, bf16[8,48,48]{2,1,0:T(8,128)(2,1)S(1)}, u32[]{:S(2)}, u32[]{:S(2)}) collective-permute-start(bf16[8,48,48]{2,1,0:T(8,128)(2,1)S(1)} %slice.19), channel_id=1, source_target_pairs={{0,17},{1,18},{2,19},{3,20},{4,21},{5,22},{6,23},{7,24},{8,25},{9,... | collective-permute-start | bytes 110600 | tf_op jit(solution)/shard_map/ppermute | solution.py:526

commit v6 on v5

--- a/solution.py
+++ b/solution.py
@@ -152,7 +152,7 @@
 
 NEAR = ((1, 0), (0, 1), (3, 0), (0, 3), (1, 1), (3, 3), (1, 3), (3, 1))
 FAR = ((2, 0), (0, 2), (2, 1), (2, 3), (1, 2), (3, 2), (2, 2))
-THROUGH = ((3, 0), (0, 3), (3, 1), (3, 3), (1, 3), (3, 3), (3, 3))
+THROUGH = ((1, 0), (0, 1), (1, 1), (1, 3), (1, 1), (3, 1), (1, 1))
 
 
 def choose(j, values):
@@ -582,16 +582,23 @@
     coefficient = jnp.einsum("bcyx,bkx->bcyk", row_sec, columns, preferred_element_type=F32)
     limits = thresholds.astype(F32)
     shrunk = (coefficient - jnp.clip(coefficient, -limits, limits)).astype(BF)
-    col_sec = jnp.einsum("bcyk,bkx->bcyx", shrunk, columns, preferred_element_type=F32).astype(BF)
-    cells = jnp.einsum("bkn,bckx->cnx", rows, col_sec, preferred_element_type=F32)
-    spill = cells.astype(BF)
-    from_left = passed(spill[:, :SIDE, SIDE:TALL], ("fx",), (1,)).astype(F32)
-    from_above = passed(spill[:, SIDE:, :SIDE], ("fy",), (1,)).astype(F32)
-    from_corner = passed(spill[:, SIDE:, SIDE:TALL], ("fy", "fx"), (1, 1)).astype(F32)
-    left = jnp.pad(from_left, ((0, 0), (0, 0), (0, SIDE - HALO)))
+    near_rows, far_rows = rows[:, :, :SIDE], rows[:, :, SIDE:]
+    near_columns, far_columns = columns[:, :, :SIDE], columns[:, :, SIDE:]
+    side = jnp.einsum("bcyk,bkx->bcyx", shrunk, far_columns, preferred_element_type=F32).astype(BF)
+    right = jnp.einsum("bkn,bckx->cnx", rows, side, preferred_element_type=F32).astype(BF)
+    from_left = passed(right[:, :SIDE], ("fx",), (1,)).astype(F32)
+    from_corner = passed(right[:, SIDE:], ("fy", "fx"), (1, 1)).astype(F32)
+    low = jnp.einsum("bkn,bckx->bcnx", far_rows, shrunk, preferred_element_type=F32).astype(BF)
+    bottom = jnp.einsum("bcnk,bkx->cnx", low, near_columns, preferred_element_type=F32).astype(BF)
+    from_above = passed(bottom, ("fy",), (1,)).astype(F32)
+    col_sec = jnp.einsum(
+        "bcyk,bkx->bcyx", shrunk, near_columns, preferred_element_type=F32
+    ).astype(BF)
+    cells = jnp.einsum("bkn,bckx->cnx", near_rows, col_sec, preferred_element_type=F32)
+    left = jnp.pad(from_left, ((0, 0), (0, 0), (0, 128)))
     above = jnp.pad(from_above, ((0, 0), (0, SIDE - HALO), (0, 0)))
-    corner = jnp.pad(from_corner, ((0, 0), (0, SIDE - HALO), (0, SIDE - HALO)))
-    summed = cells[:, :SIDE, :SIDE] + left + above + corner
+    corner = jnp.pad(from_corner, ((0, 0), (0, SIDE - HALO), (0, 128)))
+    summed = cells + left + above + corner
     return jnp.maximum(summed * (1.0 / BASES), 0.0)
 
 

time: 136 us -> 134 us (0.985)
  matrix products: 29.3 us -> 37.6 us
  waiting for transfers between devices: 16 us -> 10.8 us
  other arithmetic: 3.29 us -> 0 us
  Pallas kernels: 81.3 us -> 79.8 us
    dot_general x1 -> x3, matrix products: 12.6 us -> 20.8 us  [the longest x1 7.96 us: per_device(): jnp.einsum('bkn,bckx->cnx', near_rows, col_sec, preferred_element_type=F32)]
    ppermute x3, waiting for transfers between devices: 16 us -> 10.8 us  [passed(): return lax.ppermute(value, axes if len(axes) > 1 else axes[0], pairs)]
    max x1 -> x0, other arithmetic: 3.29 us -> none  [per_device(): return jnp.maximum(summed * (1.0 / BASES), 0.0)]
    pallas_call x1, Pallas kernels: 81.3 us -> 79.8 us  [per_device(): pl.pallas_call(functools.partial(exchange_kernel, n_fy, n_fx), out_shape=...]
  transfers between devices with their start and end apart: 3 -> 3, of which waited for: 1 -> 1; matrix products, arithmetic and copies ran while one was open for 0% -> 4% of each run, Pallas kernels for 0% -> 0%
where the time goes in v6:
time: 134 us; the launch traced here: 133 us
  Pallas kernels  79.8 us (60%)
  matrix products  37.6 us (28%)
  waiting for transfers between devices  10.8 us (8%)
  starting transfers between devices  5.18 us (4%)
    pallas_call x1, Pallas kernels, per_device(): pl.pallas_call(functools.partial(exchange_kernel, n_fy, n_fx), out_shape=...  79.8 us
    dot_general x1, matrix products, per_device(): jnp.einsum('bcyx,bkx->bcyk', row_sec, columns, preferred_element_type=F32)  16.7 us
    ppermute x3, waiting for transfers between devices, passed(): return lax.ppermute(value, axes if len(axes) > 1 else axes[0], pairs)  10.8 us
    dot_general x1, matrix products, per_device(): jnp.einsum('bkn,bckx->cnx', near_rows, col_sec, preferred_element_type=F32)  7.96 us
    dot_general x1, matrix products, per_device(): jnp.einsum('bkn,bckx->cnx', rows, side, preferred_element_type=F32)  7.02 us
    dot_general x1, matrix products, per_device(): jnp.einsum('bcnk,bkx->cnx', low, near_columns, preferred_element_type=F32)  5.84 us
    ppermute x3, starting transfers between devices, passed(): return lax.ppermute(value, axes if len(axes) > 1 else axes[0], pairs)  5.18 us
  transfers between devices with their start and end apart: 3, of which 1 were waited for; matrix products, arithmetic and copies ran while one was open for 4% of the time, Pallas kernels for 0%

profile of v6, /device:TPU:1, one launch (start us, length us, event | category | flops | bytes accessed | tf_op | source)
XLA Modules:
  0.0 133.5 jit_solution(7001086021291003542)
XLA Ops:
  0.0 0.0 copy-start
  0.0 79.8 %shard_map.109 = bf16[8,304,384]{2,1,0:T(8,128)(2,1)} custom-call(s32[16]{0:T(128)} %bitcast.60, s32[16]{0:T(128)} %chan_ref.1, s32[16]{0:T(128)} %count_ref.1, bf16[512,512]{1,0:T(8,128)(2,1)} %constant.20.clone.fourier, bf16[256,512]{1,0:T(8,128)(2,1)} %constant.21.clone.back, bf16[256,256]{1,0:T(8,128)(2,1)} %constant.22.clone.excess, ...), custom_call_target="tpu_custom_call" | custom-call | tf_op jit(solution)/shard_map/pallas_call | solution.py:536
  79.8 0.0 copy-done
  79.8 0.0 copy-start.1
  79.8 0.0 copy-start.3
  79.8 16.7 %fusion.2 = bf16[8,8,256,256]{3,2,1,0:T(8,128)(2,1)} fusion(bf16[8,8,256,256]{3,2,1,0:T(8,128)(2,1)} %param.16, bf16[8,256,384,1]{2,1,3,0:T(8,128)(2,1)S(1)} %copy-done, bf16[8,256,304,1]{1,2,3,0:T(8,128)(2,1)} %constant.37, bf16[8,304,384]{2,1,0:T(8,128)(2,1)} %shard_map.109), kind=kOutput, calls=%fused_computation.4 | convolution fusion | flops 7077888000 | bytes 21463040 | tf_op jit(solution)/shard_map/bcyx,bkx->bcyk/dot_general | solution.py:582
  96.6 0.0 copy-done.1
  96.6 0.0 copy-done.3
  96.6 7.0 %fusion.49 = bf16[8,304,128]{2,1,0:T(8,128)(2,1)S(1)} fusion(bf16[8,256,304,1]{1,2,0,3:T(8,128)(2,1)S(1)} %copy-done.1, bf16[8,256,128,1]{2,1,0,3:T(8,128)(2,1)S(1)} %copy-done.3, bf16[8,8,256,256]{3,2,1,0:T(8,128)(2,1)} %fusion.2), kind=kOutput, calls=%fused_computation.30 | convolution fusion | flops 2351218688 | bytes 10780672 | tf_op jit(solution)/shard_map/bkn,bckx->cnx/dot_general | solution.py:588
  103.7 0.0 copy-start.2
  103.7 1.1 collective-permute-start
  104.7 5.8 %fusion.63 = bf16[8,48,256]{2,1,0:T(8,128)(2,1)S(1)} fusion(bf16[8,256,256,1]{2,1,0,3:T(8,128)(2,1)} %constant.39, bf16[8,256,48,1]{2,1,0,3:T(8,128)(2,1)} %constant.42, bf16[8,8,256,256]{3,2,1,0:T(8,128)(2,1)} %fusion.2), kind=kOutput, calls=%fused_computation.32 | convolution fusion | flops 806191104 | bytes 9830400 | tf_op jit(solution)/shard_map/bcnk,bkx->cnx/dot_general | solution.py:592
  110.6 3.0 %collective-permute-start.1 = (bf16[8,48,256]{2,1,0:T(8,128)(2,1)S(1)}, bf16[8,48,256]{2,1,0:T(8,128)(2,1)S(1)}, u32[]{:S(2)}, u32[]{:S(2)}) collective-permute-start(bf16[8,48,256]{2,1,0:T(8,128)(2,1)S(1)} %fusion.63), channel_id=1, source_target_pairs={{0,16},{16,32},{32,48},{48,64},{64,80},{80,96},{96,112},{112,0},{1... | collective-permute-start | bytes 589832 | tf_op jit(solution)/shard_map/ppermute | solution.py:526
  113.6 1.1 collective-permute-start.2
  114.7 10.8 %collective-permute-done.2 = bf16[8,48,128]{2,1,0:T(8,128)(2,1)S(1)} collective-permute-done((bf16[8,48,128]{2,1,0:T(8,128)(2,1)S(1)}, bf16[8,48,128]{2,1,0:T(8,128)(2,1)S(1)}, u32[]{:S(2)}, u32[]{:S(2)}) %collective-permute-start.2) | collective-permute-done | bytes 98336 | tf_op jit(solution)/shard_map/ppermute | solution.py:526
  125.5 0.0 collective-permute-done.1
  125.5 0.0 collective-permute-done
  125.5 0.0 copy-done.2
  125.5 8.0 %fusion.31 = f32[8,256,256]{2,1,0:T(8,128)} fusion(bf16[8,48,128]{2,1,0:T(8,128)(2,1)S(1)} %collective-permute-done.2, bf16[8,48,256]{2,1,0:T(8,128)(2,1)S(1)} %collective-permute-done.1, bf16[8,256,128]{2,1,0:T(8,128)(2,1)S(1)} %collective-permute-done, bf16[8,256,256,1]{2,1,0,3:T(8,128)(2,1)S(1)} %copy-done.2, bf16[8,8,256,256]{3,2,1,0:T(8,128)(2,1)} %fusion.2), kind=kOutput, calls=%fused_computation.23 | convolution fusion | flops 4303355904 | bytes 12353536 | tf_op jit(solution)/shard_map/bkn,bckx->cnx/dot_general | solution.py:597
  (2 shorter events, 0.0 us)
Async XLA Ops:
  0.0 79.8 %copy-start = (bf16[8,256,384,1]{2,1,3,0:T(8,128)(2,1)S(1)}, bf16[8,256,384,1]{2,1,3,0:T(8,128)(2,1)}, u32[]{:S(2)}) copy-start(bf16[8,256,384,1]{2,1,3,0:T(8,128)(2,1)} %constant.38) | copy-start | bytes 4718596
  79.8 16.8 %copy-start.1 = (bf16[8,256,304,1]{1,2,0,3:T(8,128)(2,1)S(1)}, bf16[8,256,304,1]{1,2,0,3:T(8,128)(2,1)}, u32[]{:S(2)}) copy-start(bf16[8,256,304,1]{1,2,0,3:T(8,128)(2,1)} %constant.41) | copy-start | bytes 3735556
  79.8 16.8 %copy-start.3 = (bf16[8,256,128,1]{2,1,0,3:T(8,128)(2,1)S(1)}, bf16[8,256,128,1]{2,1,0,3:T(8,128)(2,1)}, u32[]{:S(2)}) copy-start(bf16[8,256,128,1]{2,1,0,3:T(8,128)(2,1)} %constant.40) | copy-start | bytes 1572868
  103.7 21.8 %copy-start.2 = (bf16[8,256,256,1]{2,1,0,3:T(8,128)(2,1)S(1)}, bf16[8,256,256,1]{2,1,0,3:T(8,128)(2,1)}, u32[]{:S(2)}) copy-start(bf16[8,256,256,1]{2,1,0,3:T(8,128)(2,1)} %constant.39) | copy-start | bytes 3145732
  103.7 21.8 %collective-permute-start = (bf16[8,256,128]{2,1,0:T(8,128)(2,1)S(1)}, bf16[8,256,128]{2,1,0:T(8,128)(2,1)S(1)}, u32[]{:S(2)}, u32[]{:S(2)}) collective-permute-start(bf16[8,256,128]{2,1,0:T(8,128)(2,1)S(1)} %slice.24), channel_id=1, source_target_pairs={{0,1},{1,2},{2,3},{3,4},{4,5},{5,6},{6,7},{7,8},{8,9},{9,10},{10,1... | collective-permute-start | bytes 1572872 | tf_op jit(solution)/shard_map/ppermute | solution.py:526
  110.6 14.9 %collective-permute-start.1 = (bf16[8,48,256]{2,1,0:T(8,128)(2,1)S(1)}, bf16[8,48,256]{2,1,0:T(8,128)(2,1)S(1)}, u32[]{:S(2)}, u32[]{:S(2)}) collective-permute-start(bf16[8,48,256]{2,1,0:T(8,128)(2,1)S(1)} %fusion.63), channel_id=1, source_target_pairs={{0,16},{16,32},{32,48},{48,64},{64,80},{80,96},{96,112},{112,0},{1... | collective-permute-start | bytes 589832 | tf_op jit(solution)/shard_map/ppermute | solution.py:526
  113.6 11.9 %collective-permute-start.2 = (bf16[8,48,128]{2,1,0:T(8,128)(2,1)S(1)}, bf16[8,48,128]{2,1,0:T(8,128)(2,1)S(1)}, u32[]{:S(2)}, u32[]{:S(2)}) collective-permute-start(bf16[8,48,128]{2,1,0:T(8,128)(2,1)S(1)} %slice.25), channel_id=1, source_target_pairs={{0,17},{1,18},{2,19},{3,20},{4,21},{5,22},{6,23},{7,24},{8,25},{9,... | collective-permute-start | bytes 294920 | tf_op jit(solution)/shard_map/ppermute | solution.py:526

commit v7 on v5

--- a/solution.py
+++ b/solution.py
@@ -7,6 +7,7 @@
 import numpy as np
 from jax import lax
 from jax.experimental import pallas as pl
+from jax.experimental.layout import Layout, with_layout_constraint
 from jax.experimental.pallas import tpu as pltpu
 from jax.sharding import PartitionSpec as P
 
@@ -152,7 +153,15 @@
 
 NEAR = ((1, 0), (0, 1), (3, 0), (0, 3), (1, 1), (3, 3), (1, 3), (3, 1))
 FAR = ((2, 0), (0, 2), (2, 1), (2, 3), (1, 2), (3, 2), (2, 2))
-THROUGH = ((3, 0), (0, 3), (3, 1), (3, 3), (1, 3), (3, 3), (3, 3))
+THROUGH = (
+    ((1, 0), (3, 0)),
+    ((0, 1), (0, 3)),
+    ((1, 1), (3, 1)),
+    ((1, 3), (3, 3)),
+    ((1, 1), (1, 3)),
+    ((3, 1), (3, 3)),
+    ((1, 1), (3, 3)),
+)
 
 
 def choose(j, values):
@@ -251,15 +260,18 @@
     def far(j):
         return choose(j, [o[0] for o in FAR]), choose(j, [o[1] for o in FAR])
 
-    def through(j):
-        return choose(j, [o[0] for o in THROUGH]), choose(j, [o[1] for o in THROUGH])
-
-    def near_copy(j):
+    def through(j, r):
+        return (
+            choose(j, [o[r][0] for o in THROUGH]),
+            choose(j, [o[r][1] for o in THROUGH]),
+        )
+
+    def near_copy(j, r):
         return pltpu.make_async_remote_copy(
-            src_ref=sending.at[len(FAR) + j],
-            dst_ref=arrived.at[fx],
-            send_sem=tile_send.at[len(FAR) + j, 0],
-            recv_sem=tile_recv.at[fx, 0],
+            src_ref=sending.at[len(FAR) + j, r],
+            dst_ref=arrived.at[fx, r],
+            send_sem=tile_send.at[len(FAR) + j, r],
+            recv_sem=tile_recv.at[fx, r],
             device_id={"fx": at(*near(j))},
             device_id_type=pl.DeviceIdType.MESH,
         )
@@ -267,40 +279,26 @@
     def far_copy(j, r):
         return pltpu.make_async_remote_copy(
             src_ref=sending.at[j, r],
-            dst_ref=arrived.at[fx, 0] if r == 0 else relay.at[j],
+            dst_ref=relay.at[j, r],
             send_sem=tile_send.at[j, r],
-            recv_sem=tile_recv.at[fx, 0] if r == 0 else relay_recv.at[j],
-            device_id={"fx": at(*far(j)) if r == 0 else at(*through(j))},
+            recv_sem=relay_recv.at[j, r],
+            device_id={"fx": at(*through(j, r))},
             device_id_type=pl.DeviceIdType.MESH,
         )
 
-    def relay_copy(j):
-        end, mid = far(j), through(j)
+    def relay_copy(j, r):
+        end, mid = far(j), through(j, r)
         source = at(4 - mid[0], 4 - mid[1])
         return pltpu.make_async_remote_copy(
-            src_ref=relay.at[j],
-            dst_ref=arrived.at[source, 1],
-            send_sem=relay_send.at[j],
-            recv_sem=tile_recv.at[source, 1],
+            src_ref=relay.at[j, r],
+            dst_ref=arrived.at[source, r],
+            send_sem=relay_send.at[j, r],
+            recv_sem=tile_recv.at[source, r],
             device_id={"fx": at(end[0] + 4 - mid[0], end[1] + 4 - mid[1])},
             device_id_type=pl.DeviceIdType.MESH,
         )
 
-    def near_arrival(j):
-        dx, dz = near(j)
-        source = at(4 - dx, 4 - dz)
-        return pltpu.make_async_remote_copy(
-            src_ref=arrived.at[source],
-            dst_ref=arrived.at[source],
-            send_sem=tile_send.at[0, 0],
-            recv_sem=tile_recv.at[source, 0],
-            device_id={"fx": source},
-            device_id_type=pl.DeviceIdType.MESH,
-        )
-
-    def far_arrival(j, r):
-        dx, dz = far(j)
-        source = at(4 - dx, 4 - dz)
+    def arrival(source, r):
         return pltpu.make_async_remote_copy(
             src_ref=arrived.at[source, r],
             dst_ref=arrived.at[source, r],
@@ -351,20 +349,22 @@
 
     def send_far(j, carry):
         prepare(at(*far(j)), j)
+        far_copy(j, 0).start()
         far_copy(j, 1).start()
-        far_copy(j, 0).start()
         return carry
 
     lax.fori_loop(0, len(FAR), send_far, 0)
 
     def send_near(j, carry):
         prepare(at(*near(j)), len(FAR) + j)
-        near_copy(j).start()
+        near_copy(j, 0).start()
+        near_copy(j, 1).start()
 
         @pl.when(j >= 1)
         def _():
-            far_copy(j - 1, 1).wait_recv()
-            relay_copy(j - 1).start()
+            for r in range(2):
+                far_copy(j - 1, r).wait_recv()
+                relay_copy(j - 1, r).start()
 
         return carry
 
@@ -415,17 +415,12 @@
     kron[...] = jnp.where(diagonal, widened, 0.0).astype(BF)
     scale = 1.0 / (1.0 + totals)
 
-    def wait_near(j, carry):
-        near_arrival(j).wait_recv()
-        return carry
-
-    def wait_far(j, carry):
+    def wait_tiles(k, carry):
         for r in range(2):
-            far_arrival(j, r).wait_recv()
-        return carry
-
-    lax.fori_loop(0, len(NEAR), wait_near, 0)
-    lax.fori_loop(0, len(FAR), wait_far, 0)
+            arrival(peer(k), r).wait_recv()
+        return carry
+
+    lax.fori_loop(1, n_fx, wait_tiles, 0)
 
     def combine(g):
         rows = pl.ds(pl.multiple_of(g * 16, 16), 16)
@@ -499,13 +494,14 @@
         return carry
 
     def finish_near(j, carry):
-        near_copy(j).wait_send()
+        for r in range(2):
+            near_copy(j, r).wait_send()
         return carry
 
     def finish_far(j, carry):
         for r in range(2):
             far_copy(j, r).wait_send()
-        relay_copy(j).wait_send()
+            relay_copy(j, r).wait_send()
         return carry
 
     lax.fori_loop(1, n_fx, finish_shares, 0)
@@ -544,7 +540,7 @@
             pltpu.VMEM((CH, SIDE, SIDE), F32),
             pltpu.VMEM((n_fx, 2, SIDE, SIDE), BF),
             pltpu.VMEM((n_fx, 2, SIDE, SIDE), BF),
-            pltpu.VMEM((len(FAR), SIDE, SIDE), BF),
+            pltpu.VMEM((len(FAR), 2, SIDE, SIDE), BF),
             pltpu.VMEM((2, 2 * SIDE, SIDE), BF),
             pltpu.VMEM((n_fx, 8, 128), F32),
             pltpu.VMEM((n_fx, 8, 128), F32),
@@ -555,8 +551,8 @@
             dma((2,)),
             dma((n_fx, 2)),
             dma((n_fx, 2)),
-            dma((len(FAR),)),
-            dma((len(FAR),)),
+            dma((len(FAR), 2)),
+            dma((len(FAR), 2)),
             dma((n_fx,)),
             dma((n_fx,)),
             dma((2,)),
@@ -578,12 +574,13 @@
         vis_tiles,
     )
     rows, columns = made["rows"], made["columns"]
-    row_sec = jnp.einsum("bkn,cnx->bckx", rows, extended, preferred_element_type=F32).astype(BF)
-    coefficient = jnp.einsum("bcyx,bkx->bcyk", row_sec, columns, preferred_element_type=F32)
+    col_sec = jnp.einsum("cyx,bkx->bcyk", extended, columns, preferred_element_type=F32).astype(BF)
+    coefficient = jnp.einsum("bjy,bcyk->bcjk", rows, col_sec, preferred_element_type=F32)
+    coefficient = with_layout_constraint(coefficient, Layout(major_to_minor=(0, 1, 2, 3)))
     limits = thresholds.astype(F32)
     shrunk = (coefficient - jnp.clip(coefficient, -limits, limits)).astype(BF)
-    col_sec = jnp.einsum("bcyk,bkx->bcyx", shrunk, columns, preferred_element_type=F32).astype(BF)
-    cells = jnp.einsum("bkn,bckx->cnx", rows, col_sec, preferred_element_type=F32)
+    row_sec = jnp.einsum("bjy,bcjk->bcyk", rows, shrunk, preferred_element_type=F32).astype(BF)
+    cells = jnp.einsum("bcyk,bkx->cyx", row_sec, columns, preferred_element_type=F32)
     spill = cells.astype(BF)
     from_left = passed(spill[:, :SIDE, SIDE:TALL], ("fx",), (1,)).astype(F32)
     from_above = passed(spill[:, SIDE:, :SIDE], ("fy",), (1,)).astype(F32)

time: 136 us -> 128 us (0.941)
  Pallas kernels: 81.3 us -> 69.4 us
  waiting for transfers between devices: 16 us -> 18.2 us
    pallas_call x1, Pallas kernels: 81.3 us -> 69.4 us  [per_device(): pl.pallas_call(functools.partial(exchange_kernel, n_fy, n_fx), out_shape=...]
    ppermute x3, waiting for transfers between devices: 16 us -> 18.2 us  [passed(): return lax.ppermute(value, axes if len(axes) > 1 else axes[0], pairs)]
  transfers between devices with their start and end apart: 3 -> 3, of which waited for: 1 -> 2; matrix products, arithmetic and copies ran while one was open for 0% -> 0% of each run, Pallas kernels for 0% -> 0%
where the time goes in v7:
time: 128 us; the launch traced here: 126 us
  Pallas kernels  69.4 us (54%)
  matrix products  29.9 us (23%)
  waiting for transfers between devices  18.2 us (14%)
  starting transfers between devices  4.97 us (4%)
  other arithmetic  3.28 us (3%)
    pallas_call x1, Pallas kernels, per_device(): pl.pallas_call(functools.partial(exchange_kernel, n_fy, n_fx), out_shape=...  69.4 us
    ppermute x3, waiting for transfers between devices, passed(): return lax.ppermute(value, axes if len(axes) > 1 else axes[0], pairs)  18.2 us
    dot_general x1, matrix products, per_device(): jnp.einsum('bjy,bcyk->bcjk', rows, col_sec, preferred_element_type=F32)  18 us
    dot_general x1, matrix products, per_device(): jnp.einsum('bcyk,bkx->cyx', row_sec, columns, preferred_element_type=F32)  11.9 us
    ppermute x3, starting transfers between devices, passed(): return lax.ppermute(value, axes if len(axes) > 1 else axes[0], pairs)  4.97 us
    max x1, other arithmetic, per_device(): return jnp.maximum(summed * (1.0 / BASES), 0.0)  3.28 us
  transfers between devices with their start and end apart: 3, of which 2 were waited for; matrix products, arithmetic and copies ran while one was open for 0% of the time, Pallas kernels for 0%

profile of v7, /device:TPU:1, one launch (start us, length us, event | category | flops | bytes accessed | tf_op | source)
XLA Modules:
  0.0 126.0 jit_solution(5049517822193989186)
XLA Ops:
  0.0 0.0 copy-start.1
  0.0 69.4 %shard_map.109 = bf16[8,304,384]{2,1,0:T(8,128)(2,1)} custom-call(s32[16]{0:T(128)} %bitcast.32, s32[16]{0:T(128)} %chan_ref.1, s32[16]{0:T(128)} %count_ref.1, bf16[512,512]{1,0:T(8,128)(2,1)} %constant.20.clone.fourier, bf16[256,512]{1,0:T(8,128)(2,1)} %constant.21.clone.back, bf16[256,256]{1,0:T(8,128)(2,1)} %constant.22.clone.excess, ...), custom_call_target="tpu_custom_call" | custom-call | tf_op jit(solution)/shard_map/pallas_call | solution.py:532
  69.4 0.0 copy-done.1
  69.5 0.0 copy-start
  69.5 18.0 %fusion.2 = bf16[8,8,256,256]{3,2,1,0:T(8,128)(2,1)} fusion(bf16[8,8,256,256]{3,2,1,0:T(8,128)(2,1)} %param.16, bf16[8,256,304,1]{1,2,3,0:T(8,128)(2,1)} %constant.34, bf16[8,256,384,1]{2,1,3,0:T(8,128)(2,1)S(1)} %copy-done.1, bf16[8,304,384]{2,1,0:T(8,128)(2,1)} %shard_map.109), kind=kOutput, calls=%fused_computation.4 | convolution fusion | flops 6405488640 | bytes 21463040 | tf_op jit(solution)/shard_map/bjy,bcyk->bcjk/dot_general | solution.py:578
  87.5 0.0 copy-done
  87.5 11.9 %fusion.30 = (bf16[8,304,384]{2,1,0:T(8,128)(2,1)S(1)}, f32[8,304,384]{2,1,0:T(8,128)}) fusion(bf16[8,256,384,1]{2,1,0,3:T(8,128)(2,1)S(1)} %copy-done, bf16[8,256,304,1]{1,2,0,3:T(8,128)(2,1)} %constant.35, bf16[8,8,256,256]{3,2,1,0:T(8,128)(2,1)} %fusion.2), kind=kOutput, calls=%fused_computation.21 | convolution fusion | flops 6381256704 | bytes 16809984 | tf_op jit(solution)/shard_map/bcyk,bkx->cyx/dot_general | solution.py:583
  99.4 2.7 %collective-permute-start.1 = (bf16[8,48,256]{2,1,0:T(8,128)(2,1)S(1)}, bf16[8,48,256]{2,1,0:T(8,128)(2,1)S(1)}, u32[]{:S(2)}, u32[]{:S(2)}) collective-permute-start(bf16[8,48,256]{2,1,0:T(8,128)(2,1)S(1)} %slice.18), channel_id=1, source_target_pairs={{0,16},{16,32},{32,48},{48,64},{64,80},{80,96},{96,112},{112,0},{1... | collective-permute-start | bytes 589832 | tf_op jit(solution)/shard_map/ppermute | solution.py:522
  102.1 0.1 slice.17
  102.2 0.3 collective-permute-start
  102.5 2.0 %collective-permute-start.2 = (bf16[8,48,48]{2,1,0:T(8,128)(2,1)S(1)}, bf16[8,48,48]{2,1,0:T(8,128)(2,1)S(1)}, u32[]{:S(2)}, u32[]{:S(2)}) collective-permute-start(bf16[8,48,48]{2,1,0:T(8,128)(2,1)S(1)} %slice.19), channel_id=1, source_target_pairs={{0,17},{1,18},{2,19},{3,20},{4,21},{5,22},{6,23},{7,24},{8,25},{9,... | collective-permute-start | bytes 110600 | tf_op jit(solution)/shard_map/ppermute | solution.py:522
  104.5 17.0 %collective-permute-done.2 = bf16[8,48,48]{2,1,0:T(8,128)(2,1)S(1)} collective-permute-done((bf16[8,48,48]{2,1,0:T(8,128)(2,1)S(1)}, bf16[8,48,48]{2,1,0:T(8,128)(2,1)S(1)}, u32[]{:S(2)}, u32[]{:S(2)}) %collective-permute-start.2) | collective-permute-done | bytes 36896 | tf_op jit(solution)/shard_map/ppermute | solution.py:522
  121.5 0.0 collective-permute-done.1
  121.5 1.2 collective-permute-done
  122.7 3.3 %fusion.22 = f32[8,256,256]{2,1,0:T(8,128)} fusion(f32[8,304,384]{2,1,0:T(8,128)} %get-tuple-element.6, bf16[8,48,48]{2,1,0:T(8,128)(2,1)S(1)} %collective-permute-done.2, bf16[8,48,256]{2,1,0:T(8,128)(2,1)S(1)} %collective-permute-done.1, bf16[8,256,48]{2,1,0:T(8,128)(2,1)S(1)} %collective-permute-done), kind=kLoop, calls=%fused_computation.18 | loop fusion | flops 4194304 | bytes 4624384 | tf_op jit(solution)/shard_map/max | solution.py:592
  (2 shorter events, 0.0 us)
Async XLA Ops:
  0.0 69.4 %copy-start.1 = (bf16[8,256,384,1]{2,1,3,0:T(8,128)(2,1)S(1)}, bf16[8,256,384,1]{2,1,3,0:T(8,128)(2,1)}, u32[]{:S(2)}) copy-start(bf16[8,256,384,1]{2,1,3,0:T(8,128)(2,1)} %constant.33) | copy-start | bytes 4718596
  69.5 18.0 %copy-start = (bf16[8,256,384,1]{2,1,0,3:T(8,128)(2,1)S(1)}, bf16[8,256,384,1]{2,1,0,3:T(8,128)(2,1)}, u32[]{:S(2)}) copy-start(bf16[8,256,384,1]{2,1,0,3:T(8,128)(2,1)} %constant.36) | copy-start | bytes 4718596
  99.4 22.1 %collective-permute-start.1 = (bf16[8,48,256]{2,1,0:T(8,128)(2,1)S(1)}, bf16[8,48,256]{2,1,0:T(8,128)(2,1)S(1)}, u32[]{:S(2)}, u32[]{:S(2)}) collective-permute-start(bf16[8,48,256]{2,1,0:T(8,128)(2,1)S(1)} %slice.18), channel_id=1, source_target_pairs={{0,16},{16,32},{32,48},{48,64},{64,80},{80,96},{96,112},{112,0},{1... | collective-permute-start | bytes 589832 | tf_op jit(solution)/shard_map/ppermute | solution.py:522
  102.2 20.5 %collective-permute-start = (bf16[8,256,48]{2,1,0:T(8,128)(2,1)S(1)}, bf16[8,256,48]{2,1,0:T(8,128)(2,1)S(1)}, u32[]{:S(2)}, u32[]{:S(2)}) collective-permute-start(bf16[8,256,48]{2,1,0:T(8,128)(2,1)S(1)} %slice.17), channel_id=1, source_target_pairs={{0,1},{1,2},{2,3},{3,4},{4,5},{5,6},{6,7},{7,8},{8,9},{9,10},{10,1... | collective-permute-start | bytes 589832 | tf_op jit(solution)/shard_map/ppermute | solution.py:522
  102.5 19.0 %collective-permute-start.2 = (bf16[8,48,48]{2,1,0:T(8,128)(2,1)S(1)}, bf16[8,48,48]{2,1,0:T(8,128)(2,1)S(1)}, u32[]{:S(2)}, u32[]{:S(2)}) collective-permute-start(bf16[8,48,48]{2,1,0:T(8,128)(2,1)S(1)} %slice.19), channel_id=1, source_target_pairs={{0,17},{1,18},{2,19},{3,20},{4,21},{5,22},{6,23},{7,24},{8,25},{9,... | collective-permute-start | bytes 110600 | tf_op jit(solution)/shard_map/ppermute | solution.py:522

commit v8 on v7

--- a/solution.py
+++ b/solution.py
@@ -7,7 +7,6 @@
 import numpy as np
 from jax import lax
 from jax.experimental import pallas as pl
-from jax.experimental.layout import Layout, with_layout_constraint
 from jax.experimental.pallas import tpu as pltpu
 from jax.sharding import PartitionSpec as P
 
@@ -151,17 +150,36 @@
     return {name: rounded(table) for name, table in out.items()}
 
 
-NEAR = ((1, 0), (0, 1), (3, 0), (0, 3), (1, 1), (3, 3), (1, 3), (3, 1))
-FAR = ((2, 0), (0, 2), (2, 1), (2, 3), (1, 2), (3, 2), (2, 2))
-THROUGH = (
-    ((1, 0), (3, 0)),
-    ((0, 1), (0, 3)),
-    ((1, 1), (3, 1)),
-    ((1, 3), (3, 3)),
-    ((1, 1), (1, 3)),
-    ((3, 1), (3, 3)),
-    ((1, 1), (3, 3)),
+PLACES = (
+    (2, 2),
+    (2, 1),
+    (1, 2),
+    (2, 3),
+    (3, 2),
+    (1, 1),
+    (3, 3),
+    (1, 3),
+    (3, 1),
+    (2, 0),
+    (0, 2),
+    (1, 0),
+    (0, 1),
+    (3, 0),
+    (0, 3),
 )
+
+
+def path(place, r):
+    ups = {0: (), 1: (1,), 2: (1, 1) if r == 0 else (3, 3), 3: (3,)}
+    along_x = [(d, 0) for d in ups[place[0]]]
+    along_z = [(0, d) for d in ups[place[1]]]
+    return along_x + along_z if r == 0 else along_z + along_x
+
+
+PATHS = [[path(place, r) for place in PLACES] for r in range(2)]
+HOPS = [sum(len(p) > h for p in PATHS[0]) for h in range(5)]
+BASE = [0] + [2 * sum(HOPS[1:h]) for h in range(1, 5)]
+LAG = 3
 
 
 def choose(j, values):
@@ -254,55 +272,50 @@
             device_id_type=pl.DeviceIdType.MESH,
         )
 
-    def near(j):
-        return choose(j, [o[0] for o in NEAR]), choose(j, [o[1] for o in NEAR])
-
-    def far(j):
-        return choose(j, [o[0] for o in FAR]), choose(j, [o[1] for o in FAR])
-
-    def through(j, r):
-        return (
-            choose(j, [o[r][0] for o in THROUGH]),
-            choose(j, [o[r][1] for o in THROUGH]),
-        )
-
-    def near_copy(j, r):
+    def hop_copy(h, i, r, last):
+        paths = PATHS[r][: HOPS[h]]
+        so_far = [[sum(step[a] for step in p[:h]) % 4 for p in paths] for a in range(2)]
+        source = at(4 - choose(i, so_far[0]), 4 - choose(i, so_far[1]))
+        to = at(choose(i, [p[h][0] for p in paths]), choose(i, [p[h][1] for p in paths]))
+        own = i * 2 + r
         return pltpu.make_async_remote_copy(
-            src_ref=sending.at[len(FAR) + j, r],
-            dst_ref=arrived.at[fx, r],
-            send_sem=tile_send.at[len(FAR) + j, r],
-            recv_sem=tile_recv.at[fx, r],
-            device_id={"fx": at(*near(j))},
+            src_ref=sending.at[i, r] if h == 0 else relay.at[BASE[h] + own],
+            dst_ref=arrived.at[source, r] if last else relay.at[BASE[h + 1] + own],
+            send_sem=tile_send.at[own] if h == 0 else relay_send.at[BASE[h] + own],
+            recv_sem=tile_recv.at[source, r] if last else relay_recv.at[BASE[h + 1] + own],
+            device_id={"fx": to},
             device_id_type=pl.DeviceIdType.MESH,
         )
 
-    def far_copy(j, r):
-        return pltpu.make_async_remote_copy(
-            src_ref=sending.at[j, r],
-            dst_ref=relay.at[j, r],
-            send_sem=tile_send.at[j, r],
-            recv_sem=relay_recv.at[j, r],
-            device_id={"fx": at(*through(j, r))},
-            device_id_type=pl.DeviceIdType.MESH,
-        )
-
-    def relay_copy(j, r):
-        end, mid = far(j), through(j, r)
-        source = at(4 - mid[0], 4 - mid[1])
-        return pltpu.make_async_remote_copy(
-            src_ref=relay.at[j, r],
-            dst_ref=arrived.at[source, r],
-            send_sem=relay_send.at[j, r],
-            recv_sem=tile_recv.at[source, r],
-            device_id={"fx": at(end[0] + 4 - mid[0], end[1] + 4 - mid[1])},
-            device_id_type=pl.DeviceIdType.MESH,
-        )
+    def hop_start(h, i):
+        for r in range(2):
+            if h > 0:
+                slot = BASE[h] + i * 2 + r
+                pltpu.make_async_remote_copy(
+                    src_ref=relay.at[slot],
+                    dst_ref=relay.at[slot],
+                    send_sem=relay_send.at[slot],
+                    recv_sem=relay_recv.at[slot],
+                    device_id={"fx": at(1, 0)},
+                    device_id_type=pl.DeviceIdType.MESH,
+                ).wait_recv()
+            if HOPS[h + 1] == 0:
+                hop_copy(h, i, r, True).start()
+            else:
+
+                @pl.when(i >= HOPS[h + 1])
+                def _():
+                    hop_copy(h, i, r, True).start()
+
+                @pl.when(i < HOPS[h + 1])
+                def _():
+                    hop_copy(h, i, r, False).start()
 
     def arrival(source, r):
         return pltpu.make_async_remote_copy(
             src_ref=arrived.at[source, r],
             dst_ref=arrived.at[source, r],
-            send_sem=tile_send.at[0, 0],
+            send_sem=tile_send.at[0],
             recv_sem=tile_recv.at[source, r],
             device_id={"fx": source},
             device_id_type=pl.DeviceIdType.MESH,
@@ -347,28 +360,20 @@
         share_copy(to, fx).start()
         sending[place, 0], sending[place, 1] = planes(slots)
 
-    def send_far(j, carry):
-        prepare(at(*far(j)), j)
-        far_copy(j, 0).start()
-        far_copy(j, 1).start()
-        return carry
-
-    lax.fori_loop(0, len(FAR), send_far, 0)
-
-    def send_near(j, carry):
-        prepare(at(*near(j)), len(FAR) + j)
-        near_copy(j, 0).start()
-        near_copy(j, 1).start()
-
-        @pl.when(j >= 1)
-        def _():
-            for r in range(2):
-                far_copy(j - 1, r).wait_recv()
-                relay_copy(j - 1, r).start()
-
-        return carry
-
-    lax.fori_loop(0, len(NEAR), send_near, 0)
+    def send_tiles(i, carry):
+        prepare(at(choose(i, [p[0] for p in PLACES]), choose(i, [p[1] for p in PLACES])), i)
+        hop_start(0, i)
+        for h in range(1, 4):
+            before = i - h * LAG
+
+            @pl.when((before >= 0) & (before < HOPS[h]))
+            def _():
+                hop_start(h, before)
+
+        return carry
+
+    assert all(HOPS[h] + h * LAG <= len(PLACES) for h in range(4))
+    lax.fori_loop(0, len(PLACES), send_tiles, 0)
     own = slots_for(fx)
     shares[fx] = share_rows(own)
     arrived[fx, 0], arrived[fx, 1] = planes(own)
@@ -493,20 +498,14 @@
         share_copy(peer(k), fx).wait_send()
         return carry
 
-    def finish_near(j, carry):
+    def finish_hops(h, i, carry):
         for r in range(2):
-            near_copy(j, r).wait_send()
-        return carry
-
-    def finish_far(j, carry):
-        for r in range(2):
-            far_copy(j, r).wait_send()
-            relay_copy(j, r).wait_send()
+            hop_copy(h, i, r, True).wait_send()
         return carry
 
     lax.fori_loop(1, n_fx, finish_shares, 0)
-    lax.fori_loop(0, len(NEAR), finish_near, 0)
-    lax.fori_loop(0, len(FAR), finish_far, 0)
+    for h in range(4):
+        lax.fori_loop(0, HOPS[h], functools.partial(finish_hops, h), 0)
     for i in range(2):
         halo_copy(i).wait_send()
     for q in range(chunks):
@@ -540,7 +539,7 @@
             pltpu.VMEM((CH, SIDE, SIDE), F32),
             pltpu.VMEM((n_fx, 2, SIDE, SIDE), BF),
             pltpu.VMEM((n_fx, 2, SIDE, SIDE), BF),
-            pltpu.VMEM((len(FAR), 2, SIDE, SIDE), BF),
+            pltpu.VMEM((BASE[4], SIDE, SIDE), BF),
             pltpu.VMEM((2, 2 * SIDE, SIDE), BF),
             pltpu.VMEM((n_fx, 8, 128), F32),
             pltpu.VMEM((n_fx, 8, 128), F32),
@@ -549,10 +548,10 @@
             pltpu.VMEM((CH // 2, SIDE, 128), BF),
             pltpu.VMEM((CH // 2, HALO, 128), BF),
             dma((2,)),
+            dma((2 * len(PLACES),)),
             dma((n_fx, 2)),
-            dma((n_fx, 2)),
-            dma((len(FAR), 2)),
-            dma((len(FAR), 2)),
+            dma((BASE[4],)),
+            dma((BASE[4],)),
             dma((n_fx,)),
             dma((n_fx,)),
             dma((2,)),
@@ -574,9 +573,8 @@
         vis_tiles,
     )
     rows, columns = made["rows"], made["columns"]
-    col_sec = jnp.einsum("cyx,bkx->bcyk", extended, columns, preferred_element_type=F32).astype(BF)
-    coefficient = jnp.einsum("bjy,bcyk->bcjk", rows, col_sec, preferred_element_type=F32)
-    coefficient = with_layout_constraint(coefficient, Layout(major_to_minor=(0, 1, 2, 3)))
+    row_sec = jnp.einsum("bkn,cnx->bckx", rows, extended, preferred_element_type=F32).astype(BF)
+    coefficient = jnp.einsum("bcyx,bkx->bcyk", row_sec, columns, preferred_element_type=F32)
     limits = thresholds.astype(F32)
     shrunk = (coefficient - jnp.clip(coefficient, -limits, limits)).astype(BF)
     row_sec = jnp.einsum("bjy,bcjk->bcyk", rows, shrunk, preferred_element_type=F32).astype(BF)

time: 128 us -> 127 us (level); the launches traced: 126 us -> 127 us
  Pallas kernels: 69.4 us -> 74.1 us
  waiting for transfers between devices: 18.2 us -> 14.9 us
    pallas_call x1, Pallas kernels: 69.4 us -> 74.1 us  [per_device(): pl.pallas_call(functools.partial(exchange_kernel, n_fy, n_fx), out_shape=...]
    ppermute x3, waiting for transfers between devices: 18.2 us -> 14.9 us  [passed(): return lax.ppermute(value, axes if len(axes) > 1 else axes[0], pairs)]
where the time goes in v8:
time: 127 us
  Pallas kernels  74.1 us (58%)
  matrix products  28.9 us (23%)
  waiting for transfers between devices  14.9 us (12%)
  starting transfers between devices  5.2 us (4%)
  other arithmetic  3.28 us (3%)
    pallas_call x1, Pallas kernels, per_device(): pl.pallas_call(functools.partial(exchange_kernel, n_fy, n_fx), out_shape=...  74.1 us
    dot_general x1, matrix products, per_device(): jnp.einsum('bcyx,bkx->bcyk', row_sec, columns, preferred_element_type=F32)  16.8 us
    ppermute x3, waiting for transfers between devices, passed(): return lax.ppermute(value, axes if len(axes) > 1 else axes[0], pairs)  14.9 us
    dot_general x1, matrix products, per_device(): jnp.einsum('bcyk,bkx->cyx', row_sec, columns, preferred_element_type=F32)  12.1 us
    ppermute x3, starting transfers between devices, passed(): return lax.ppermute(value, axes if len(axes) > 1 else axes[0], pairs)  5.2 us
    max x1, other arithmetic, per_device(): return jnp.maximum(summed * (1.0 / BASES), 0.0)  3.28 us
  transfers between devices with their start and end apart: 3, of which 2 were waited for; matrix products, arithmetic and copies ran while one was open for 0% of the time, Pallas kernels for 0%

profile of v8, /device:TPU:1, one launch (start us, length us, event | category | flops | bytes accessed | tf_op | source)
XLA Modules:
  0.0 126.6 jit_solution(16203216404807385660)
XLA Ops:
  0.0 0.0 copy-start.1
  0.0 74.1 %shard_map.109 = bf16[8,304,384]{2,1,0:T(8,128)(2,1)} custom-call(s32[16]{0:T(128)} %bitcast.30, s32[16]{0:T(128)} %chan_ref.1, s32[16]{0:T(128)} %count_ref.1, bf16[512,512]{1,0:T(8,128)(2,1)} %constant.20.clone.fourier, bf16[256,512]{1,0:T(8,128)(2,1)} %constant.21.clone.back, bf16[256,256]{1,0:T(8,128)(2,1)} %constant.22.clone.excess, ...), custom_call_target="tpu_custom_call" | custom-call | tf_op jit(solution)/shard_map/pallas_call | solution.py:531
  74.2 0.0 copy-done.1
  74.2 0.0 copy-start
  74.2 16.8 %fusion.2 = bf16[8,8,256,256]{3,2,1,0:T(8,128)(2,1)} fusion(bf16[8,8,256,256]{3,2,1,0:T(8,128)(2,1)} %param.16, bf16[8,256,384,1]{2,1,3,0:T(8,128)(2,1)S(1)} %copy-done.1, bf16[8,256,304,1]{2,1,3,0:T(8,128)(2,1)} %constant.33, bf16[8,304,384]{2,1,0:T(8,128)(2,1)} %shard_map.109), kind=kOutput, calls=%fused_computation.4 | convolution fusion | flops 7077888000 | bytes 21463040 | tf_op jit(solution)/shard_map/bcyx,bkx->bcyk/dot_general | solution.py:577
  90.9 0.0 copy-done
  90.9 12.1 %fusion.30 = (bf16[8,304,384]{2,1,0:T(8,128)(2,1)S(1)}, f32[8,304,384]{2,1,0:T(8,128)}) fusion(bf16[8,256,384,1]{2,1,0,3:T(8,128)(2,1)S(1)} %copy-done, bf16[8,256,304,1]{2,1,0,3:T(8,128)(2,1)} %constant.35, bf16[8,8,256,256]{3,2,1,0:T(8,128)(2,1)} %fusion.2), kind=kOutput, calls=%fused_computation.21 | convolution fusion | flops 6381256704 | bytes 16809984 | tf_op jit(solution)/shard_map/bcyk,bkx->cyx/dot_general | solution.py:581
  103.1 1.0 collective-permute-start.1
  104.1 0.1 slice.17
  104.2 0.1 collective-permute-start
  104.3 4.1 %collective-permute-start.2 = (bf16[8,48,48]{2,1,0:T(8,128)(2,1)S(1)}, bf16[8,48,48]{2,1,0:T(8,128)(2,1)S(1)}, u32[]{:S(2)}, u32[]{:S(2)}) collective-permute-start(bf16[8,48,48]{2,1,0:T(8,128)(2,1)S(1)} %slice.19), channel_id=1, source_target_pairs={{0,17},{1,18},{2,19},{3,20},{4,21},{5,22},{6,23},{7,24},{8,25},{9,... | collective-permute-start | bytes 110600 | tf_op jit(solution)/shard_map/ppermute | solution.py:521
  108.4 14.6 %collective-permute-done.2 = bf16[8,48,48]{2,1,0:T(8,128)(2,1)S(1)} collective-permute-done((bf16[8,48,48]{2,1,0:T(8,128)(2,1)S(1)}, bf16[8,48,48]{2,1,0:T(8,128)(2,1)S(1)}, u32[]{:S(2)}, u32[]{:S(2)}) %collective-permute-start.2) | collective-permute-done | bytes 36896 | tf_op jit(solution)/shard_map/ppermute | solution.py:521
  123.0 0.0 collective-permute-done.1
  123.0 0.3 collective-permute-done
  123.3 3.3 %fusion.22 = f32[8,256,256]{2,1,0:T(8,128)} fusion(f32[8,304,384]{2,1,0:T(8,128)} %get-tuple-element.6, bf16[8,48,48]{2,1,0:T(8,128)(2,1)S(1)} %collective-permute-done.2, bf16[8,48,256]{2,1,0:T(8,128)(2,1)S(1)} %collective-permute-done.1, bf16[8,256,48]{2,1,0:T(8,128)(2,1)S(1)} %collective-permute-done), kind=kLoop, calls=%fused_computation.18 | loop fusion | flops 4194304 | bytes 4624384 | tf_op jit(solution)/shard_map/max | solution.py:590
  (2 shorter events, 0.0 us)
Async XLA Ops:
  0.0 74.2 %copy-start.1 = (bf16[8,256,384,1]{2,1,3,0:T(8,128)(2,1)S(1)}, bf16[8,256,384,1]{2,1,3,0:T(8,128)(2,1)}, u32[]{:S(2)}) copy-start(bf16[8,256,384,1]{2,1,3,0:T(8,128)(2,1)} %constant.34) | copy-start | bytes 4718596
  74.2 16.8 %copy-start = (bf16[8,256,384,1]{2,1,0,3:T(8,128)(2,1)S(1)}, bf16[8,256,384,1]{2,1,0,3:T(8,128)(2,1)}, u32[]{:S(2)}) copy-start(bf16[8,256,384,1]{2,1,0,3:T(8,128)(2,1)} %constant.36) | copy-start | bytes 4718596
  103.1 20.0 %collective-permute-start.1 = (bf16[8,48,256]{2,1,0:T(8,128)(2,1)S(1)}, bf16[8,48,256]{2,1,0:T(8,128)(2,1)S(1)}, u32[]{:S(2)}, u32[]{:S(2)}) collective-permute-start(bf16[8,48,256]{2,1,0:T(8,128)(2,1)S(1)} %slice.18), channel_id=1, source_target_pairs={{0,16},{16,32},{32,48},{48,64},{64,80},{80,96},{96,112},{112,0},{1... | collective-permute-start | bytes 589832 | tf_op jit(solution)/shard_map/ppermute | solution.py:521
  104.2 19.1 %collective-permute-start = (bf16[8,256,48]{2,1,0:T(8,128)(2,1)S(1)}, bf16[8,256,48]{2,1,0:T(8,128)(2,1)S(1)}, u32[]{:S(2)}, u32[]{:S(2)}) collective-permute-start(bf16[8,256,48]{2,1,0:T(8,128)(2,1)S(1)} %slice.17), channel_id=1, source_target_pairs={{0,1},{1,2},{2,3},{3,4},{4,5},{5,6},{6,7},{7,8},{8,9},{9,10},{10,1... | collective-permute-start | bytes 589832 | tf_op jit(solution)/shard_map/ppermute | solution.py:521
  104.3 18.7 %collective-permute-start.2 = (bf16[8,48,48]{2,1,0:T(8,128)(2,1)S(1)}, bf16[8,48,48]{2,1,0:T(8,128)(2,1)S(1)}, u32[]{:S(2)}, u32[]{:S(2)}) collective-permute-start(bf16[8,48,48]{2,1,0:T(8,128)(2,1)S(1)} %slice.19), channel_id=1, source_target_pairs={{0,17},{1,18},{2,19},{3,20},{4,21},{5,22},{6,23},{7,24},{8,25},{9,... | collective-permute-start | bytes 110600 | tf_op jit(solution)/shard_map/ppermute | solution.py:521

commit v9 on v8

--- a/solution.py
+++ b/solution.py
@@ -139,7 +139,9 @@
 def tables():
     full = composite_tables()
     wide = np.concatenate([full, np.zeros((BASES, SIDE, 128 - HALO), np.float32)], axis=2)
-    out = {"rows": full, "columns": wide}
+    spread = wide.copy()
+    spread[:, :, TALL + 16 : TALL + 16 + HALO] = full[:, :, SIDE:]
+    out = {"rows": full, "columns": wide, "spread": spread}
     grid = np.arange(SIDE)[:, None] * np.arange(SIDE)[None, :] % SIDE
     angle = grid * (2.0 * math.pi / SIDE)
     cosine = rounded(np.cos(angle) / math.sqrt(SIDE)).astype(np.float64)
@@ -208,6 +210,7 @@
     vis,
     sky,
     model,
+    partial,
     sending,
     arrived,
     relay,
@@ -260,29 +263,29 @@
     prev, nxt = (fx + n_fx - 1) % n_fx, (fx + 1) % n_fx
     for where in ({"fy": up}, {"fy": down}, {"fy": up, "fx": prev}, {"fy": down, "fx": nxt}):
         pl.semaphore_signal(barrier, inc=1, device_id=where, device_id_type=pl.DeviceIdType.MESH)
-    pl.semaphore_wait(barrier, n_fx - 1 + 4)
-
-    def share_copy(to, source):
+
+    def place_of(i):
+        return at(choose(i, [p[0] for p in PLACES]), choose(i, [p[1] for p in PLACES]))
+
+    def share_copy(i):
         return pltpu.make_async_remote_copy(
-            src_ref=share_ref.at[to],
-            dst_ref=shares.at[source],
-            send_sem=share_send.at[to],
-            recv_sem=share_recv.at[source],
-            device_id={"fx": to},
+            src_ref=share_ref.at[1 + i],
+            dst_ref=shares.at[1 + i],
+            send_sem=share_send.at[1 + i],
+            recv_sem=share_recv.at[1 + i],
+            device_id={"fx": place_of(i)},
             device_id_type=pl.DeviceIdType.MESH,
         )
 
     def hop_copy(h, i, r, last):
         paths = PATHS[r][: HOPS[h]]
-        so_far = [[sum(step[a] for step in p[:h]) % 4 for p in paths] for a in range(2)]
-        source = at(4 - choose(i, so_far[0]), 4 - choose(i, so_far[1]))
         to = at(choose(i, [p[h][0] for p in paths]), choose(i, [p[h][1] for p in paths]))
         own = i * 2 + r
         return pltpu.make_async_remote_copy(
             src_ref=sending.at[i, r] if h == 0 else relay.at[BASE[h] + own],
-            dst_ref=arrived.at[source, r] if last else relay.at[BASE[h + 1] + own],
+            dst_ref=arrived.at[1 + i, r] if last else relay.at[BASE[h + 1] + own],
             send_sem=tile_send.at[own] if h == 0 else relay_send.at[BASE[h] + own],
-            recv_sem=tile_recv.at[source, r] if last else relay_recv.at[BASE[h + 1] + own],
+            recv_sem=tile_recv.at[1 + i, r] if last else relay_recv.at[BASE[h + 1] + own],
             device_id={"fx": to},
             device_id_type=pl.DeviceIdType.MESH,
         )
@@ -311,13 +314,13 @@
                 def _():
                     hop_copy(h, i, r, False).start()
 
-    def arrival(source, r):
+    def arrival(i, r):
         return pltpu.make_async_remote_copy(
-            src_ref=arrived.at[source, r],
-            dst_ref=arrived.at[source, r],
+            src_ref=arrived.at[1 + i, r],
+            dst_ref=arrived.at[1 + i, r],
             send_sem=tile_send.at[0],
-            recv_sem=tile_recv.at[source, r],
-            device_id={"fx": source},
+            recv_sem=tile_recv.at[1 + i, r],
+            device_id={"fx": at(1, 0)},
             device_id_type=pl.DeviceIdType.MESH,
         )
 
@@ -354,14 +357,16 @@
                 ).astype(BF)
         return [(dot(back[...], half[i]) * slots[i][1]).astype(BF) for i in range(2)]
 
-    def prepare(to, place):
-        slots = slots_for(to)
-        share_ref[to] = share_rows(slots)
-        share_copy(to, fx).start()
-        sending[place, 0], sending[place, 1] = planes(slots)
+    def prepare(i):
+        slots = slots_for(place_of(i))
+        share_ref[1 + i] = share_rows(slots)
+        sending[i, 0], sending[i, 1] = planes(slots)
+
+    prepare(jnp.int32(0))
+    pl.semaphore_wait(barrier, n_fx - 1 + 4)
 
     def send_tiles(i, carry):
-        prepare(at(choose(i, [p[0] for p in PLACES]), choose(i, [p[1] for p in PLACES])), i)
+        share_copy(i).start()
         hop_start(0, i)
         for h in range(1, 4):
             before = i - h * LAG
@@ -370,13 +375,17 @@
             def _():
                 hop_start(h, before)
 
+        @pl.when(i < len(PLACES) - 1)
+        def _():
+            prepare(i + 1)
+
         return carry
 
     assert all(HOPS[h] + h * LAG <= len(PLACES) for h in range(4))
     lax.fori_loop(0, len(PLACES), send_tiles, 0)
     own = slots_for(fx)
-    shares[fx] = share_rows(own)
-    arrived[fx, 0], arrived[fx, 1] = planes(own)
+    shares[0] = share_rows(own)
+    arrived[0, 0], arrived[0, 1] = planes(own)
 
     load_sky.wait()
 
@@ -388,11 +397,11 @@
 
     lax.fori_loop(0, CH, there_and_back, 0)
 
-    def wait_share(k, carry):
-        share_copy(peer(k), peer(k)).wait_recv()
-        return carry
-
-    lax.fori_loop(1, n_fx, wait_share, 0)
+    def wait_share(i, carry):
+        share_copy(i).wait_recv()
+        return carry
+
+    lax.fori_loop(0, len(PLACES), wait_share, 0)
     slots = n_fx * 2
     wide = slots * 16
     all_shares = shares[...].reshape(n_fx * 8, 128)
@@ -420,20 +429,40 @@
     kron[...] = jnp.where(diagonal, widened, 0.0).astype(BF)
     scale = 1.0 / (1.0 + totals)
 
-    def wait_tiles(k, carry):
+    def group_rows(g):
+        return pl.ds(pl.multiple_of(g * 16, 16), 16)
+
+    def begin(g, carry):
+        pixels = sky[:, group_rows(g), :].reshape(CH * 16, SIDE)
+        there = model[:, group_rows(g), :].reshape(CH * 16, SIDE)
+        partial[g] = pixels - (totals * scale) * there
+        return carry
+
+    lax.fori_loop(0, SIDE // 16, begin, 0)
+
+    def wait_tiles(i, carry):
         for r in range(2):
-            arrival(peer(k), r).wait_recv()
-        return carry
-
-    lax.fori_loop(1, n_fx, wait_tiles, 0)
+            arrival(i, r).wait_recv()
+        return carry
+
+    def with_sources(g, first, last):
+        held = arrived[first:last, :, group_rows(g), :].reshape((last - first) * 32, SIDE)
+        return partial[g] + scale * dot(kron[:, first * 32 : last * 32], held)
+
+    for first, last in ((0, 8), (8, 12)):
+        lax.fori_loop(max(first - 1, 0), last - 1, wait_tiles, 0)
+
+        def add_sources(q, carry):
+            for i in range(4):
+                partial[q * 4 + i] = with_sources(q * 4 + i, first, last)
+            return carry
+
+        lax.fori_loop(0, SIDE // 64, add_sources, 0)
+    lax.fori_loop(11, len(PLACES), wait_tiles, 0)
 
     def combine(g):
-        rows = pl.ds(pl.multiple_of(g * 16, 16), 16)
-        gathered = dot(kron[...], arrived[:, :, rows, :].reshape(wide, SIDE))
-        pixels = sky[:, rows, :].reshape(CH * 16, SIDE)
-        there = model[:, rows, :].reshape(CH * 16, SIDE)
-        new = pixels - (totals * there - gathered) * scale
-        new = new.reshape(CH // 2, 2, 16, SIDE)
+        rows = group_rows(g)
+        new = with_sources(g, 12, 16).reshape(CH // 2, 2, 16, SIDE)
         extended[:, rows, :SIDE] = new.reshape(CH, 16, SIDE).astype(BF)
         low = lax.broadcasted_iota(jnp.int32, (CH // 2, 16, 128), 2) < 64
         second = pltpu.roll(new[:, 1, :, :128].reshape(CH // 2 * 16, 128), 64, 1)
@@ -494,8 +523,8 @@
         place(beside.at[:, q * deep : (q + 1) * deep, :], q * deep, (q + 1) * deep)
     halo_copy(0).wait_recv()
 
-    def finish_shares(k, carry):
-        share_copy(peer(k), fx).wait_send()
+    def finish_shares(i, carry):
+        share_copy(i).wait_send()
         return carry
 
     def finish_hops(h, i, carry):
@@ -503,7 +532,7 @@
             hop_copy(h, i, r, True).wait_send()
         return carry
 
-    lax.fori_loop(1, n_fx, finish_shares, 0)
+    lax.fori_loop(0, len(PLACES), finish_shares, 0)
     for h in range(4):
         lax.fori_loop(0, HOPS[h], functools.partial(finish_hops, h), 0)
     for i in range(2):
@@ -519,6 +548,45 @@
         j = [(a + b) % n for a, b, n in zip(i, to, sizes)]
         pairs.append((int(np.ravel_multi_index(i, sizes)), int(np.ravel_multi_index(j, sizes))))
     return lax.ppermute(value, axes if len(axes) > 1 else axes[0], pairs)
+
+
+def first_half(shape):
+    return lax.broadcasted_iota(jnp.int32, shape, len(shape) - 1) < 64
+
+
+def pack_kernel(cells, right, corner, below, side, bottom, sem):
+    load_side = pltpu.make_async_copy(cells.at[:, :, SIDE:], side, sem.at[0])
+    load_bottom = pltpu.make_async_copy(cells.at[:, SIDE:, :SIDE], bottom, sem.at[1])
+    load_side.start()
+    load_bottom.start()
+    load_side.wait()
+    for p in range(CH // 2):
+        both = jnp.where(first_half((TALL, 128)), side[2 * p], side[2 * p + 1]).astype(BF)
+        right[p] = both[:SIDE]
+        corner[p] = both[SIDE:]
+    load_bottom.wait()
+    below[...] = bottom[...].astype(BF)
+
+
+def add_kernel(cells, left, above, corner, out):
+    for h in range(2):
+
+        def columns(pairs):
+            pairs = pairs.astype(F32)
+            if h == 1:
+                pairs = pltpu.roll(pairs, 64, 1)
+            return jnp.where(first_half(pairs.shape), pairs, 0.0)
+
+        def finished(total):
+            return jnp.maximum(total * (1.0 / BASES), 0.0)
+
+        from_left = columns(left[0])
+        from_above = above[h].astype(F32)
+        first = from_left[:HALO] + from_above[:, :128] + columns(corner[0])
+        out[h, :HALO, :128] = finished(cells[h, :HALO, :128] + first)
+        out[h, :HALO, 128:] = finished(cells[h, :HALO, 128:] + from_above[:, 128:])
+        out[h, HALO:, :128] = finished(cells[h, HALO:, :128] + from_left[HALO:])
+        out[h, HALO:, 128:] = finished(cells[h, HALO:, 128:])
 
 
 def per_device(n_fy, n_fx, sky_image, vis_tiles, tile_dest, tile_chan, tile_count, thresholds):
@@ -530,13 +598,13 @@
     tiles = vis_tiles.shape[0]
     extended = pl.pallas_call(
         functools.partial(exchange_kernel, n_fy, n_fx),
-        out_shape=jax.ShapeDtypeStruct((CH, TALL, WIDE), BF),
+        out_shape=pltpu.VMEM((CH, TALL, WIDE), BF),
         in_specs=[smem] * 3 + [vmem] * 3 + [anywhere] * 2,
-        out_specs=vmem,
         scratch_shapes=[
             pltpu.VMEM((tiles, 2, SIDE, SIDE), BF),
             pltpu.VMEM((CH, SIDE, SIDE), F32),
             pltpu.VMEM((CH, SIDE, SIDE), F32),
+            pltpu.VMEM((SIDE // 16, CH * 16, SIDE), F32),
             pltpu.VMEM((n_fx, 2, SIDE, SIDE), BF),
             pltpu.VMEM((n_fx, 2, SIDE, SIDE), BF),
             pltpu.VMEM((BASE[4], SIDE, SIDE), BF),
@@ -578,16 +646,39 @@
     limits = thresholds.astype(F32)
     shrunk = (coefficient - jnp.clip(coefficient, -limits, limits)).astype(BF)
     row_sec = jnp.einsum("bjy,bcjk->bcyk", rows, shrunk, preferred_element_type=F32).astype(BF)
-    cells = jnp.einsum("bcyk,bkx->cyx", row_sec, columns, preferred_element_type=F32)
-    spill = cells.astype(BF)
-    from_left = passed(spill[:, :SIDE, SIDE:TALL], ("fx",), (1,)).astype(F32)
-    from_above = passed(spill[:, SIDE:, :SIDE], ("fy",), (1,)).astype(F32)
-    from_corner = passed(spill[:, SIDE:, SIDE:TALL], ("fy", "fx"), (1, 1)).astype(F32)
-    left = jnp.pad(from_left, ((0, 0), (0, 0), (0, SIDE - HALO)))
-    above = jnp.pad(from_above, ((0, 0), (0, SIDE - HALO), (0, 0)))
-    corner = jnp.pad(from_corner, ((0, 0), (0, SIDE - HALO), (0, SIDE - HALO)))
-    summed = cells[:, :SIDE, :SIDE] + left + above + corner
-    return jnp.maximum(summed * (1.0 / BASES), 0.0)
+    cells = jnp.einsum("bcyk,bkx->cyx", row_sec, made["spread"], preferred_element_type=F32)
+    right, corner, below = pl.pallas_call(
+        pack_kernel,
+        out_shape=(
+            jax.ShapeDtypeStruct((CH // 2, SIDE, 128), BF),
+            jax.ShapeDtypeStruct((CH // 2, HALO, 128), BF),
+            jax.ShapeDtypeStruct((CH, HALO, SIDE), BF),
+        ),
+        in_specs=[anywhere],
+        out_specs=[vmem] * 3,
+        scratch_shapes=[
+            pltpu.VMEM((CH, TALL, 128), F32),
+            pltpu.VMEM((CH, HALO, SIDE), F32),
+            dma((2,)),
+        ],
+        compiler_params=pltpu.CompilerParams(vmem_limit_bytes=16 * 1024 * 1024),
+    )(cells)
+    left = passed(right, ("fx",), (1,))
+    above = passed(below, ("fy",), (1,))
+    corner = passed(corner, ("fy", "fx"), (1, 1))
+    return pl.pallas_call(
+        add_kernel,
+        out_shape=jax.ShapeDtypeStruct((CH, SIDE, SIDE), F32),
+        grid=(CH // 2,),
+        in_specs=[
+            pl.BlockSpec((2, SIDE, SIDE), lambda p: (p, 0, 0)),
+            pl.BlockSpec((1, SIDE, 128), lambda p: (p, 0, 0)),
+            pl.BlockSpec((2, HALO, SIDE), lambda p: (p, 0, 0)),
+            pl.BlockSpec((1, HALO, 128), lambda p: (p, 0, 0)),
+        ],
+        out_specs=pl.BlockSpec((2, SIDE, SIDE), lambda p: (p, 0, 0)),
+        compiler_params=pltpu.CompilerParams(vmem_limit_bytes=16 * 1024 * 1024),
+    )(cells, left, above, corner)
 
 
 def solution(mesh):

time: 127 us -> 119 us (0.937)
  waiting for transfers between devices: 14.9 us -> 7.8 us
  other arithmetic: 3.28 us -> 0 us
  local copies, waits for them, and re-layouts: 0.13 us -> 2.06 us
    ppermute x3, waiting for transfers between devices: 14.9 us -> 7.8 us  [passed(): return lax.ppermute(value, axes if len(axes) > 1 else axes[0], pairs)]
    max x1 -> x0, other arithmetic: 3.28 us -> none  [per_device(): return jnp.maximum(summed * (1.0 / BASES), 0.0)]
    pallas_call x0 -> x2, Pallas kernels: none -> 2.3 us  [the longest x1 2.1 us: per_device(): pl.pallas_call(add_kernel, out_shape=jax.ShapeDtypeStruct((CH, SIDE, SIDE...]
    unnamed x4, local copies, waits for them, and re-layouts: 0.01 us -> 2.06 us
    pallas_call x1, Pallas kernels: 74.1 us -> 72.5 us  [per_device(): pl.pallas_call(functools.partial(exchange_kernel, n_fy, n_fx), out_shape=...]
  transfers between devices with their start and end apart: 3 -> 3, of which waited for: 2 -> 1; matrix products, arithmetic and copies ran while one was open for 0% -> 0% of each run, Pallas kernels for 0% -> 0%
where the time goes in v9:
time: 119 us
  Pallas kernels  74.8 us (63%)
  matrix products  29 us (24%)
  waiting for transfers between devices  7.8 us (7%)
  starting transfers between devices  4.82 us (4%)
  local copies, waits for them, and re-layouts  2.06 us (2%)
    pallas_call x1, Pallas kernels, per_device(): pl.pallas_call(functools.partial(exchange_kernel, n_fy, n_fx), out_shape=...  72.5 us
    dot_general x1, matrix products, per_device(): jnp.einsum('bcyx,bkx->bcyk', row_sec, columns, preferred_element_type=F32)  16.9 us
    dot_general x1, matrix products, per_device(): jnp.einsum('bcyk,bkx->cyx', row_sec, made['spread'], preferred_element_ty...  12.1 us
    ppermute x3, waiting for transfers between devices, passed(): return lax.ppermute(value, axes if len(axes) > 1 else axes[0], pairs)  7.8 us
    ppermute x3, starting transfers between devices, passed(): return lax.ppermute(value, axes if len(axes) > 1 else axes[0], pairs)  4.82 us
  transfers between devices with their start and end apart: 3, of which 1 were waited for; matrix products, arithmetic and copies ran while one was open for 0% of the time, Pallas kernels for 0%

profile of v9, /device:TPU:1, one launch (start us, length us, event | category | flops | bytes accessed | tf_op | source)
XLA Modules:
  0.0 118.5 jit_solution(14770230867473611527)
XLA Ops:
  0.0 72.5 %shard_map.118 = bf16[8,304,384]{2,1,0:T(8,128)(2,1)S(1)} custom-call(s32[16]{0:T(128)} %bitcast.29, s32[16]{0:T(128)} %chan_ref.1, s32[16]{0:T(128)} %count_ref.1, bf16[512,512]{1,0:T(8,128)(2,1)} %constant.15.clone.fourier, bf16[256,512]{1,0:T(8,128)(2,1)} %constant.16.clone.back, bf16[256,256]{1,0:T(8,128)(2,1)} %constant.17.clone.excess, ...), custom_call_target="tpu_custom_call" | custom-call | tf_op jit(solution)/shard_map/pallas_call | solution.py:599
  72.5 0.0 copy-start.1
  72.5 16.9 %fusion.2 = bf16[8,8,256,256]{3,2,1,0:T(8,128)(2,1)} fusion(bf16[8,8,256,256]{3,2,1,0:T(8,128)(2,1)} %param.17, bf16[8,256,384,1]{2,1,3,0:T(8,128)(2,1)} %constant.23, bf16[8,256,304,1]{2,1,3,0:T(8,128)(2,1)} %constant.22, bf16[8,304,384]{2,1,0:T(8,128)(2,1)S(1)} %shard_map.118), kind=kOutput, calls=%fused_computation.4 | convolution fusion | flops 7077888000 | bytes 21463040 | tf_op jit(solution)/shard_map/bcyx,bkx->bcyk/dot_general | solution.py:645
  89.4 0.0 copy-done.1
  89.4 12.1 %fusion.19.cells = f32[8,304,384]{2,1,0:T(8,128)} fusion(bf16[8,256,384,1]{2,1,0,3:T(8,128)(2,1)S(1)} %copy-done.1, bf16[8,256,304,1]{2,1,0,3:T(8,128)(2,1)} %constant.24, bf16[8,8,256,256]{3,2,1,0:T(8,128)(2,1)} %fusion.2), kind=kOutput, calls=%fused_computation.14 | convolution fusion | flops 6380322816 | bytes 14942208 | tf_op jit(solution)/shard_map/bcyk,bkx->cyx/dot_general | solution.py:649
  101.5 0.0 copy-start
  101.5 2.1 %copy-done = f32[8,304,384]{2,1,0:T(8,128)S(1)} copy-done((f32[8,304,384]{2,1,0:T(8,128)S(1)}, f32[8,304,384]{2,1,0:T(8,128)}, u32[]{:S(2)}) %copy-start) | copy-done | bytes 3735576
  103.6 0.2 shard_map.119
  103.8 0.3 collective-permute-start
  104.1 1.0 collective-permute-start.1
  105.1 3.5 %collective-permute-start.2 = (bf16[4,48,128]{2,1,0:T(8,128)(2,1)S(1)}, bf16[4,48,128]{2,1,0:T(8,128)(2,1)S(1)}, u32[]{:S(2)}, u32[]{:S(2)}) collective-permute-start(bf16[4,48,128]{2,1,0:T(8,128)(2,1)S(1)} %get-tuple-element.10), channel_id=1, source_target_pairs={{0,17},{1,18},{2,19},{3,20},{4,21},{5,22},{6,23},{7,24},{8,25},{9,... | collective-permute-start | bytes 147464 | tf_op jit(solution)/shard_map/ppermute | solution.py:550
  108.6 7.8 %collective-permute-done.2.corner = bf16[4,48,128]{2,1,0:T(8,128)(2,1)S(1)} collective-permute-done((bf16[4,48,128]{2,1,0:T(8,128)(2,1)S(1)}, bf16[4,48,128]{2,1,0:T(8,128)(2,1)S(1)}, u32[]{:S(2)}, u32[]{:S(2)}) %collective-permute-start.2) | collective-permute-done | bytes 49184 | tf_op jit(solution)/shard_map/ppermute | solution.py:550
  116.4 0.0 collective-permute-done.1.above
  116.4 0.0 collective-permute-done.left
  116.4 2.1 %shard_map.120 = f32[8,256,256]{2,1,0:T(8,128)} custom-call(f32[8,304,384]{2,1,0:T(8,128)S(1)} %copy-done, bf16[4,256,128]{2,1,0:T(8,128)(2,1)S(1)} %collective-permute-done.left, bf16[8,48,256]{2,1,0:T(8,128)(2,1)S(1)} %collective-permute-done.1.above, bf16[4,48,128]{2,1,0:T(8,128)(2,1)S(1)} %collective-permute-done.2.corner), custom_call_target="tpu_custom_call" | custom-call | tf_op jit(solution)/shard_map/pallas_call | solution.py:669
Async XLA Ops:
  72.5 16.9 %copy-start.1 = (bf16[8,256,384,1]{2,1,0,3:T(8,128)(2,1)S(1)}, bf16[8,256,384,1]{2,1,0,3:T(8,128)(2,1)}, u32[]{:S(2)}) copy-start(bf16[8,256,384,1]{2,1,0,3:T(8,128)(2,1)} %constant.25) | copy-start | bytes 4718596
  101.5 2.1 %copy-start = (f32[8,304,384]{2,1,0:T(8,128)S(1)}, f32[8,304,384]{2,1,0:T(8,128)}, u32[]{:S(2)}) copy-start(f32[8,304,384]{2,1,0:T(8,128)} %fusion.19.cells) | copy-start | bytes 11206660
  103.8 12.6 %collective-permute-start = (bf16[4,256,128]{2,1,0:T(8,128)(2,1)S(1)}, bf16[4,256,128]{2,1,0:T(8,128)(2,1)S(1)}, u32[]{:S(2)}, u32[]{:S(2)}) collective-permute-start(bf16[4,256,128]{2,1,0:T(8,128)(2,1)S(1)} %get-tuple-element.8), channel_id=1, source_target_pairs={{0,1},{1,2},{2,3},{3,4},{4,5},{5,6},{6,7},{7,8},{8,9},{9,10},{10,1... | collective-permute-start | bytes 786440 | tf_op jit(solution)/shard_map/ppermute | solution.py:550
  104.1 12.3 %collective-permute-start.1 = (bf16[8,48,256]{2,1,0:T(8,128)(2,1)S(1)}, bf16[8,48,256]{2,1,0:T(8,128)(2,1)S(1)}, u32[]{:S(2)}, u32[]{:S(2)}) collective-permute-start(bf16[8,48,256]{2,1,0:T(8,128)(2,1)S(1)} %get-tuple-element.9), channel_id=1, source_target_pairs={{0,16},{16,32},{32,48},{48,64},{64,80},{80,96},{96,112},{112,0},{1... | collective-permute-start | bytes 589832 | tf_op jit(solution)/shard_map/ppermute | solution.py:550
  105.1 11.3 %collective-permute-start.2 = (bf16[4,48,128]{2,1,0:T(8,128)(2,1)S(1)}, bf16[4,48,128]{2,1,0:T(8,128)(2,1)S(1)}, u32[]{:S(2)}, u32[]{:S(2)}) collective-permute-start(bf16[4,48,128]{2,1,0:T(8,128)(2,1)S(1)} %get-tuple-element.10), channel_id=1, source_target_pairs={{0,17},{1,18},{2,19},{3,20},{4,21},{5,22},{6,23},{7,24},{8,25},{9,... | collective-permute-start | bytes 147464 | tf_op jit(solution)/shard_map/ppermute | solution.py:550

commit v10 on v9

--- a/solution.py
+++ b/solution.py
@@ -154,34 +154,94 @@
 
 PLACES = (
     (2, 2),
+    (1, 2),
+    (3, 3),
+    (3, 2),
+    (3, 1),
     (2, 1),
-    (1, 2),
     (2, 3),
-    (3, 2),
     (1, 1),
-    (3, 3),
+    (0, 3),
     (1, 3),
-    (3, 1),
+    (0, 2),
+    (0, 1),
+    (1, 0),
     (2, 0),
-    (0, 2),
-    (1, 0),
-    (0, 1),
     (3, 0),
-    (0, 3),
 )
-
-
-def path(place, r):
-    ups = {0: (), 1: (1,), 2: (1, 1) if r == 0 else (3, 3), 3: (3,)}
-    along_x = [(d, 0) for d in ups[place[0]]]
-    along_z = [(0, d) for d in ups[place[1]]]
-    return along_x + along_z if r == 0 else along_z + along_x
-
-
-PATHS = [[path(place, r) for place in PLACES] for r in range(2)]
-HOPS = [sum(len(p) > h for p in PATHS[0]) for h in range(5)]
-BASE = [0] + [2 * sum(HOPS[1:h]) for h in range(1, 5)]
-LAG = 3
+STEP_X, STEP_Z = (1, 3, 0, 0), (0, 0, 1, 3)
+PATHS = (
+    (
+        (3, 0, 0, 3),
+        (2, 0, 2),
+        (1, 3),
+        (1, 3, 3),
+        (2, 1),
+        (2, 1, 1),
+        (1, 1, 3),
+        (0, 2),
+        (3,),
+        (0, 3),
+        (3, 3),
+        (2,),
+        (0,),
+        (0, 0),
+        (1,),
+    ),
+    (
+        (1, 2, 2, 1),
+        (0, 2, 2),
+        (3, 1),
+        (3, 3, 1),
+        (1, 2),
+        (0, 2, 0),
+        (0, 0, 3),
+        (0, 2),
+        (3,),
+        (3, 0),
+        (2, 2),
+        (2,),
+        (0,),
+        (1, 1),
+        (1,),
+    ),
+)
+FORWARDS = (
+    (),
+    (),
+    ((0, 0, 1), (0, 1, 1)),
+    ((1, 0, 1), (1, 1, 1)),
+    ((2, 0, 1), (2, 1, 1)),
+    ((0, 0, 2), (0, 1, 2)),
+    ((3, 0, 1), (3, 1, 1), (1, 0, 2), (1, 1, 2)),
+    ((4, 1, 1), (4, 0, 1), (5, 1, 1)),
+    ((3, 0, 2),),
+    ((0, 0, 3), (5, 0, 1)),
+    ((3, 1, 2), (6, 0, 1), (0, 1, 3), (6, 1, 1)),
+    (),
+    ((7, 0, 1),),
+    ((5, 0, 2), (7, 1, 1)),
+    ((9, 0, 1),),
+    ((6, 0, 2), (9, 1, 1), (5, 1, 2), (6, 1, 2), (10, 1, 1), (10, 0, 1), (13, 1, 1), (13, 0, 1)),
+)
+COMING = (2, 8, 1, 3, 4, 0, 12, 11, 9, 6, 14, 5, 7, 10, 13)
+
+IN_ORDER = [hop for step in FORWARDS for hop in step]
+FIRST = [sum(len(step) for step in FORWARDS[:i]) for i in range(len(FORWARDS) + 1)]
+RANK = [COMING.index(i) for i in range(len(PLACES))]
+
+
+def coded(place, r, hop):
+    steps = PATHS[r][place]
+    if hop + 1 == len(steps):
+        return steps[hop] + 4 + 8 * (2 * (1 + RANK[place]) + r)
+    return steps[hop] + 8 * IN_ORDER.index((place, r, hop + 1))
+
+
+START = [[coded(place, r, 0) for place in range(len(PLACES))] for r in range(2)]
+ONWARD = [coded(*hop) for hop in IN_ORDER]
+assert len(IN_ORDER) == sum(len(p) - 1 for r in range(2) for p in PATHS[r])
+assert len(IN_ORDER) - FIRST[-2] >= CH
 
 
 def choose(j, values):
@@ -268,61 +328,50 @@
         return at(choose(i, [p[0] for p in PLACES]), choose(i, [p[1] for p in PLACES]))
 
     def share_copy(i):
+        rank = 1 + choose(i, RANK)
         return pltpu.make_async_remote_copy(
-            src_ref=share_ref.at[1 + i],
-            dst_ref=shares.at[1 + i],
-            send_sem=share_send.at[1 + i],
-            recv_sem=share_recv.at[1 + i],
+            src_ref=share_ref.at[rank],
+            dst_ref=shares.at[rank],
+            send_sem=share_send.at[rank],
+            recv_sem=share_recv.at[rank],
             device_id={"fx": place_of(i)},
             device_id_type=pl.DeviceIdType.MESH,
         )
 
-    def hop_copy(h, i, r, last):
-        paths = PATHS[r][: HOPS[h]]
-        to = at(choose(i, [p[h][0] for p in paths]), choose(i, [p[h][1] for p in paths]))
-        own = i * 2 + r
+    def hop_copy(source, send_sem, code, last):
+        step, to = code % 4, code // 8
         return pltpu.make_async_remote_copy(
-            src_ref=sending.at[i, r] if h == 0 else relay.at[BASE[h] + own],
-            dst_ref=arrived.at[1 + i, r] if last else relay.at[BASE[h + 1] + own],
-            send_sem=tile_send.at[own] if h == 0 else relay_send.at[BASE[h] + own],
-            recv_sem=tile_recv.at[1 + i, r] if last else relay_recv.at[BASE[h + 1] + own],
-            device_id={"fx": to},
+            src_ref=source,
+            dst_ref=arrived.at[to] if last else relay.at[to],
+            send_sem=send_sem,
+            recv_sem=tile_recv.at[to] if last else relay_recv.at[to],
+            device_id={"fx": at(choose(step, STEP_X), choose(step, STEP_Z))},
             device_id_type=pl.DeviceIdType.MESH,
         )
 
-    def hop_start(h, i):
-        for r in range(2):
-            if h > 0:
-                slot = BASE[h] + i * 2 + r
-                pltpu.make_async_remote_copy(
-                    src_ref=relay.at[slot],
-                    dst_ref=relay.at[slot],
-                    send_sem=relay_send.at[slot],
-                    recv_sem=relay_recv.at[slot],
-                    device_id={"fx": at(1, 0)},
-                    device_id_type=pl.DeviceIdType.MESH,
-                ).wait_recv()
-            if HOPS[h + 1] == 0:
-                hop_copy(h, i, r, True).start()
-            else:
-
-                @pl.when(i >= HOPS[h + 1])
-                def _():
-                    hop_copy(h, i, r, True).start()
-
-                @pl.when(i < HOPS[h + 1])
-                def _():
-                    hop_copy(h, i, r, False).start()
-
-    def arrival(i, r):
+    def hop_start(source, send_sem, code):
+        @pl.when(code // 4 % 2 == 1)
+        def _():
+            hop_copy(source, send_sem, code, True).start()
+
+        @pl.when(code // 4 % 2 == 0)
+        def _():
+            hop_copy(source, send_sem, code, False).start()
+
+    def landed(buffer, sem):
         return pltpu.make_async_remote_copy(
-            src_ref=arrived.at[1 + i, r],
-            dst_ref=arrived.at[1 + i, r],
+            src_ref=buffer,
+            dst_ref=buffer,
             send_sem=tile_send.at[0],
-            recv_sem=tile_recv.at[1 + i, r],
+            recv_sem=sem,
             device_id={"fx": at(1, 0)},
             device_id_type=pl.DeviceIdType.MESH,
         )
+
+    def forward(f, carry):
+        landed(relay.at[f], relay_recv.at[f]).wait_recv()
+        hop_start(relay.at[f], relay_send.at[f], choose(f, ONWARD))
+        return carry
 
     tiles = vis_hbm.shape[0]
     row = lax.broadcasted_iota(jnp.int32, (8, 128), 0)
@@ -359,7 +408,7 @@
 
     def prepare(i):
         slots = slots_for(place_of(i))
-        share_ref[1 + i] = share_rows(slots)
+        share_ref[1 + choose(i, RANK)] = share_rows(slots)
         sending[i, 0], sending[i, 1] = planes(slots)
 
     prepare(jnp.int32(0))
@@ -367,13 +416,9 @@
 
     def send_tiles(i, carry):
         share_copy(i).start()
-        hop_start(0, i)
-        for h in range(1, 4):
-            before = i - h * LAG
-
-            @pl.when((before >= 0) & (before < HOPS[h]))
-            def _():
-                hop_start(h, before)
+        for r in range(2):
+            hop_start(sending.at[i, r], tile_send.at[2 * i + r], choose(i, START[r]))
+        lax.fori_loop(choose(i, FIRST), choose(i + 1, FIRST), forward, 0)
 
         @pl.when(i < len(PLACES) - 1)
         def _():
@@ -381,11 +426,7 @@
 
         return carry
 
-    assert all(HOPS[h] + h * LAG <= len(PLACES) for h in range(4))
     lax.fori_loop(0, len(PLACES), send_tiles, 0)
-    own = slots_for(fx)
-    shares[0] = share_rows(own)
-    arrived[0, 0], arrived[0, 1] = planes(own)
 
     load_sky.wait()
 
@@ -395,7 +436,22 @@
         model[c] = once + dot(once.astype(BF), excess[...])
         return carry
 
-    lax.fori_loop(0, CH, there_and_back, 0)
+    def forward_and_work(j, carry):
+        forward(FIRST[-2] + j, 0)
+
+        @pl.when(j == 0)
+        def _():
+            own = slots_for(fx)
+            shares[0] = share_rows(own)
+            arrived[0], arrived[1] = planes(own)
+
+        @pl.when(j < CH)
+        def _():
+            there_and_back(j, 0)
+
+        return carry
+
+    lax.fori_loop(0, len(IN_ORDER) - FIRST[-2], forward_and_work, 0)
 
     def wait_share(i, carry):
         share_copy(i).wait_recv()
@@ -432,25 +488,22 @@
     def group_rows(g):
         return pl.ds(pl.multiple_of(g * 16, 16), 16)
 
-    def begin(g, carry):
+    def without_tiles(g):
         pixels = sky[:, group_rows(g), :].reshape(CH * 16, SIDE)
         there = model[:, group_rows(g), :].reshape(CH * 16, SIDE)
-        partial[g] = pixels - (totals * scale) * there
-        return carry
-
-    lax.fori_loop(0, SIDE // 16, begin, 0)
+        return pixels - (totals * scale) * there
 
     def wait_tiles(i, carry):
-        for r in range(2):
-            arrival(i, r).wait_recv()
+        landed(arrived.at[2 + i], tile_recv.at[2 + i]).wait_recv()
         return carry
 
     def with_sources(g, first, last):
-        held = arrived[first:last, :, group_rows(g), :].reshape((last - first) * 32, SIDE)
-        return partial[g] + scale * dot(kron[:, first * 32 : last * 32], held)
+        held = arrived[2 * first : 2 * last, group_rows(g), :].reshape((last - first) * 32, SIDE)
+        before = without_tiles(g) if first == 0 else partial[g]
+        return before + scale * dot(kron[:, first * 32 : last * 32], held)
 
     for first, last in ((0, 8), (8, 12)):
-        lax.fori_loop(max(first - 1, 0), last - 1, wait_tiles, 0)
+        lax.fori_loop(max(2 * first - 2, 0), 2 * last - 2, wait_tiles, 0)
 
         def add_sources(q, carry):
             for i in range(4):
@@ -458,7 +511,7 @@
             return carry
 
         lax.fori_loop(0, SIDE // 64, add_sources, 0)
-    lax.fori_loop(11, len(PLACES), wait_tiles, 0)
+    lax.fori_loop(22, 2 * len(PLACES), wait_tiles, 0)
 
     def combine(g):
         rows = group_rows(g)
@@ -527,14 +580,18 @@
         share_copy(i).wait_send()
         return carry
 
-    def finish_hops(h, i, carry):
+    def finish_sent(i, carry):
         for r in range(2):
-            hop_copy(h, i, r, True).wait_send()
+            hop_copy(sending.at[i, r], tile_send.at[2 * i + r], jnp.int32(0), False).wait_send()
+        return carry
+
+    def finish_forwards(f, carry):
+        hop_copy(relay.at[f], relay_send.at[f], jnp.int32(0), False).wait_send()
         return carry
 
     lax.fori_loop(0, len(PLACES), finish_shares, 0)
-    for h in range(4):
-        lax.fori_loop(0, HOPS[h], functools.partial(finish_hops, h), 0)
+    lax.fori_loop(0, len(PLACES), finish_sent, 0)
+    lax.fori_loop(0, len(IN_ORDER), finish_forwards, 0)
     for i in range(2):
         halo_copy(i).wait_send()
     for q in range(chunks):
@@ -606,8 +663,8 @@
             pltpu.VMEM((CH, SIDE, SIDE), F32),
             pltpu.VMEM((SIDE // 16, CH * 16, SIDE), F32),
             pltpu.VMEM((n_fx, 2, SIDE, SIDE), BF),
-            pltpu.VMEM((n_fx, 2, SIDE, SIDE), BF),
-            pltpu.VMEM((BASE[4], SIDE, SIDE), BF),
+            pltpu.VMEM((2 * n_fx, SIDE, SIDE), BF),
+            pltpu.VMEM((len(IN_ORDER), SIDE, SIDE), BF),
             pltpu.VMEM((2, 2 * SIDE, SIDE), BF),
             pltpu.VMEM((n_fx, 8, 128), F32),
             pltpu.VMEM((n_fx, 8, 128), F32),
@@ -617,9 +674,9 @@
             pltpu.VMEM((CH // 2, HALO, 128), BF),
             dma((2,)),
             dma((2 * len(PLACES),)),
-            dma((n_fx, 2)),
-            dma((BASE[4],)),
-            dma((BASE[4],)),
+            dma((2 * n_fx,)),
+            dma((len(IN_ORDER),)),
+            dma((len(IN_ORDER),)),
             dma((n_fx,)),
             dma((n_fx,)),
             dma((2,)),
@@ -654,7 +711,7 @@
             jax.ShapeDtypeStruct((CH // 2, HALO, 128), BF),
             jax.ShapeDtypeStruct((CH, HALO, SIDE), BF),
         ),
-        in_specs=[anywhere],
+        in_specs=[pl.BlockSpec(memory_space=pltpu.HBM)],
         out_specs=[vmem] * 3,
         scratch_shapes=[
             pltpu.VMEM((CH, TALL, 128), F32),

time: 119 us -> 113 us (0.950)
  Pallas kernels: 74.8 us -> 69.2 us
  waiting for transfers between devices: 7.8 us -> 9.18 us
  starting transfers between devices: 4.82 us -> 3.45 us
    pallas_call x1, Pallas kernels: 72.5 us -> 66.9 us  [per_device(): pl.pallas_call(functools.partial(exchange_kernel, n_fy, n_fx), out_shape=...]
    ppermute x3, waiting for transfers between devices: 7.8 us -> 9.18 us  [passed(): return lax.ppermute(value, axes if len(axes) > 1 else axes[0], pairs)]
    ppermute x3, starting transfers between devices: 4.82 us -> 3.45 us  [passed(): return lax.ppermute(value, axes if len(axes) > 1 else axes[0], pairs)]
where the time goes in v10:
time: 113 us
  Pallas kernels  69.2 us (61%)
  matrix products  29 us (26%)
  waiting for transfers between devices  9.18 us (8%)
  starting transfers between devices  3.45 us (3%)
  local copies, waits for them, and re-layouts  2.06 us (2%)
    pallas_call x1, Pallas kernels, per_device(): pl.pallas_call(functools.partial(exchange_kernel, n_fy, n_fx), out_shape=...  66.9 us
    dot_general x1, matrix products, per_device(): jnp.einsum('bcyx,bkx->bcyk', row_sec, columns, preferred_element_type=F32)  16.9 us
    dot_general x1, matrix products, per_device(): jnp.einsum('bcyk,bkx->cyx', row_sec, made['spread'], preferred_element_ty...  12.1 us
    ppermute x3, waiting for transfers between devices, passed(): return lax.ppermute(value, axes if len(axes) > 1 else axes[0], pairs)  9.18 us
    ppermute x3, starting transfers between devices, passed(): return lax.ppermute(value, axes if len(axes) > 1 else axes[0], pairs)  3.45 us
  transfers between devices with their start and end apart: 3, of which 1 were waited for; matrix products, arithmetic and copies ran while one was open for 0% of the time, Pallas kernels for 0%

profile of v10, /device:TPU:1, one launch (start us, length us, event | category | flops | bytes accessed | tf_op | source)
XLA Modules:
  0.0 113.0 jit_solution(17237402654461191439)
XLA Ops:
  0.0 66.9 %shard_map.118 = bf16[8,304,384]{2,1,0:T(8,128)(2,1)S(1)} custom-call(s32[16]{0:T(128)} %bitcast.29, s32[16]{0:T(128)} %chan_ref.1, s32[16]{0:T(128)} %count_ref.1, bf16[512,512]{1,0:T(8,128)(2,1)} %constant.15.clone.fourier, bf16[256,512]{1,0:T(8,128)(2,1)} %constant.16.clone.back, bf16[256,256]{1,0:T(8,128)(2,1)} %constant.17.clone.excess, ...), custom_call_target="tpu_custom_call" | custom-call | tf_op jit(solution)/shard_map/pallas_call | solution.py:656
  66.9 0.0 copy-start.1
  67.0 16.9 %fusion.2 = bf16[8,8,256,256]{3,2,1,0:T(8,128)(2,1)} fusion(bf16[8,8,256,256]{3,2,1,0:T(8,128)(2,1)} %param.17, bf16[8,256,384,1]{2,1,3,0:T(8,128)(2,1)} %constant.23, bf16[8,256,304,1]{2,1,3,0:T(8,128)(2,1)} %constant.22, bf16[8,304,384]{2,1,0:T(8,128)(2,1)S(1)} %shard_map.118), kind=kOutput, calls=%fused_computation.4 | convolution fusion | flops 7077888000 | bytes 21463040 | tf_op jit(solution)/shard_map/bcyx,bkx->bcyk/dot_general | solution.py:702
  83.9 0.0 copy-done.1
  83.9 12.1 %fusion.19.cells = f32[8,304,384]{2,1,0:T(8,128)} fusion(bf16[8,256,384,1]{2,1,0,3:T(8,128)(2,1)S(1)} %copy-done.1, bf16[8,256,304,1]{2,1,0,3:T(8,128)(2,1)} %constant.24, bf16[8,8,256,256]{3,2,1,0:T(8,128)(2,1)} %fusion.2), kind=kOutput, calls=%fused_computation.14 | convolution fusion | flops 6380322816 | bytes 14942208 | tf_op jit(solution)/shard_map/bcyk,bkx->cyx/dot_general | solution.py:706
  96.0 0.0 copy-start
  96.0 2.1 %copy-done = f32[8,304,384]{2,1,0:T(8,128)S(1)} copy-done((f32[8,304,384]{2,1,0:T(8,128)S(1)}, f32[8,304,384]{2,1,0:T(8,128)}, u32[]{:S(2)}) %copy-start) | copy-done | bytes 3735576
  98.0 0.2 shard_map.119
  98.2 0.7 collective-permute-start
  99.0 2.3 %collective-permute-start.1 = (bf16[8,48,256]{2,1,0:T(8,128)(2,1)S(1)}, bf16[8,48,256]{2,1,0:T(8,128)(2,1)S(1)}, u32[]{:S(2)}, u32[]{:S(2)}) collective-permute-start(bf16[8,48,256]{2,1,0:T(8,128)(2,1)S(1)} %get-tuple-element.9), channel_id=1, source_target_pairs={{0,16},{16,32},{32,48},{48,64},{64,80},{80,96},{96,112},{112,0},{1... | collective-permute-start | bytes 589832 | tf_op jit(solution)/shard_map/ppermute | solution.py:607
  101.3 0.4 collective-permute-start.2
  101.7 9.2 %collective-permute-done.2.corner = bf16[4,48,128]{2,1,0:T(8,128)(2,1)S(1)} collective-permute-done((bf16[4,48,128]{2,1,0:T(8,128)(2,1)S(1)}, bf16[4,48,128]{2,1,0:T(8,128)(2,1)S(1)}, u32[]{:S(2)}, u32[]{:S(2)}) %collective-permute-start.2) | collective-permute-done | bytes 49184 | tf_op jit(solution)/shard_map/ppermute | solution.py:607
  110.9 0.0 collective-permute-done.1.above
  110.9 0.0 collective-permute-done.left
  110.9 2.1 %shard_map.120 = f32[8,256,256]{2,1,0:T(8,128)} custom-call(f32[8,304,384]{2,1,0:T(8,128)S(1)} %copy-done, bf16[4,256,128]{2,1,0:T(8,128)(2,1)S(1)} %collective-permute-done.left, bf16[8,48,256]{2,1,0:T(8,128)(2,1)S(1)} %collective-permute-done.1.above, bf16[4,48,128]{2,1,0:T(8,128)(2,1)S(1)} %collective-permute-done.2.corner), custom_call_target="tpu_custom_call" | custom-call | tf_op jit(solution)/shard_map/pallas_call | solution.py:726
Async XLA Ops:
  66.9 16.9 %copy-start.1 = (bf16[8,256,384,1]{2,1,0,3:T(8,128)(2,1)S(1)}, bf16[8,256,384,1]{2,1,0,3:T(8,128)(2,1)}, u32[]{:S(2)}) copy-start(bf16[8,256,384,1]{2,1,0,3:T(8,128)(2,1)} %constant.25) | copy-start | bytes 4718596
  96.0 2.1 %copy-start = (f32[8,304,384]{2,1,0:T(8,128)S(1)}, f32[8,304,384]{2,1,0:T(8,128)}, u32[]{:S(2)}) copy-start(f32[8,304,384]{2,1,0:T(8,128)} %fusion.19.cells) | copy-start | bytes 11206660
  98.2 12.6 %collective-permute-start = (bf16[4,256,128]{2,1,0:T(8,128)(2,1)S(1)}, bf16[4,256,128]{2,1,0:T(8,128)(2,1)S(1)}, u32[]{:S(2)}, u32[]{:S(2)}) collective-permute-start(bf16[4,256,128]{2,1,0:T(8,128)(2,1)S(1)} %get-tuple-element.8), channel_id=1, source_target_pairs={{0,1},{1,2},{2,3},{3,4},{4,5},{5,6},{6,7},{7,8},{8,9},{9,10},{10,1... | collective-permute-start | bytes 786440 | tf_op jit(solution)/shard_map/ppermute | solution.py:607
  99.0 11.9 %collective-permute-start.1 = (bf16[8,48,256]{2,1,0:T(8,128)(2,1)S(1)}, bf16[8,48,256]{2,1,0:T(8,128)(2,1)S(1)}, u32[]{:S(2)}, u32[]{:S(2)}) collective-permute-start(bf16[8,48,256]{2,1,0:T(8,128)(2,1)S(1)} %get-tuple-element.9), channel_id=1, source_target_pairs={{0,16},{16,32},{32,48},{48,64},{64,80},{80,96},{96,112},{112,0},{1... | collective-permute-start | bytes 589832 | tf_op jit(solution)/shard_map/ppermute | solution.py:607
  101.3 9.6 %collective-permute-start.2 = (bf16[4,48,128]{2,1,0:T(8,128)(2,1)S(1)}, bf16[4,48,128]{2,1,0:T(8,128)(2,1)S(1)}, u32[]{:S(2)}, u32[]{:S(2)}) collective-permute-start(bf16[4,48,128]{2,1,0:T(8,128)(2,1)S(1)} %get-tuple-element.10), channel_id=1, source_target_pairs={{0,17},{1,18},{2,19},{3,20},{4,21},{5,22},{6,23},{7,24},{8,25},{9,... | collective-permute-start | bytes 147464 | tf_op jit(solution)/shard_map/ppermute | solution.py:607

commit v11 on v10

--- a/solution.py
+++ b/solution.py
@@ -102,6 +102,8 @@
 F32 = jnp.float32
 WIDE = SIDE + 128
 TALL = SIDE + HALO
+PART = SIDE // 2
+PART_TALL = PART + HALO
 
 
 def rounded(table):
@@ -135,13 +137,24 @@
     return rounded(full).astype(np.float32)
 
 
+def half_blocks(g):
+    return ((32 * g, 32), (64 + 32 * g, 32), (128 + 64 * g, 64))
+
+
+def half_rows(g):
+    return np.concatenate([np.arange(first, first + rows) for first, rows in half_blocks(g)])
+
+
 @functools.lru_cache(maxsize=1)
 def tables():
     full = composite_tables()
     wide = np.concatenate([full, np.zeros((BASES, SIDE, 128 - HALO), np.float32)], axis=2)
     spread = wide.copy()
     spread[:, :, TALL + 16 : TALL + 16 + HALO] = full[:, :, SIDE:]
-    out = {"rows": full, "columns": wide, "spread": spread}
+    halves = [full[:, half_rows(g), g * PART : g * PART + PART_TALL] for g in range(2)]
+    assert np.array_equal(halves[0], halves[1])
+    assert np.count_nonzero(halves[0]) * 2 == np.count_nonzero(full)
+    out = {"rows": halves[0], "columns": wide, "spread": spread}
     grid = np.arange(SIDE)[:, None] * np.arange(SIDE)[None, :] % SIDE
     angle = grid * (2.0 * math.pi / SIDE)
     cosine = rounded(np.cos(angle) / math.sqrt(SIDE)).astype(np.float64)
@@ -266,7 +279,11 @@
     excess,
     sky_hbm,
     vis_hbm,
-    extended,
+    thr_hbm,
+    upper,
+    lower,
+    thr_upper,
+    thr_lower,
     vis,
     sky,
     model,
@@ -292,6 +309,7 @@
     halo_recv,
     columns_send,
     columns_recv,
+    thr_sem,
 ):
     fy = lax.axis_index("fy")
     fx = lax.axis_index("fx")
@@ -396,6 +414,20 @@
         return total
 
     load_vis.wait()
+    thr_copies = []
+    for g, target in enumerate((thr_upper, thr_lower)):
+        begin = 0
+        for i, (first, rows) in enumerate(half_blocks(g)):
+            thr_copies.append(
+                pltpu.make_async_copy(
+                    thr_hbm.at[:, :, first : first + rows, :],
+                    target.at[:, :, begin : begin + rows, :],
+                    thr_sem.at[3 * g + i],
+                )
+            )
+            begin += rows
+    for copy in thr_copies:
+        copy.start()
 
     def planes(slots):
         for i, (t, _, _) in enumerate(slots):
@@ -516,7 +548,16 @@
     def combine(g):
         rows = group_rows(g)
         new = with_sources(g, 12, 16).reshape(CH // 2, 2, 16, SIDE)
-        extended[:, rows, :SIDE] = new.reshape(CH, 16, SIDE).astype(BF)
+        made = new.reshape(CH, 16, SIDE).astype(BF)
+
+        @pl.when(g < PART_TALL // 16)
+        def _():
+            upper[:, rows, :SIDE] = made
+
+        @pl.when(g >= PART // 16)
+        def _():
+            lower[:, group_rows(g - PART // 16), :SIDE] = made
+
         low = lax.broadcasted_iota(jnp.int32, (CH // 2, 16, 128), 2) < 64
         second = pltpu.roll(new[:, 1, :, :128].reshape(CH // 2 * 16, 128), 64, 1)
         pair = jnp.where(low, new[:, 0, :, :128], second.reshape(CH // 2, 16, 128))
@@ -537,8 +578,8 @@
         )
 
     def halo_copy(i):
-        source = (extended.at[:, :HALO, :SIDE], columns.at[:, :HALO, :])[i]
-        target = (extended.at[:, SIDE:, :SIDE], corner)[i]
+        source = (upper.at[:, :HALO, :SIDE], columns.at[:, :HALO, :])[i]
+        target = (lower.at[:, PART:, :SIDE], corner)[i]
         where = ({"fy": up}, {"fy": up, "fx": prev})[i]
         return pltpu.make_async_remote_copy(
             src_ref=source,
@@ -566,8 +607,12 @@
     def place(source, begin, end):
         for p in range(CH // 2):
             first = source[p]
-            extended[2 * p, begin:end, SIDE:] = first
-            extended[2 * p + 1, begin:end, SIDE:] = pltpu.roll(first.astype(F32), 64, 1).astype(BF)
+            second = pltpu.roll(first.astype(F32), 64, 1).astype(BF)
+            for target, low, high in ((upper, 0, PART_TALL), (lower, PART, TALL)):
+                a, e = max(begin, low), min(end, high)
+                if a < e:
+                    target[2 * p, a - low : e - low, SIDE:] = first[a - begin : e - begin]
+                    target[2 * p + 1, a - low : e - low, SIDE:] = second[a - begin : e - begin]
 
     halo_copy(1).wait_recv()
     place(corner, SIDE, TALL)
@@ -596,6 +641,8 @@
         halo_copy(i).wait_send()
     for q in range(chunks):
         columns_copy(q).wait_send()
+    for copy in thr_copies:
+        copy.wait()
 
 
 def passed(value, axes, to):
@@ -611,21 +658,31 @@
     return lax.broadcasted_iota(jnp.int32, shape, len(shape) - 1) < 64
 
 
-def pack_kernel(cells, right, corner, below, side, bottom, sem):
-    load_side = pltpu.make_async_copy(cells.at[:, :, SIDE:], side, sem.at[0])
-    load_bottom = pltpu.make_async_copy(cells.at[:, SIDE:, :SIDE], bottom, sem.at[1])
-    load_side.start()
-    load_bottom.start()
-    load_side.wait()
+def pack_kernel(upper, lower, right, corner, below, side_up, side_low, bottom, sem):
+    loads = [
+        pltpu.make_async_copy(upper.at[:, :, SIDE:], side_up, sem.at[0]),
+        pltpu.make_async_copy(lower.at[:, :, SIDE:], side_low, sem.at[1]),
+        pltpu.make_async_copy(lower.at[:, PART:, :SIDE], bottom, sem.at[2]),
+    ]
+    for load in loads:
+        load.start()
+    for load in loads:
+        load.wait()
+
+    def pair(side, p, begin, end):
+        first, second = side[2 * p, begin:end], side[2 * p + 1, begin:end]
+        return jnp.where(first_half(first.shape), first, second)
+
     for p in range(CH // 2):
-        both = jnp.where(first_half((TALL, 128)), side[2 * p], side[2 * p + 1]).astype(BF)
-        right[p] = both[:SIDE]
-        corner[p] = both[SIDE:]
-    load_bottom.wait()
+        right[p, :PART] = pair(side_up, p, 0, PART).astype(BF)
+        shared = pair(side_up, p, PART, PART_TALL) + pair(side_low, p, 0, HALO)
+        right[p, PART:PART_TALL] = shared.astype(BF)
+        right[p, PART_TALL:] = pair(side_low, p, HALO, PART).astype(BF)
+        corner[p] = pair(side_low, p, PART, PART_TALL).astype(BF)
     below[...] = bottom[...].astype(BF)
 
 
-def add_kernel(cells, left, above, corner, out):
+def add_kernel(upper, lower, left, above, corner, out):
     for h in range(2):
 
         def columns(pairs):
@@ -640,10 +697,19 @@
         from_left = columns(left[0])
         from_above = above[h].astype(F32)
         first = from_left[:HALO] + from_above[:, :128] + columns(corner[0])
-        out[h, :HALO, :128] = finished(cells[h, :HALO, :128] + first)
-        out[h, :HALO, 128:] = finished(cells[h, :HALO, 128:] + from_above[:, 128:])
-        out[h, HALO:, :128] = finished(cells[h, HALO:, :128] + from_left[HALO:])
-        out[h, HALO:, 128:] = finished(cells[h, HALO:, 128:])
+        out[h, :HALO, :128] = finished(upper[h, :HALO, :128] + first)
+        out[h, :HALO, 128:] = finished(upper[h, :HALO, 128:] + from_above[:, 128:])
+        for lanes in (slice(0, 128), slice(128, SIDE)):
+
+            def more(begin, end):
+                return from_left[begin:end] if lanes.start == 0 else 0.0
+
+            out[h, HALO:PART, lanes] = finished(upper[h, HALO:PART, lanes] + more(HALO, PART))
+            shared = upper[h, PART:PART_TALL, lanes] + lower[h, :HALO, lanes]
+            out[h, PART:PART_TALL, lanes] = finished(shared + more(PART, PART_TALL))
+            out[h, PART_TALL:, lanes] = finished(
+                lower[h, HALO:PART, lanes] + more(PART_TALL, SIDE)
+            )
 
 
 def per_device(n_fy, n_fx, sky_image, vis_tiles, tile_dest, tile_chan, tile_count, thresholds):
@@ -653,10 +719,15 @@
     anywhere = pl.BlockSpec(memory_space=pl.ANY)
     dma = pltpu.SemaphoreType.DMA
     tiles = vis_tiles.shape[0]
-    extended = pl.pallas_call(
+    upper, lower, thr_upper, thr_lower = pl.pallas_call(
         functools.partial(exchange_kernel, n_fy, n_fx),
-        out_shape=pltpu.VMEM((CH, TALL, WIDE), BF),
-        in_specs=[smem] * 3 + [vmem] * 3 + [anywhere] * 2,
+        out_shape=(
+            pltpu.VMEM((CH, PART_TALL, WIDE), BF),
+            pltpu.VMEM((CH, PART_TALL, WIDE), BF),
+            pltpu.HBM((BASES, CH, PART, SIDE), BF),
+            pltpu.HBM((BASES, CH, PART, SIDE), BF),
+        ),
+        in_specs=[smem] * 3 + [vmem] * 3 + [anywhere] * 3,
         scratch_shapes=[
             pltpu.VMEM((tiles, 2, SIDE, SIDE), BF),
             pltpu.VMEM((CH, SIDE, SIDE), F32),
@@ -683,6 +754,7 @@
             dma((2,)),
             dma((4,)),
             dma((4,)),
+            dma((6,)),
         ],
         compiler_params=pltpu.CompilerParams(
             collective_id=0, has_side_effects=True, vmem_limit_bytes=58 * 1024 * 1024
@@ -696,14 +768,19 @@
         made["excess"],
         sky_image,
         vis_tiles,
+        thresholds,
     )
-    rows, columns = made["rows"], made["columns"]
-    row_sec = jnp.einsum("bkn,cnx->bckx", rows, extended, preferred_element_type=F32).astype(BF)
-    coefficient = jnp.einsum("bcyx,bkx->bcyk", row_sec, columns, preferred_element_type=F32)
-    limits = thresholds.astype(F32)
-    shrunk = (coefficient - jnp.clip(coefficient, -limits, limits)).astype(BF)
-    row_sec = jnp.einsum("bjy,bcjk->bcyk", rows, shrunk, preferred_element_type=F32).astype(BF)
-    cells = jnp.einsum("bcyk,bkx->cyx", row_sec, made["spread"], preferred_element_type=F32)
+    rows, columns, spread = made["rows"], made["columns"], made["spread"]
+    cells = []
+    for near, limits in ((upper, thr_upper), (lower, thr_lower)):
+        row_sec = jnp.einsum("bjy,cyx->bcjx", rows, near, preferred_element_type=F32).astype(BF)
+        coefficient = jnp.einsum("bcjx,bkx->bcjk", row_sec, columns, preferred_element_type=F32)
+        limits = limits.astype(F32)
+        shrunk = (coefficient - jnp.clip(coefficient, -limits, limits)).astype(BF)
+        col_sec = jnp.einsum("bcjk,bkx->bcjx", shrunk, spread, preferred_element_type=F32)
+        cells.append(
+            jnp.einsum("bjy,bcjx->cyx", rows, col_sec.astype(BF), preferred_element_type=F32)
+        )
     right, corner, below = pl.pallas_call(
         pack_kernel,
         out_shape=(
@@ -711,15 +788,16 @@
             jax.ShapeDtypeStruct((CH // 2, HALO, 128), BF),
             jax.ShapeDtypeStruct((CH, HALO, SIDE), BF),
         ),
-        in_specs=[pl.BlockSpec(memory_space=pltpu.HBM)],
+        in_specs=[pl.BlockSpec(memory_space=pltpu.HBM)] * 2,
         out_specs=[vmem] * 3,
         scratch_shapes=[
-            pltpu.VMEM((CH, TALL, 128), F32),
+            pltpu.VMEM((CH, PART_TALL, 128), F32),
+            pltpu.VMEM((CH, PART_TALL, 128), F32),
             pltpu.VMEM((CH, HALO, SIDE), F32),
-            dma((2,)),
+            dma((3,)),
         ],
-        compiler_params=pltpu.CompilerParams(vmem_limit_bytes=16 * 1024 * 1024),
-    )(cells)
+        compiler_params=pltpu.CompilerParams(vmem_limit_bytes=58 * 1024 * 1024),
+    )(*cells)
     left = passed(right, ("fx",), (1,))
     above = passed(below, ("fy",), (1,))
     corner = passed(corner, ("fy", "fx"), (1, 1))
@@ -728,14 +806,15 @@
         out_shape=jax.ShapeDtypeStruct((CH, SIDE, SIDE), F32),
         grid=(CH // 2,),
         in_specs=[
-            pl.BlockSpec((2, SIDE, SIDE), lambda p: (p, 0, 0)),
+            pl.BlockSpec((2, PART_TALL, SIDE), lambda p: (p, 0, 0)),
+            pl.BlockSpec((2, PART_TALL, SIDE), lambda p: (p, 0, 0)),
             pl.BlockSpec((1, SIDE, 128), lambda p: (p, 0, 0)),
             pl.BlockSpec((2, HALO, SIDE), lambda p: (p, 0, 0)),
             pl.BlockSpec((1, HALO, 128), lambda p: (p, 0, 0)),
         ],
         out_specs=pl.BlockSpec((2, SIDE, SIDE), lambda p: (p, 0, 0)),
         compiler_params=pltpu.CompilerParams(vmem_limit_bytes=16 * 1024 * 1024),
-    )(cells, left, above, corner)
+    )(*cells, left, above, corner)
 
 
 def solution(mesh):

time: 113 us -> 119 us (1.053)
  Pallas kernels: 69.2 us -> 75.4 us
  local copies, waits for them, and re-layouts: 2.06 us -> 0.02 us
  matrix products: 29 us -> 30.3 us
    pallas_call x1, Pallas kernels: 66.9 us -> 70.8 us  [per_device(): pl.pallas_call(functools.partial(exchange_kernel, n_fy, n_fx), out_shape=...]
    pallas_call x1, Pallas kernels: 0.2 us -> 2.45 us  [per_device(): pl.pallas_call(pack_kernel, out_shape=(jax.ShapeDtypeStruct((CH // 2, SID...]
    unnamed x4 -> x10, local copies, waits for them, and re-layouts: 2.06 us -> 0.02 us
    dot_general x2 -> x4, matrix products: 29 us -> 30.3 us  [the longest x2 16.3 us: per_device(): jnp.einsum('bcjx,bkx->bcjk', row_sec, columns, preferred_element_type=F32)]
where the time goes in v11:
time: 119 us
  Pallas kernels  75.4 us (63%)
  matrix products  30.3 us (25%)
  waiting for transfers between devices  9.39 us (8%)
  starting transfers between devices  3.44 us (3%)
    pallas_call x1, Pallas kernels, per_device(): pl.pallas_call(functools.partial(exchange_kernel, n_fy, n_fx), out_shape=...  70.8 us
    dot_general x2, matrix products, per_device(): jnp.einsum('bcjx,bkx->bcjk', row_sec, columns, preferred_element_type=F32)  16.3 us
    dot_general x2, matrix products, per_device(): jnp.einsum('bjy,bcjx->cyx', rows, col_sec.astype(BF), preferred_element_t...  14 us
    ppermute x3, waiting for transfers between devices, passed(): return lax.ppermute(value, axes if len(axes) > 1 else axes[0], pairs)  9.39 us
    ppermute x3, starting transfers between devices, passed(): return lax.ppermute(value, axes if len(axes) > 1 else axes[0], pairs)  3.44 us
    pallas_call x1, Pallas kernels, per_device(): pl.pallas_call(pack_kernel, out_shape=(jax.ShapeDtypeStruct((CH // 2, SID...  2.45 us
  transfers between devices with their start and end apart: 3, of which 1 were waited for; matrix products, arithmetic and copies ran while one was open for 0% of the time, Pallas kernels for 0%

profile of v11, /device:TPU:1, one launch (start us, length us, event | category | flops | bytes accessed | tf_op | source)
XLA Modules:
  0.0 118.6 jit_solution(13732944734285832579)
XLA Ops:
  0.0 0.0 copy-start.4
  0.0 70.8 %shard_map.118 = (bf16[8,176,384]{2,1,0:T(8,128)(2,1)S(1)}, bf16[8,176,384]{2,1,0:T(8,128)(2,1)S(1)}, bf16[8,8,128,256]{3,2,1,0:T(8,128)(2,1)}, bf16[8,8,128,256]{3,2,1,0:T(8,128)(2,1)}) custom-call(s32[16]{0:T(128)} %bitcast.44, s32[16]{0:T(128)} %chan_ref.1, s32[16]{0:T(128)} %count_ref.1, bf16[512,512]{1,0:T(8,128)(2,1)} %constant.15.clone.fourier, ...), custom_call_target="tpu_custom_call" | custom-call | tf_op jit(solution)/shard_map/pallas_call | solution.py:722
  70.8 0.0 copy-done.4
  70.8 8.1 %fusion.2 = bf16[8,8,128,256]{3,2,1,0:T(8,128)(2,1)} fusion(bf16[8,8,128,256]{3,2,1,0:T(8,128)(2,1)} %get-tuple-element.13, bf16[8,256,384,1]{2,1,3,0:T(8,128)(2,1)} %constant.23, bf16[8,128,176,1]{1,2,3,0:T(8,128)(2,1)S(1)} %copy-done.4, bf16[8,176,384]{2,1,0:T(8,128)(2,1)S(1)} %get-tuple-element.12), kind=kOutput, calls=%fused_computation.6 | convolution fusion | flops 2733637632 | bytes 11403264 | tf_op jit(solution)/shard_map/bcjx,bkx->bcjk/dot_general | solution.py:777
  78.9 0.0 copy-start.2
  78.9 0.0 copy-start.3
  78.9 8.2 %fusion.5 = bf16[8,8,128,256]{3,2,1,0:T(8,128)(2,1)} fusion(bf16[8,8,128,256]{3,2,1,0:T(8,128)(2,1)} %get-tuple-element.15, bf16[8,256,384,1]{2,1,3,0:T(8,128)(2,1)} %constant.23, bf16[8,128,176,1]{1,2,3,0:T(8,128)(2,1)S(1)} %copy-done.4, bf16[8,176,384]{2,1,0:T(8,128)(2,1)S(1)} %get-tuple-element.14), kind=kOutput, calls=%fused_computation.9 | convolution fusion | flops 2733637632 | bytes 11403264 | tf_op jit(solution)/shard_map/bcjx,bkx->bcjk/dot_general | solution.py:777
  87.1 0.0 copy-done.2
  87.1 0.0 copy-done.3
  87.1 7.0 %fusion.36.upper = f32[8,176,384]{2,1,0:T(8,128)} fusion(bf16[8,128,176,1]{1,2,0,3:T(8,128)(2,1)S(1)} %copy-done.3, bf16[8,256,384,1]{2,1,0,3:T(8,128)(2,1)S(1)} %copy-done.2, bf16[8,8,128,256]{3,2,1,0:T(8,128)(2,1)} %fusion.2), kind=kOutput, calls=%fused_computation.26 | convolution fusion | flops 2721054720 | bytes 8290304 | tf_op jit(solution)/shard_map/bjy,bcjx->cyx/dot_general | solution.py:782
  94.1 7.0 %fusion.41.lower = f32[8,176,384]{2,1,0:T(8,128)} fusion(bf16[8,128,176,1]{1,2,0,3:T(8,128)(2,1)S(1)} %copy-done.3, bf16[8,256,384,1]{2,1,0,3:T(8,128)(2,1)S(1)} %copy-done.2, bf16[8,8,128,256]{3,2,1,0:T(8,128)(2,1)} %fusion.5), kind=kOutput, calls=%fused_computation.27 | convolution fusion | flops 2721054720 | bytes 8290304 | tf_op jit(solution)/shard_map/bjy,bcjx->cyx/dot_general | solution.py:782
  101.1 0.0 copy-start
  101.1 0.0 copy-start.1
  101.1 2.5 %shard_map.119 = (bf16[4,256,128]{2,1,0:T(8,128)(2,1)}, bf16[4,48,128]{2,1,0:T(8,128)(2,1)}, bf16[8,48,256]{2,1,0:T(8,128)(2,1)}) custom-call(f32[8,176,384]{2,1,0:T(8,128)} %fusion.36.upper, f32[8,176,384]{2,1,0:T(8,128)} %fusion.41.lower), custom_call_target="tpu_custom_call" | custom-call | tf_op jit(solution)/shard_map/pallas_call | solution.py:784
  103.6 0.7 collective-permute-start
  104.3 2.3 %collective-permute-start.1 = (bf16[8,48,256]{2,1,0:T(8,128)(2,1)}, bf16[8,48,256]{2,1,0:T(8,128)(2,1)S(1)}, u32[]{:S(2)}, u32[]{:S(2)}) collective-permute-start(bf16[8,48,256]{2,1,0:T(8,128)(2,1)} %get-tuple-element.17), channel_id=1, source_target_pairs={{0,16},{16,32},{32,48},{48,64},{64,80},{80,96},{96,112},{112,0},{1... | collective-permute-start | bytes 589832 | tf_op jit(solution)/shard_map/ppermute | solution.py:654
  106.6 0.4 collective-permute-start.2
  107.0 9.4 %collective-permute-done.2.corner = bf16[4,48,128]{2,1,0:T(8,128)(2,1)S(1)} collective-permute-done((bf16[4,48,128]{2,1,0:T(8,128)(2,1)}, bf16[4,48,128]{2,1,0:T(8,128)(2,1)S(1)}, u32[]{:S(2)}, u32[]{:S(2)}) %collective-permute-start.2) | collective-permute-done | bytes 49184 | tf_op jit(solution)/shard_map/ppermute | solution.py:654
  116.4 0.0 collective-permute-done.1.above
  116.4 0.0 collective-permute-done.left
  116.4 0.0 copy-done
  116.4 0.0 copy-done.1
  116.4 2.2 %shard_map.120 = f32[8,256,256]{2,1,0:T(8,128)} custom-call(f32[8,176,384]{2,1,0:T(8,128)S(1)} %copy-done, f32[8,176,384]{2,1,0:T(8,128)S(1)} %copy-done.1, bf16[4,256,128]{2,1,0:T(8,128)(2,1)S(1)} %collective-permute-done.left, bf16[8,48,256]{2,1,0:T(8,128)(2,1)S(1)} %collective-permute-done.1.above, bf16[4,48,128]{2,1,0:T(8,128)(2,1)S(1)} %collective-permute-done.2.corner), custom_call_target="tpu_custom_call" | custom-call | tf_op jit(solution)/shard_map/pallas_call | solution.py:804
Async XLA Ops:
  0.0 70.8 %copy-start.4 = (bf16[8,128,176,1]{1,2,3,0:T(8,128)(2,1)S(1)}, bf16[8,128,176,1]{1,2,3,0:T(8,128)(2,1)}, u32[]{:S(2)}) copy-start(bf16[8,128,176,1]{1,2,3,0:T(8,128)(2,1)} %constant.22) | copy-start | bytes 1081348
  78.9 8.2 %copy-start.2 = (bf16[8,256,384,1]{2,1,0,3:T(8,128)(2,1)S(1)}, bf16[8,256,384,1]{2,1,0,3:T(8,128)(2,1)}, u32[]{:S(2)}) copy-start(bf16[8,256,384,1]{2,1,0,3:T(8,128)(2,1)} %constant.24) | copy-start | bytes 4718596
  78.9 8.2 %copy-start.3 = (bf16[8,128,176,1]{1,2,0,3:T(8,128)(2,1)S(1)}, bf16[8,128,176,1]{1,2,0,3:T(8,128)(2,1)}, u32[]{:S(2)}) copy-start(bf16[8,128,176,1]{1,2,0,3:T(8,128)(2,1)} %constant.25) | copy-start | bytes 1081348
  101.1 15.3 %copy-start = (f32[8,176,384]{2,1,0:T(8,128)S(1)}, f32[8,176,384]{2,1,0:T(8,128)}, u32[]{:S(2)}) copy-start(f32[8,176,384]{2,1,0:T(8,128)} %fusion.36.upper) | copy-start | bytes 6488068
  101.1 15.3 %copy-start.1 = (f32[8,176,384]{2,1,0:T(8,128)S(1)}, f32[8,176,384]{2,1,0:T(8,128)}, u32[]{:S(2)}) copy-start(f32[8,176,384]{2,1,0:T(8,128)} %fusion.41.lower) | copy-start | bytes 6488068
  103.6 12.8 %collective-permute-start = (bf16[4,256,128]{2,1,0:T(8,128)(2,1)}, bf16[4,256,128]{2,1,0:T(8,128)(2,1)S(1)}, u32[]{:S(2)}, u32[]{:S(2)}) collective-permute-start(bf16[4,256,128]{2,1,0:T(8,128)(2,1)} %get-tuple-element.16), channel_id=1, source_target_pairs={{0,1},{1,2},{2,3},{3,4},{4,5},{5,6},{6,7},{7,8},{8,9},{9,10},{10,1... | collective-permute-start | bytes 786440 | tf_op jit(solution)/shard_map/ppermute | solution.py:654
  104.3 12.1 %collective-permute-start.1 = (bf16[8,48,256]{2,1,0:T(8,128)(2,1)}, bf16[8,48,256]{2,1,0:T(8,128)(2,1)S(1)}, u32[]{:S(2)}, u32[]{:S(2)}) collective-permute-start(bf16[8,48,256]{2,1,0:T(8,128)(2,1)} %get-tuple-element.17), channel_id=1, source_target_pairs={{0,16},{16,32},{32,48},{48,64},{64,80},{80,96},{96,112},{112,0},{1... | collective-permute-start | bytes 589832 | tf_op jit(solution)/shard_map/ppermute | solution.py:654
  106.6 9.8 %collective-permute-start.2 = (bf16[4,48,128]{2,1,0:T(8,128)(2,1)}, bf16[4,48,128]{2,1,0:T(8,128)(2,1)S(1)}, u32[]{:S(2)}, u32[]{:S(2)}) collective-permute-start(bf16[4,48,128]{2,1,0:T(8,128)(2,1)} %get-tuple-element.18), channel_id=1, source_target_pairs={{0,17},{1,18},{2,19},{3,20},{4,21},{5,22},{6,23},{7,24},{8,25},{9,... | collective-permute-start | bytes 147464 | tf_op jit(solution)/shard_map/ppermute | solution.py:654

commit v12 on v10

--- a/solution.py
+++ b/solution.py
@@ -102,6 +102,8 @@
 F32 = jnp.float32
 WIDE = SIDE + 128
 TALL = SIDE + HALO
+REACH = 42
+PACKS = 3
 
 
 def rounded(table):
@@ -139,8 +141,11 @@
 def tables():
     full = composite_tables()
     wide = np.concatenate([full, np.zeros((BASES, SIDE, 128 - HALO), np.float32)], axis=2)
+    assert not np.any(full[:, :, SIDE + REACH :])
     spread = wide.copy()
-    spread[:, :, TALL + 16 : TALL + 16 + HALO] = full[:, :, SIDE:]
+    for m in range(1, 3):
+        at = SIDE + m * REACH
+        spread[:, :, at : at + REACH] = full[:, :, SIDE : SIDE + REACH]
     out = {"rows": full, "columns": wide, "spread": spread}
     grid = np.arange(SIDE)[:, None] * np.arange(SIDE)[None, :] % SIDE
     angle = grid * (2.0 * math.pi / SIDE)
@@ -241,7 +246,7 @@
 START = [[coded(place, r, 0) for place in range(len(PLACES))] for r in range(2)]
 ONWARD = [coded(*hop) for hop in IN_ORDER]
 assert len(IN_ORDER) == sum(len(p) - 1 for r in range(2) for p in PATHS[r])
-assert len(IN_ORDER) - FIRST[-2] >= CH
+assert len(IN_ORDER) - FIRST[-2] > CH // 2
 
 
 def choose(j, values):
@@ -249,6 +254,15 @@
     for i, value in enumerate(values):
         out = jnp.where(j == i, jnp.int32(value), out)
     return out
+
+
+def three_beside(first, second, third):
+    lane = lax.broadcasted_iota(jnp.int32, first.shape, len(first.shape) - 1)
+    return jnp.where(lane < REACH, first, jnp.where(lane < 2 * REACH, second, third))
+
+
+def turned(values, m):
+    return pltpu.roll(values, 128 - m * REACH, 1) if m else values
 
 
 def dot(a, b):
@@ -261,12 +275,15 @@
     dest_ref,
     chan_ref,
     count_ref,
+    fourier_hbm,
+    back_hbm,
+    excess_hbm,
+    sky_hbm,
+    vis_hbm,
+    extended,
     fourier,
     back,
     excess,
-    sky_hbm,
-    vis_hbm,
-    extended,
     vis,
     sky,
     model,
@@ -308,6 +325,12 @@
     load_vis = pltpu.make_async_copy(vis_hbm, vis, load_sem.at[0])
     load_sky = pltpu.make_async_copy(sky_hbm, sky, load_sem.at[1])
     load_vis.start()
+    load_fourier = pltpu.make_async_copy(fourier_hbm, fourier, load_sem.at[2])
+    load_back = pltpu.make_async_copy(back_hbm, back, load_sem.at[3])
+    load_excess = pltpu.make_async_copy(excess_hbm, excess, load_sem.at[4])
+    load_fourier.start()
+    load_back.start()
+    load_excess.start()
     load_sky.start()
 
     barrier = pltpu.get_barrier_semaphore()
@@ -395,6 +418,8 @@
             total = total + jnp.where((row == r) & (lane == chan), weight, 0.0)
         return total
 
+    load_fourier.wait()
+    load_back.wait()
     load_vis.wait()
 
     def planes(slots):
@@ -429,12 +454,15 @@
     lax.fori_loop(0, len(PLACES), send_tiles, 0)
 
     load_sky.wait()
-
-    def there_and_back(c, carry):
-        pixels = sky[c].astype(BF)
+    load_excess.wait()
+
+    def there_and_back(c):
+        pixels = jnp.concatenate([sky[c].astype(BF), sky[c + 1].astype(BF)], axis=1)
         once = pixels.astype(F32) + dot(excess[...], pixels)
-        model[c] = once + dot(once.astype(BF), excess[...])
-        return carry
+        once = jnp.concatenate([once[:, :SIDE], once[:, SIDE:]], axis=0)
+        both = once + dot(once.astype(BF), excess[...])
+        model[c] = both[:SIDE]
+        model[c + 1] = both[SIDE:]
 
     def forward_and_work(j, carry):
         forward(FIRST[-2] + j, 0)
@@ -445,9 +473,9 @@
             shares[0] = share_rows(own)
             arrived[0], arrived[1] = planes(own)
 
-        @pl.when(j < CH)
+        @pl.when((j >= 1) & (j <= CH // 2))
         def _():
-            there_and_back(j, 0)
+            there_and_back(2 * (j - 1))
 
         return carry
 
@@ -515,12 +543,12 @@
 
     def combine(g):
         rows = group_rows(g)
-        new = with_sources(g, 12, 16).reshape(CH // 2, 2, 16, SIDE)
-        extended[:, rows, :SIDE] = new.reshape(CH, 16, SIDE).astype(BF)
-        low = lax.broadcasted_iota(jnp.int32, (CH // 2, 16, 128), 2) < 64
-        second = pltpu.roll(new[:, 1, :, :128].reshape(CH // 2 * 16, 128), 64, 1)
-        pair = jnp.where(low, new[:, 0, :, :128], second.reshape(CH // 2, 16, 128))
-        columns[:, rows, :] = pair.astype(BF)
+        new = with_sources(g, 12, 16).reshape(CH, 16, SIDE)
+        extended[:, rows, :SIDE] = new.astype(BF)
+        for k in range(PACKS):
+            parts = [new[min(3 * k + m, CH - 1), :, :128] for m in range(3)]
+            parts = [pltpu.roll(part, m * REACH, 1) if m else part for m, part in enumerate(parts)]
+            columns[k, rows, :] = three_beside(*parts).astype(BF)
 
     chunks = 4
     deep = SIDE // chunks
@@ -564,10 +592,9 @@
     lax.fori_loop(0, chunks, make_chunk, 0)
 
     def place(source, begin, end):
-        for p in range(CH // 2):
-            first = source[p]
-            extended[2 * p, begin:end, SIDE:] = first
-            extended[2 * p + 1, begin:end, SIDE:] = pltpu.roll(first.astype(F32), 64, 1).astype(BF)
+        for c in range(CH):
+            values = turned(source[c // 3].astype(F32), c % 3)
+            extended[c, begin:end, SIDE:] = values.astype(BF)
 
     halo_copy(1).wait_recv()
     place(corner, SIDE, TALL)
@@ -607,20 +634,16 @@
     return lax.ppermute(value, axes if len(axes) > 1 else axes[0], pairs)
 
 
-def first_half(shape):
-    return lax.broadcasted_iota(jnp.int32, shape, len(shape) - 1) < 64
-
-
 def pack_kernel(cells, right, corner, below, side, bottom, sem):
     load_side = pltpu.make_async_copy(cells.at[:, :, SIDE:], side, sem.at[0])
     load_bottom = pltpu.make_async_copy(cells.at[:, SIDE:, :SIDE], bottom, sem.at[1])
     load_side.start()
     load_bottom.start()
     load_side.wait()
-    for p in range(CH // 2):
-        both = jnp.where(first_half((TALL, 128)), side[2 * p], side[2 * p + 1]).astype(BF)
-        right[p] = both[:SIDE]
-        corner[p] = both[SIDE:]
+    for k in range(PACKS):
+        packed = three_beside(*[side[min(3 * k + m, CH - 1)] for m in range(3)]).astype(BF)
+        right[k] = packed[:SIDE]
+        corner[k] = packed[SIDE:]
     load_bottom.wait()
     below[...] = bottom[...].astype(BF)
 
@@ -628,18 +651,21 @@
 def add_kernel(cells, left, above, corner, out):
     for h in range(2):
 
-        def columns(pairs):
-            pairs = pairs.astype(F32)
-            if h == 1:
-                pairs = pltpu.roll(pairs, 64, 1)
-            return jnp.where(first_half(pairs.shape), pairs, 0.0)
+        channel = 2 * pl.program_id(0) + h
+
+        def columns(packed):
+            values = packed[channel // 3].astype(F32)
+            for m in range(1, 3):
+                values = jnp.where(channel % 3 == m, turned(packed[channel // 3].astype(F32), m), values)
+            lane = lax.broadcasted_iota(jnp.int32, values.shape, 1)
+            return jnp.where(lane < REACH, values, 0.0)
 
         def finished(total):
             return jnp.maximum(total * (1.0 / BASES), 0.0)
 
-        from_left = columns(left[0])
+        from_left = columns(left)
         from_above = above[h].astype(F32)
-        first = from_left[:HALO] + from_above[:, :128] + columns(corner[0])
+        first = from_left[:HALO] + from_above[:, :128] + columns(corner)
         out[h, :HALO, :128] = finished(cells[h, :HALO, :128] + first)
         out[h, :HALO, 128:] = finished(cells[h, :HALO, 128:] + from_above[:, 128:])
         out[h, HALO:, :128] = finished(cells[h, HALO:, :128] + from_left[HALO:])
@@ -656,8 +682,11 @@
     extended = pl.pallas_call(
         functools.partial(exchange_kernel, n_fy, n_fx),
         out_shape=pltpu.VMEM((CH, TALL, WIDE), BF),
-        in_specs=[smem] * 3 + [vmem] * 3 + [anywhere] * 2,
+        in_specs=[smem] * 3 + [anywhere] * 5,
         scratch_shapes=[
+            pltpu.VMEM((2 * SIDE, 2 * SIDE), BF),
+            pltpu.VMEM((SIDE, 2 * SIDE), BF),
+            pltpu.VMEM((SIDE, SIDE), BF),
             pltpu.VMEM((tiles, 2, SIDE, SIDE), BF),
             pltpu.VMEM((CH, SIDE, SIDE), F32),
             pltpu.VMEM((CH, SIDE, SIDE), F32),
@@ -669,10 +698,10 @@
             pltpu.VMEM((n_fx, 8, 128), F32),
             pltpu.VMEM((n_fx, 8, 128), F32),
             pltpu.VMEM((CH * 16, n_fx * 32), BF),
-            pltpu.VMEM((CH // 2, SIDE, 128), BF),
-            pltpu.VMEM((CH // 2, SIDE, 128), BF),
-            pltpu.VMEM((CH // 2, HALO, 128), BF),
-            dma((2,)),
+            pltpu.VMEM((PACKS, SIDE, 128), BF),
+            pltpu.VMEM((PACKS, SIDE, 128), BF),
+            pltpu.VMEM((PACKS, HALO, 128), BF),
+            dma((5,)),
             dma((2 * len(PLACES),)),
             dma((2 * n_fx,)),
             dma((len(IN_ORDER),)),
@@ -707,11 +736,11 @@
     right, corner, below = pl.pallas_call(
         pack_kernel,
         out_shape=(
-            jax.ShapeDtypeStruct((CH // 2, SIDE, 128), BF),
-            jax.ShapeDtypeStruct((CH // 2, HALO, 128), BF),
+            jax.ShapeDtypeStruct((PACKS, SIDE, 128), BF),
+            jax.ShapeDtypeStruct((PACKS, HALO, 128), BF),
             jax.ShapeDtypeStruct((CH, HALO, SIDE), BF),
         ),
-        in_specs=[pl.BlockSpec(memory_space=pltpu.HBM)],
+        in_specs=[anywhere],
         out_specs=[vmem] * 3,
         scratch_shapes=[
             pltpu.VMEM((CH, TALL, 128), F32),
@@ -729,9 +758,9 @@
         grid=(CH // 2,),
         in_specs=[
             pl.BlockSpec((2, SIDE, SIDE), lambda p: (p, 0, 0)),
-            pl.BlockSpec((1, SIDE, 128), lambda p: (p, 0, 0)),
+            pl.BlockSpec((PACKS, SIDE, 128), lambda p: (0, 0, 0)),
             pl.BlockSpec((2, HALO, SIDE), lambda p: (p, 0, 0)),
-            pl.BlockSpec((1, HALO, 128), lambda p: (p, 0, 0)),
+            pl.BlockSpec((PACKS, HALO, 128), lambda p: (0, 0, 0)),
         ],
         out_specs=pl.BlockSpec((2, SIDE, SIDE), lambda p: (p, 0, 0)),
         compiler_params=pltpu.CompilerParams(vmem_limit_bytes=16 * 1024 * 1024),

time: 113 us -> 111 us (0.982)
  no operation moved by 1% of the time
where the time goes in v12:
time: 111 us
  Pallas kernels  68.6 us (62%)
  matrix products  29.2 us (26%)
  waiting for transfers between devices  8.07 us (7%)
  starting transfers between devices  3.03 us (3%)
  local copies, waits for them, and re-layouts  2.06 us (2%)
    pallas_call x1, Pallas kernels, per_device(): pl.pallas_call(functools.partial(exchange_kernel, n_fy, n_fx), out_shape=...  66.1 us
    dot_general x1, matrix products, per_device(): jnp.einsum('bcyx,bkx->bcyk', row_sec, columns, preferred_element_type=F32)  16.9 us
    dot_general x1, matrix products, per_device(): jnp.einsum('bcyk,bkx->cyx', row_sec, made['spread'], preferred_element_ty...  12.3 us
    ppermute x3, waiting for transfers between devices, passed(): return lax.ppermute(value, axes if len(axes) > 1 else axes[0], pairs)  8.07 us
    ppermute x3, starting transfers between devices, passed(): return lax.ppermute(value, axes if len(axes) > 1 else axes[0], pairs)  3.03 us
    pallas_call x1, Pallas kernels, per_device(): pl.pallas_call(add_kernel, out_shape=jax.ShapeDtypeStruct((CH, SIDE, SIDE...  2.33 us
  transfers between devices with their start and end apart: 3, of which 1 were waited for; matrix products, arithmetic and copies ran while one was open for 0% of the time, Pallas kernels for 0%

profile of v12, /device:TPU:1, one launch (start us, length us, event | category | flops | bytes accessed | tf_op | source)
XLA Modules:
  0.0 111.0 jit_solution(13609440282658603080)
XLA Ops:
  0.0 66.1 %shard_map.118 = bf16[8,304,384]{2,1,0:T(8,128)(2,1)S(1)} custom-call(s32[16]{0:T(128)} %bitcast.29, s32[16]{0:T(128)} %chan_ref.1, s32[16]{0:T(128)} %count_ref.1, bf16[512,512]{1,0:T(8,128)(2,1)} %constant.15.clone.fourier_hbm, bf16[256,512]{1,0:T(8,128)(2,1)} %constant.16.clone.back_hbm, bf16[256,256]{1,0:T(8,128)(2,1)} %constant.17.clone.excess_hbm, ...), custom_call_target="tpu_custom_call" | custom-call | tf_op jit(solution)/shard_map/pallas_call | solution.py:682
  66.1 0.0 copy-start.1
  66.1 16.9 %fusion.2 = bf16[8,8,256,256]{3,2,1,0:T(8,128)(2,1)} fusion(bf16[8,8,256,256]{3,2,1,0:T(8,128)(2,1)} %param.17, bf16[8,256,384,1]{2,1,3,0:T(8,128)(2,1)} %constant.23, bf16[8,256,304,1]{2,1,3,0:T(8,128)(2,1)} %constant.22, bf16[8,304,384]{2,1,0:T(8,128)(2,1)S(1)} %shard_map.118), kind=kOutput, calls=%fused_computation.4 | convolution fusion | flops 7077888000 | bytes 21463040 | tf_op jit(solution)/shard_map/bcyx,bkx->bcyk/dot_general | solution.py:731
  83.0 0.0 copy-done.1
  83.0 12.3 %fusion.19.cells = f32[8,304,384]{2,1,0:T(8,128)} fusion(bf16[8,256,384,1]{2,1,0,3:T(8,128)(2,1)S(1)} %copy-done.1, bf16[8,256,304,1]{2,1,0,3:T(8,128)(2,1)} %constant.24, bf16[8,8,256,256]{3,2,1,0:T(8,128)(2,1)} %fusion.2), kind=kOutput, calls=%fused_computation.14 | convolution fusion | flops 6380322816 | bytes 14942208 | tf_op jit(solution)/shard_map/bcyk,bkx->cyx/dot_general | solution.py:735
  95.3 0.0 copy-start
  95.3 2.1 %copy-done = f32[8,304,384]{2,1,0:T(8,128)S(1)} copy-done((f32[8,304,384]{2,1,0:T(8,128)S(1)}, f32[8,304,384]{2,1,0:T(8,128)}, u32[]{:S(2)}) %copy-start) | copy-done | bytes 3735576
  97.4 0.2 shard_map.119
  97.6 1.1 %collective-permute-start = (bf16[3,256,128]{2,1,0:T(8,128)(2,1)S(1)}, bf16[3,256,128]{2,1,0:T(8,128)(2,1)S(1)}, u32[]{:S(2)}, u32[]{:S(2)}) collective-permute-start(bf16[3,256,128]{2,1,0:T(8,128)(2,1)S(1)} %get-tuple-element.8), channel_id=1, source_target_pairs={{0,1},{1,2},{2,3},{3,4},{4,5},{5,6},{6,7},{7,8},{8,9},{9,10},{10,1... | collective-permute-start | bytes 589832 | tf_op jit(solution)/shard_map/ppermute | solution.py:634
  98.7 0.4 collective-permute-start.1
  99.1 1.5 %collective-permute-start.2 = (bf16[3,48,128]{2,1,0:T(8,128)(2,1)S(1)}, bf16[3,48,128]{2,1,0:T(8,128)(2,1)S(1)}, u32[]{:S(2)}, u32[]{:S(2)}) collective-permute-start(bf16[3,48,128]{2,1,0:T(8,128)(2,1)S(1)} %get-tuple-element.10), channel_id=1, source_target_pairs={{0,17},{1,18},{2,19},{3,20},{4,21},{5,22},{6,23},{7,24},{8,25},{9,... | collective-permute-start | bytes 110600 | tf_op jit(solution)/shard_map/ppermute | solution.py:634
  100.6 8.1 %collective-permute-done.2.corner = bf16[3,48,128]{2,1,0:T(8,128)(2,1)S(1)} collective-permute-done((bf16[3,48,128]{2,1,0:T(8,128)(2,1)S(1)}, bf16[3,48,128]{2,1,0:T(8,128)(2,1)S(1)}, u32[]{:S(2)}, u32[]{:S(2)}) %collective-permute-start.2) | collective-permute-done | bytes 36896 | tf_op jit(solution)/shard_map/ppermute | solution.py:634
  108.7 0.0 collective-permute-done.left
  108.7 0.0 collective-permute-done.1.above
  108.7 2.3 %shard_map.120 = f32[8,256,256]{2,1,0:T(8,128)} custom-call(f32[8,304,384]{2,1,0:T(8,128)S(1)} %copy-done, bf16[3,256,128]{2,1,0:T(8,128)(2,1)S(1)} %collective-permute-done.left, bf16[8,48,256]{2,1,0:T(8,128)(2,1)S(1)} %collective-permute-done.1.above, bf16[3,48,128]{2,1,0:T(8,128)(2,1)S(1)} %collective-permute-done.2.corner), custom_call_target="tpu_custom_call" | custom-call | tf_op jit(solution)/shard_map/pallas_call | solution.py:755
Async XLA Ops:
  66.1 16.9 %copy-start.1 = (bf16[8,256,384,1]{2,1,0,3:T(8,128)(2,1)S(1)}, bf16[8,256,384,1]{2,1,0,3:T(8,128)(2,1)}, u32[]{:S(2)}) copy-start(bf16[8,256,384,1]{2,1,0,3:T(8,128)(2,1)} %constant.25) | copy-start | bytes 4718596
  95.3 2.1 %copy-start = (f32[8,304,384]{2,1,0:T(8,128)S(1)}, f32[8,304,384]{2,1,0:T(8,128)}, u32[]{:S(2)}) copy-start(f32[8,304,384]{2,1,0:T(8,128)} %fusion.19.cells) | copy-start | bytes 11206660
  97.6 11.1 %collective-permute-start = (bf16[3,256,128]{2,1,0:T(8,128)(2,1)S(1)}, bf16[3,256,128]{2,1,0:T(8,128)(2,1)S(1)}, u32[]{:S(2)}, u32[]{:S(2)}) collective-permute-start(bf16[3,256,128]{2,1,0:T(8,128)(2,1)S(1)} %get-tuple-element.8), channel_id=1, source_target_pairs={{0,1},{1,2},{2,3},{3,4},{4,5},{5,6},{6,7},{7,8},{8,9},{9,10},{10,1... | collective-permute-start | bytes 589832 | tf_op jit(solution)/shard_map/ppermute | solution.py:634
  98.7 10.0 %collective-permute-start.1 = (bf16[8,48,256]{2,1,0:T(8,128)(2,1)S(1)}, bf16[8,48,256]{2,1,0:T(8,128)(2,1)S(1)}, u32[]{:S(2)}, u32[]{:S(2)}) collective-permute-start(bf16[8,48,256]{2,1,0:T(8,128)(2,1)S(1)} %get-tuple-element.9), channel_id=1, source_target_pairs={{0,16},{16,32},{32,48},{48,64},{64,80},{80,96},{96,112},{112,0},{1... | collective-permute-start | bytes 589832 | tf_op jit(solution)/shard_map/ppermute | solution.py:634
  99.1 9.5 %collective-permute-start.2 = (bf16[3,48,128]{2,1,0:T(8,128)(2,1)S(1)}, bf16[3,48,128]{2,1,0:T(8,128)(2,1)S(1)}, u32[]{:S(2)}, u32[]{:S(2)}) collective-permute-start(bf16[3,48,128]{2,1,0:T(8,128)(2,1)S(1)} %get-tuple-element.10), channel_id=1, source_target_pairs={{0,17},{1,18},{2,19},{3,20},{4,21},{5,22},{6,23},{7,24},{8,25},{9,... | collective-permute-start | bytes 110600 | tf_op jit(solution)/shard_map/ppermute | solution.py:634

commit v13 on v12

--- a/solution.py
+++ b/solution.py
@@ -625,27 +625,63 @@
         columns_copy(q).wait_send()
 
 
-def passed(value, axes, to):
-    sizes = [lax.axis_size(a) for a in axes]
-    pairs = []
-    for i in np.ndindex(*sizes):
-        j = [(a + b) % n for a, b, n in zip(i, to, sizes)]
-        pairs.append((int(np.ravel_multi_index(i, sizes)), int(np.ravel_multi_index(j, sizes))))
-    return lax.ppermute(value, axes if len(axes) > 1 else axes[0], pairs)
-
-
-def pack_kernel(cells, right, corner, below, side, bottom, sem):
-    load_side = pltpu.make_async_copy(cells.at[:, :, SIDE:], side, sem.at[0])
-    load_bottom = pltpu.make_async_copy(cells.at[:, SIDE:, :SIDE], bottom, sem.at[1])
+def spill_kernel(
+    n_fy,
+    n_fx,
+    cells,
+    left,
+    above,
+    corner,
+    side,
+    bottom,
+    to_right,
+    to_below,
+    to_corner,
+    load_sem,
+    send_sem,
+    recv_sem,
+):
+    load_side = pltpu.make_async_copy(cells.at[:, :, SIDE:], side, load_sem.at[0])
+    load_bottom = pltpu.make_async_copy(cells.at[:, SIDE:, :SIDE], bottom, load_sem.at[1])
     load_side.start()
     load_bottom.start()
+    fy = lax.axis_index("fy")
+    fx = lax.axis_index("fx")
+    up, down = (fy + n_fy - 1) % n_fy, (fy + 1) % n_fy
+    prev, nxt = (fx + n_fx - 1) % n_fx, (fx + 1) % n_fx
+    barrier = pltpu.get_barrier_semaphore()
+    for where in (
+        {"fy": up},
+        {"fy": down},
+        {"fx": prev},
+        {"fx": nxt},
+        {"fy": up, "fx": prev},
+        {"fy": down, "fx": nxt},
+    ):
+        pl.semaphore_signal(barrier, inc=1, device_id=where, device_id_type=pl.DeviceIdType.MESH)
     load_side.wait()
     for k in range(PACKS):
         packed = three_beside(*[side[min(3 * k + m, CH - 1)] for m in range(3)]).astype(BF)
-        right[k] = packed[:SIDE]
-        corner[k] = packed[SIDE:]
+        to_right[k] = packed[:SIDE]
+        to_corner[k] = packed[SIDE:]
     load_bottom.wait()
-    below[...] = bottom[...].astype(BF)
+    to_below[...] = bottom[...].astype(BF)
+    pl.semaphore_wait(barrier, 6)
+
+    def spill_copy(i):
+        return pltpu.make_async_remote_copy(
+            src_ref=(to_right, to_below, to_corner)[i],
+            dst_ref=(left, above, corner)[i],
+            send_sem=send_sem.at[i],
+            recv_sem=recv_sem.at[i],
+            device_id=({"fx": nxt}, {"fy": down}, {"fy": down, "fx": nxt})[i],
+            device_id_type=pl.DeviceIdType.MESH,
+        )
+
+    for i in range(3):
+        spill_copy(i).start()
+    for i in range(3):
+        spill_copy(i).wait()
 
 
 def add_kernel(cells, left, above, corner, out):
@@ -733,25 +769,29 @@
     shrunk = (coefficient - jnp.clip(coefficient, -limits, limits)).astype(BF)
     row_sec = jnp.einsum("bjy,bcjk->bcyk", rows, shrunk, preferred_element_type=F32).astype(BF)
     cells = jnp.einsum("bcyk,bkx->cyx", row_sec, made["spread"], preferred_element_type=F32)
-    right, corner, below = pl.pallas_call(
-        pack_kernel,
+    left, above, corner = pl.pallas_call(
+        functools.partial(spill_kernel, n_fy, n_fx),
         out_shape=(
             jax.ShapeDtypeStruct((PACKS, SIDE, 128), BF),
+            jax.ShapeDtypeStruct((CH, HALO, SIDE), BF),
             jax.ShapeDtypeStruct((PACKS, HALO, 128), BF),
-            jax.ShapeDtypeStruct((CH, HALO, SIDE), BF),
         ),
         in_specs=[anywhere],
         out_specs=[vmem] * 3,
         scratch_shapes=[
             pltpu.VMEM((CH, TALL, 128), F32),
             pltpu.VMEM((CH, HALO, SIDE), F32),
+            pltpu.VMEM((PACKS, SIDE, 128), BF),
+            pltpu.VMEM((CH, HALO, SIDE), BF),
+            pltpu.VMEM((PACKS, HALO, 128), BF),
             dma((2,)),
+            dma((3,)),
+            dma((3,)),
         ],
-        compiler_params=pltpu.CompilerParams(vmem_limit_bytes=16 * 1024 * 1024),
+        compiler_params=pltpu.CompilerParams(
+            collective_id=1, has_side_effects=True, vmem_limit_bytes=58 * 1024 * 1024
+        ),
     )(cells)
-    left = passed(right, ("fx",), (1,))
-    above = passed(below, ("fy",), (1,))
-    corner = passed(corner, ("fy", "fx"), (1, 1))
     return pl.pallas_call(
         add_kernel,
         out_shape=jax.ShapeDtypeStruct((CH, SIDE, SIDE), F32),

time: 111 us -> 113 us (1.018)
  Pallas kernels: 68.6 us -> 80.6 us
  waiting for transfers between devices: 8.07 us -> 0 us
  starting transfers between devices: 3.03 us -> 0 us
    pallas_call x1, Pallas kernels: 0.2 us -> 12.2 us  [per_device(): pl.pallas_call(functools.partial(spill_kernel, n_fy, n_fx), out_shape=(ja...]
    ppermute x3 -> x0, waiting for transfers between devices: 8.07 us -> none  [passed(): return lax.ppermute(value, axes if len(axes) > 1 else axes[0], pairs)]
    ppermute x3 -> x0, starting transfers between devices: 3.03 us -> none  [passed(): return lax.ppermute(value, axes if len(axes) > 1 else axes[0], pairs)]
    unnamed x4 -> x10, local copies, waits for them, and re-layouts: 2.06 us -> 2.62 us
  transfers between devices with their start and end apart: 3 -> 0, of which waited for: 1 -> 0; matrix products, arithmetic and copies ran while one was open for 0% -> 0% of each run, Pallas kernels for 0% -> 0%
where the time goes in v13:
time: 113 us
  Pallas kernels  80.6 us (71%)
  matrix products  29.2 us (26%)
  local copies, waits for them, and re-layouts  2.62 us (2%)
    pallas_call x1, Pallas kernels, per_device(): pl.pallas_call(functools.partial(exchange_kernel, n_fy, n_fx), out_shape=...  66.1 us
    dot_general x1, matrix products, per_device(): jnp.einsum('bcyx,bkx->bcyk', row_sec, columns, preferred_element_type=F32)  16.9 us
    dot_general x1, matrix products, per_device(): jnp.einsum('bcyk,bkx->cyx', row_sec, made['spread'], preferred_element_ty...  12.3 us
    pallas_call x1, Pallas kernels, per_device(): pl.pallas_call(functools.partial(spill_kernel, n_fy, n_fx), out_shape=(ja...  12.2 us
    unnamed x10, local copies, waits for them, and re-layouts  2.62 us
    pallas_call x1, Pallas kernels, per_device(): pl.pallas_call(add_kernel, out_shape=jax.ShapeDtypeStruct((CH, SIDE, SIDE...  2.32 us

profile of v13, /device:TPU:1, one launch (start us, length us, event | category | flops | bytes accessed | tf_op | source)
XLA Modules:
  0.0 112.5 jit_solution(10294938048879790731)
XLA Ops:
  0.0 66.1 %shard_map.118 = bf16[8,304,384]{2,1,0:T(8,128)(2,1)S(1)} custom-call(s32[16]{0:T(128)} %bitcast.29, s32[16]{0:T(128)} %chan_ref.1, s32[16]{0:T(128)} %count_ref.1, bf16[512,512]{1,0:T(8,128)(2,1)} %constant.15.clone.fourier_hbm, bf16[256,512]{1,0:T(8,128)(2,1)} %constant.16.clone.back_hbm, bf16[256,256]{1,0:T(8,128)(2,1)} %constant.17.clone.excess_hbm, ...), custom_call_target="tpu_custom_call" | custom-call | tf_op jit(solution)/shard_map/pallas_call | solution.py:718
  66.1 0.0 copy-start.4
  66.1 16.9 %fusion.2 = bf16[8,8,256,256]{3,2,1,0:T(8,128)(2,1)} fusion(bf16[8,8,256,256]{3,2,1,0:T(8,128)(2,1)} %param.17, bf16[8,256,384,1]{2,1,3,0:T(8,128)(2,1)} %constant.23, bf16[8,256,304,1]{2,1,3,0:T(8,128)(2,1)} %constant.22, bf16[8,304,384]{2,1,0:T(8,128)(2,1)S(1)} %shard_map.118), kind=kOutput, calls=%fused_computation.4 | convolution fusion | flops 7077888000 | bytes 21463040 | tf_op jit(solution)/shard_map/bcyx,bkx->bcyk/dot_general | solution.py:767
  83.0 0.0 copy-done.4
  83.0 12.3 %fusion.19.cells = f32[8,304,384]{2,1,0:T(8,128)} fusion(bf16[8,256,384,1]{2,1,0,3:T(8,128)(2,1)S(1)} %copy-done.4, bf16[8,256,304,1]{2,1,0,3:T(8,128)(2,1)} %constant.24, bf16[8,8,256,256]{3,2,1,0:T(8,128)(2,1)} %fusion.2), kind=kOutput, calls=%fused_computation.14 | convolution fusion | flops 6380322816 | bytes 14942208 | tf_op jit(solution)/shard_map/bcyk,bkx->cyx/dot_general | solution.py:771
  95.3 0.0 copy-start
  95.3 12.2 %shard_map.119 = (bf16[3,256,128]{2,1,0:T(8,128)(2,1)}, bf16[8,48,256]{2,1,0:T(8,128)(2,1)}, bf16[3,48,128]{2,1,0:T(8,128)(2,1)}) custom-call(f32[8,304,384]{2,1,0:T(8,128)} %fusion.19.cells), custom_call_target="tpu_custom_call" | custom-call | tf_op jit(solution)/shard_map/pallas_call | solution.py:772
  107.6 0.0 copy-done
  107.6 0.0 copy-start.1
  107.6 0.9 copy-done.1
  108.5 0.0 copy-start.2
  108.5 0.9 copy-done.2
  109.4 0.0 copy-start.3
  109.4 0.8 copy-done.3
  110.2 2.3 %shard_map.120 = f32[8,256,256]{2,1,0:T(8,128)} custom-call(f32[8,304,384]{2,1,0:T(8,128)S(1)} %copy-done, bf16[3,256,128]{2,1,0:T(8,128)(2,1)S(1)} %copy-done.1, bf16[8,48,256]{2,1,0:T(8,128)(2,1)S(1)} %copy-done.2, bf16[3,48,128]{2,1,0:T(8,128)(2,1)S(1)} %copy-done.3), custom_call_target="tpu_custom_call" | custom-call | tf_op jit(solution)/shard_map/pallas_call | solution.py:795
Async XLA Ops:
  66.1 16.9 %copy-start.4 = (bf16[8,256,384,1]{2,1,0,3:T(8,128)(2,1)S(1)}, bf16[8,256,384,1]{2,1,0,3:T(8,128)(2,1)}, u32[]{:S(2)}) copy-start(bf16[8,256,384,1]{2,1,0,3:T(8,128)(2,1)} %constant.25) | copy-start | bytes 4718596
  95.3 12.3 %copy-start = (f32[8,304,384]{2,1,0:T(8,128)S(1)}, f32[8,304,384]{2,1,0:T(8,128)}, u32[]{:S(2)}) copy-start(f32[8,304,384]{2,1,0:T(8,128)} %fusion.19.cells) | copy-start | bytes 11206660
  107.6 0.9 copy-start.1
  108.5 0.9 copy-start.2
  109.4 0.8 copy-start.3

commit v14 on v13

--- a/solution.py
+++ b/solution.py
@@ -246,7 +246,8 @@
 START = [[coded(place, r, 0) for place in range(len(PLACES))] for r in range(2)]
 ONWARD = [coded(*hop) for hop in IN_ORDER]
 assert len(IN_ORDER) == sum(len(p) - 1 for r in range(2) for p in PATHS[r])
-assert len(IN_ORDER) - FIRST[-2] > CH // 2
+assert len(IN_ORDER) - 2 - FIRST[-2] > CH // 2
+assert all(RANK[place] >= 7 for place, _, _ in IN_ORDER[-2:])
 
 
 def choose(j, values):
@@ -479,7 +480,7 @@
 
         return carry
 
-    lax.fori_loop(0, len(IN_ORDER) - FIRST[-2], forward_and_work, 0)
+    lax.fori_loop(0, len(IN_ORDER) - 2 - FIRST[-2], forward_and_work, 0)
 
     def wait_share(i, carry):
         share_copy(i).wait_recv()
@@ -538,7 +539,12 @@
                 partial[q * 4 + i] = with_sources(q * 4 + i, first, last)
             return carry
 
-        lax.fori_loop(0, SIDE // 64, add_sources, 0)
+        if first == 0:
+            for k in range(2):
+                forward(jnp.int32(len(IN_ORDER) - 2 + k), 0)
+                lax.fori_loop(2 * k, 2 * k + 2, add_sources, 0)
+        else:
+            lax.fori_loop(0, SIDE // 64, add_sources, 0)
     lax.fori_loop(22, 2 * len(PLACES), wait_tiles, 0)
 
     def combine(g):
@@ -772,12 +778,11 @@
     left, above, corner = pl.pallas_call(
         functools.partial(spill_kernel, n_fy, n_fx),
         out_shape=(
-            jax.ShapeDtypeStruct((PACKS, SIDE, 128), BF),
-            jax.ShapeDtypeStruct((CH, HALO, SIDE), BF),
-            jax.ShapeDtypeStruct((PACKS, HALO, 128), BF),
+            pltpu.VMEM((PACKS, SIDE, 128), BF),
+            pltpu.VMEM((CH, HALO, SIDE), BF),
+            pltpu.VMEM((PACKS, HALO, 128), BF),
         ),
         in_specs=[anywhere],
-        out_specs=[vmem] * 3,
         scratch_shapes=[
             pltpu.VMEM((CH, TALL, 128), F32),
             pltpu.VMEM((CH, HALO, SIDE), F32),

time: 113 us -> 109 us (0.965)
  local copies, waits for them, and re-layouts: 2.62 us -> 0.01 us
    unnamed x10 -> x4, local copies, waits for them, and re-layouts: 2.62 us -> 0.01 us
where the time goes in v14:
time: 109 us
  Pallas kernels  79.9 us (73%)
  matrix products  29.2 us (27%)
    pallas_call x1, Pallas kernels, per_device(): pl.pallas_call(functools.partial(exchange_kernel, n_fy, n_fx), out_shape=...  66.1 us
    dot_general x1, matrix products, per_device(): jnp.einsum('bcyx,bkx->bcyk', row_sec, columns, preferred_element_type=F32)  16.9 us
    dot_general x1, matrix products, per_device(): jnp.einsum('bcyk,bkx->cyx', row_sec, made['spread'], preferred_element_ty...  12.3 us
    pallas_call x1, Pallas kernels, per_device(): pl.pallas_call(functools.partial(spill_kernel, n_fy, n_fx), out_shape=(pl...  11.5 us
    pallas_call x1, Pallas kernels, per_device(): pl.pallas_call(add_kernel, out_shape=jax.ShapeDtypeStruct((CH, SIDE, SIDE...  2.33 us

profile of v14, /device:TPU:1, one launch (start us, length us, event | category | flops | bytes accessed | tf_op | source)
XLA Modules:
  0.0 109.1 jit_solution(7521574139843960614)
XLA Ops:
  0.0 66.1 %shard_map.118 = bf16[8,304,384]{2,1,0:T(8,128)(2,1)S(1)} custom-call(s32[16]{0:T(128)} %bitcast.29, s32[16]{0:T(128)} %chan_ref.1, s32[16]{0:T(128)} %count_ref.1, bf16[512,512]{1,0:T(8,128)(2,1)} %constant.15.clone.fourier_hbm, bf16[256,512]{1,0:T(8,128)(2,1)} %constant.16.clone.back_hbm, bf16[256,256]{1,0:T(8,128)(2,1)} %constant.17.clone.excess_hbm, ...), custom_call_target="tpu_custom_call" | custom-call | tf_op jit(solution)/shard_map/pallas_call | solution.py:724
  66.1 0.0 copy-start.1
  66.1 16.9 %fusion.2 = bf16[8,8,256,256]{3,2,1,0:T(8,128)(2,1)} fusion(bf16[8,8,256,256]{3,2,1,0:T(8,128)(2,1)} %param.17, bf16[8,256,384,1]{2,1,3,0:T(8,128)(2,1)} %constant.23, bf16[8,256,304,1]{2,1,3,0:T(8,128)(2,1)} %constant.22, bf16[8,304,384]{2,1,0:T(8,128)(2,1)S(1)} %shard_map.118), kind=kOutput, calls=%fused_computation.4 | convolution fusion | flops 7077888000 | bytes 21463040 | tf_op jit(solution)/shard_map/bcyx,bkx->bcyk/dot_general | solution.py:773
  83.0 0.0 copy-done.1
  83.0 12.3 %fusion.19.cells = f32[8,304,384]{2,1,0:T(8,128)} fusion(bf16[8,256,384,1]{2,1,0,3:T(8,128)(2,1)S(1)} %copy-done.1, bf16[8,256,304,1]{2,1,0,3:T(8,128)(2,1)} %constant.24, bf16[8,8,256,256]{3,2,1,0:T(8,128)(2,1)} %fusion.2), kind=kOutput, calls=%fused_computation.14 | convolution fusion | flops 6380322816 | bytes 14942208 | tf_op jit(solution)/shard_map/bcyk,bkx->cyx/dot_general | solution.py:777
  95.3 0.0 copy-start
  95.3 11.5 %shard_map.119 = (bf16[3,256,128]{2,1,0:T(8,128)(2,1)S(1)}, bf16[8,48,256]{2,1,0:T(8,128)(2,1)S(1)}, bf16[3,48,128]{2,1,0:T(8,128)(2,1)S(1)}) custom-call(f32[8,304,384]{2,1,0:T(8,128)} %fusion.19.cells), custom_call_target="tpu_custom_call" | custom-call | tf_op jit(solution)/shard_map/pallas_call | solution.py:778
  106.8 0.0 copy-done
  106.8 2.3 %shard_map.120 = f32[8,256,256]{2,1,0:T(8,128)} custom-call(f32[8,304,384]{2,1,0:T(8,128)S(1)} %copy-done, bf16[3,256,128]{2,1,0:T(8,128)(2,1)S(1)} %get-tuple-element.8.left, bf16[8,48,256]{2,1,0:T(8,128)(2,1)S(1)} %get-tuple-element.9.above, bf16[3,48,128]{2,1,0:T(8,128)(2,1)S(1)} %get-tuple-element.10.corner), custom_call_target="tpu_custom_call" | custom-call | tf_op jit(solution)/shard_map/pallas_call | solution.py:800
Async XLA Ops:
  66.1 16.9 %copy-start.1 = (bf16[8,256,384,1]{2,1,0,3:T(8,128)(2,1)S(1)}, bf16[8,256,384,1]{2,1,0,3:T(8,128)(2,1)}, u32[]{:S(2)}) copy-start(bf16[8,256,384,1]{2,1,0,3:T(8,128)(2,1)} %constant.25) | copy-start | bytes 4718596
  95.3 11.5 %copy-start = (f32[8,304,384]{2,1,0:T(8,128)S(1)}, f32[8,304,384]{2,1,0:T(8,128)}, u32[]{:S(2)}) copy-start(f32[8,304,384]{2,1,0:T(8,128)} %fusion.19.cells) | copy-start | bytes 11206660

commit v15 on v14

--- a/solution.py
+++ b/solution.py
@@ -556,7 +556,7 @@
             parts = [pltpu.roll(part, m * REACH, 1) if m else part for m, part in enumerate(parts)]
             columns[k, rows, :] = three_beside(*parts).astype(BF)
 
-    chunks = 4
+    chunks = 8
     deep = SIDE // chunks
 
     def columns_copy(q):
@@ -588,7 +588,7 @@
             combine(q * (deep // 16) + i)
         columns_copy(q).start()
 
-        @pl.when(q == 0)
+        @pl.when(q == (HALO - 1) // deep)
         def _():
             for i in range(2):
                 halo_copy(i).start()
@@ -647,9 +647,14 @@
     send_sem,
     recv_sem,
 ):
-    load_side = pltpu.make_async_copy(cells.at[:, :, SIDE:], side, load_sem.at[0])
-    load_bottom = pltpu.make_async_copy(cells.at[:, SIDE:, :SIDE], bottom, load_sem.at[1])
-    load_side.start()
+    threes = [(3 * k, min(3 * k + 3, CH)) for k in range(PACKS)]
+    loads = [
+        pltpu.make_async_copy(cells.at[a:e, :, SIDE:], side.at[a:e], load_sem.at[k])
+        for k, (a, e) in enumerate(threes)
+    ]
+    load_bottom = pltpu.make_async_copy(cells.at[:, SIDE:, :SIDE], bottom, load_sem.at[PACKS])
+    for load in loads:
+        load.start()
     load_bottom.start()
     fy = lax.axis_index("fy")
     fx = lax.axis_index("fx")
@@ -665,35 +670,40 @@
         {"fy": down, "fx": nxt},
     ):
         pl.semaphore_signal(barrier, inc=1, device_id=where, device_id_type=pl.DeviceIdType.MESH)
-    load_side.wait()
+    pl.semaphore_wait(barrier, 6)
+
+    def spill_copy(source, target, where, sem):
+        return pltpu.make_async_remote_copy(
+            src_ref=source,
+            dst_ref=target,
+            send_sem=send_sem.at[sem],
+            recv_sem=recv_sem.at[sem],
+            device_id=where,
+            device_id_type=pl.DeviceIdType.MESH,
+        )
+
+    copies = []
     for k in range(PACKS):
+        loads[k].wait()
         packed = three_beside(*[side[min(3 * k + m, CH - 1)] for m in range(3)]).astype(BF)
         to_right[k] = packed[:SIDE]
         to_corner[k] = packed[SIDE:]
+        copies.append(spill_copy(to_right.at[k], left.at[k], {"fx": nxt}, k))
+        copies[-1].start()
+    copies.append(spill_copy(to_corner, corner, {"fy": down, "fx": nxt}, PACKS))
+    copies[-1].start()
     load_bottom.wait()
     to_below[...] = bottom[...].astype(BF)
-    pl.semaphore_wait(barrier, 6)
-
-    def spill_copy(i):
-        return pltpu.make_async_remote_copy(
-            src_ref=(to_right, to_below, to_corner)[i],
-            dst_ref=(left, above, corner)[i],
-            send_sem=send_sem.at[i],
-            recv_sem=recv_sem.at[i],
-            device_id=({"fx": nxt}, {"fy": down}, {"fy": down, "fx": nxt})[i],
-            device_id_type=pl.DeviceIdType.MESH,
-        )
-
-    for i in range(3):
-        spill_copy(i).start()
-    for i in range(3):
-        spill_copy(i).wait()
+    copies.append(spill_copy(to_below, above, {"fy": down}, PACKS + 1))
+    copies[-1].start()
+    for copy in copies:
+        copy.wait()
 
 
 def add_kernel(cells, left, above, corner, out):
-    for h in range(2):
-
-        channel = 2 * pl.program_id(0) + h
+    for h in range(4):
+
+        channel = 4 * pl.program_id(0) + h
 
         def columns(packed):
             values = packed[channel // 3].astype(F32)
@@ -752,8 +762,8 @@
             dma((n_fx,)),
             dma((2,)),
             dma((2,)),
-            dma((4,)),
-            dma((4,)),
+            dma((8,)),
+            dma((8,)),
         ],
         compiler_params=pltpu.CompilerParams(
             collective_id=0, has_side_effects=True, vmem_limit_bytes=58 * 1024 * 1024
@@ -789,9 +799,9 @@
             pltpu.VMEM((PACKS, SIDE, 128), BF),
             pltpu.VMEM((CH, HALO, SIDE), BF),
             pltpu.VMEM((PACKS, HALO, 128), BF),
-            dma((2,)),
-            dma((3,)),
-            dma((3,)),
+            dma((PACKS + 1,)),
+            dma((PACKS + 2,)),
+            dma((PACKS + 2,)),
         ],
         compiler_params=pltpu.CompilerParams(
             collective_id=1, has_side_effects=True, vmem_limit_bytes=58 * 1024 * 1024
@@ -800,14 +810,14 @@
     return pl.pallas_call(
         add_kernel,
         out_shape=jax.ShapeDtypeStruct((CH, SIDE, SIDE), F32),
-        grid=(CH // 2,),
+        grid=(CH // 4,),
         in_specs=[
-            pl.BlockSpec((2, SIDE, SIDE), lambda p: (p, 0, 0)),
+            pl.BlockSpec((4, SIDE, SIDE), lambda p: (p, 0, 0)),
             pl.BlockSpec((PACKS, SIDE, 128), lambda p: (0, 0, 0)),
-            pl.BlockSpec((2, HALO, SIDE), lambda p: (p, 0, 0)),
+            pl.BlockSpec((4, HALO, SIDE), lambda p: (p, 0, 0)),
             pl.BlockSpec((PACKS, HALO, 128), lambda p: (0, 0, 0)),
         ],
-        out_specs=pl.BlockSpec((2, SIDE, SIDE), lambda p: (p, 0, 0)),
+        out_specs=pl.BlockSpec((4, SIDE, SIDE), lambda p: (p, 0, 0)),
         compiler_params=pltpu.CompilerParams(vmem_limit_bytes=16 * 1024 * 1024),
     )(cells, left, above, corner)
 

time: 109 us -> 109 us (level)
  no operation moved by 1% of the time
where the time goes in v15:
time: 109 us
  Pallas kernels  79.8 us (73%)
  matrix products  29.2 us (27%)
    pallas_call x1, Pallas kernels, per_device(): pl.pallas_call(functools.partial(exchange_kernel, n_fy, n_fx), out_shape=...  66.6 us
    dot_general x1, matrix products, per_device(): jnp.einsum('bcyx,bkx->bcyk', row_sec, columns, preferred_element_type=F32)  16.9 us
    dot_general x1, matrix products, per_device(): jnp.einsum('bcyk,bkx->cyx', row_sec, made['spread'], preferred_element_ty...  12.3 us
    pallas_call x1, Pallas kernels, per_device(): pl.pallas_call(functools.partial(spill_kernel, n_fy, n_fx), out_shape=(pl...  11.4 us

profile of v15, /device:TPU:1, one launch (start us, length us, event | category | flops | bytes accessed | tf_op | source)
XLA Modules:
  0.0 109.0 jit_solution(12875125820188243693)
XLA Ops:
  0.0 66.6 %shard_map.118 = bf16[8,304,384]{2,1,0:T(8,128)(2,1)S(1)} custom-call(s32[16]{0:T(128)} %bitcast.29, s32[16]{0:T(128)} %chan_ref.1, s32[16]{0:T(128)} %count_ref.1, bf16[512,512]{1,0:T(8,128)(2,1)} %constant.15.clone.fourier_hbm, bf16[256,512]{1,0:T(8,128)(2,1)} %constant.16.clone.back_hbm, bf16[256,256]{1,0:T(8,128)(2,1)} %constant.17.clone.excess_hbm, ...), custom_call_target="tpu_custom_call" | custom-call | tf_op jit(solution)/shard_map/pallas_call | solution.py:734
  66.6 0.0 copy-start.1
  66.6 16.9 %fusion.2 = bf16[8,8,256,256]{3,2,1,0:T(8,128)(2,1)} fusion(bf16[8,8,256,256]{3,2,1,0:T(8,128)(2,1)} %param.17, bf16[8,256,384,1]{2,1,3,0:T(8,128)(2,1)} %constant.23, bf16[8,256,304,1]{2,1,3,0:T(8,128)(2,1)} %constant.22, bf16[8,304,384]{2,1,0:T(8,128)(2,1)S(1)} %shard_map.118), kind=kOutput, calls=%fused_computation.4 | convolution fusion | flops 7077888000 | bytes 21463040 | tf_op jit(solution)/shard_map/bcyx,bkx->bcyk/dot_general | solution.py:783
  83.5 0.0 copy-done.1
  83.5 12.3 %fusion.19.cells = f32[8,304,384]{2,1,0:T(8,128)} fusion(bf16[8,256,384,1]{2,1,0,3:T(8,128)(2,1)S(1)} %copy-done.1, bf16[8,256,304,1]{2,1,0,3:T(8,128)(2,1)} %constant.24, bf16[8,8,256,256]{3,2,1,0:T(8,128)(2,1)} %fusion.2), kind=kOutput, calls=%fused_computation.14 | convolution fusion | flops 6380322816 | bytes 14942208 | tf_op jit(solution)/shard_map/bcyk,bkx->cyx/dot_general | solution.py:787
  95.8 0.0 copy-start
  95.8 11.4 %shard_map.119 = (bf16[3,256,128]{2,1,0:T(8,128)(2,1)S(1)}, bf16[8,48,256]{2,1,0:T(8,128)(2,1)S(1)}, bf16[3,48,128]{2,1,0:T(8,128)(2,1)S(1)}) custom-call(f32[8,304,384]{2,1,0:T(8,128)} %fusion.19.cells), custom_call_target="tpu_custom_call" | custom-call | tf_op jit(solution)/shard_map/pallas_call | solution.py:788
  107.2 0.0 copy-done
  107.2 1.8 %shard_map.120 = f32[8,256,256]{2,1,0:T(8,128)} custom-call(f32[8,304,384]{2,1,0:T(8,128)S(1)} %copy-done, bf16[3,256,128]{2,1,0:T(8,128)(2,1)S(1)} %get-tuple-element.8.left, bf16[8,48,256]{2,1,0:T(8,128)(2,1)S(1)} %get-tuple-element.9.above, bf16[3,48,128]{2,1,0:T(8,128)(2,1)S(1)} %get-tuple-element.10.corner), custom_call_target="tpu_custom_call" | custom-call | tf_op jit(solution)/shard_map/pallas_call | solution.py:810
Async XLA Ops:
  66.6 16.9 %copy-start.1 = (bf16[8,256,384,1]{2,1,0,3:T(8,128)(2,1)S(1)}, bf16[8,256,384,1]{2,1,0,3:T(8,128)(2,1)}, u32[]{:S(2)}) copy-start(bf16[8,256,384,1]{2,1,0,3:T(8,128)(2,1)} %constant.25) | copy-start | bytes 4718596
  95.8 11.4 %copy-start = (f32[8,304,384]{2,1,0:T(8,128)S(1)}, f32[8,304,384]{2,1,0:T(8,128)}, u32[]{:S(2)}) copy-start(f32[8,304,384]{2,1,0:T(8,128)} %fusion.19.cells) | copy-start | bytes 11206660

commit v16 on v15

--- a/solution.py
+++ b/solution.py
@@ -780,6 +780,7 @@
     )
     rows, columns = made["rows"], made["columns"]
     row_sec = jnp.einsum("bkn,cnx->bckx", rows, extended, preferred_element_type=F32).astype(BF)
+    row_sec = lax.optimization_barrier(row_sec)
     coefficient = jnp.einsum("bcyx,bkx->bcyk", row_sec, columns, preferred_element_type=F32)
     limits = thresholds.astype(F32)
     shrunk = (coefficient - jnp.clip(coefficient, -limits, limits)).astype(BF)

time: 109 us -> 113 us (1.037)
  matrix products: 29.2 us -> 33.2 us
    dot_general x0 -> x1, matrix products: none -> 9.44 us  [per_device(): jnp.einsum('bkn,cnx->bckx', rows, extended, preferred_element_type=F32)]
    dot_general x1, matrix products: 16.9 us -> 11.9 us  [per_device(): jnp.einsum('bcyx,bkx->bcyk', row_sec, columns, preferred_element_type=F32)]
where the time goes in v16:
time: 113 us
  Pallas kernels  79.9 us (71%)
  matrix products  33.2 us (29%)
    pallas_call x1, Pallas kernels, per_device(): pl.pallas_call(functools.partial(exchange_kernel, n_fy, n_fx), out_shape=...  66.7 us
    dot_general x1, matrix products, per_device(): jnp.einsum('bcyx,bkx->bcyk', row_sec, columns, preferred_element_type=F32)  11.9 us
    dot_general x1, matrix products, per_device(): jnp.einsum('bcyk,bkx->cyx', row_sec, made['spread'], preferred_element_ty...  11.8 us
    pallas_call x1, Pallas kernels, per_device(): pl.pallas_call(functools.partial(spill_kernel, n_fy, n_fx), out_shape=(pl...  11.4 us
    dot_general x1, matrix products, per_device(): jnp.einsum('bkn,cnx->bckx', rows, extended, preferred_element_type=F32)  9.44 us

profile of v16, /device:TPU:1, one launch (start us, length us, event | category | flops | bytes accessed | tf_op | source)
XLA Modules:
  0.0 113.1 jit_solution(12379793226456215658)
XLA Ops:
  0.0 0.0 copy-start.4
  0.0 66.7 %shard_map.118 = bf16[8,304,384]{2,1,0:T(8,128)(2,1)S(1)} custom-call(s32[16]{0:T(128)} %bitcast.26, s32[16]{0:T(128)} %chan_ref.1, s32[16]{0:T(128)} %count_ref.1, bf16[512,512]{1,0:T(8,128)(2,1)} %constant.15.clone.fourier_hbm, bf16[256,512]{1,0:T(8,128)(2,1)} %constant.16.clone.back_hbm, bf16[256,256]{1,0:T(8,128)(2,1)} %constant.17.clone.excess_hbm, ...), custom_call_target="tpu_custom_call" | custom-call | tf_op jit(solution)/shard_map/pallas_call | solution.py:734
  66.7 0.0 copy-done.4
  66.7 0.0 copy-start.3
  66.7 9.4 %convert_bitcast_fusion = bf16[8,8,256,384]{3,2,1,0:T(8,128)(2,1)} fusion(bf16[8,256,304,1]{2,1,3,0:T(8,128)(2,1)S(1)} %copy-done.4, bf16[8,304,384]{2,1,0:T(8,128)(2,1)S(1)} %shard_map.118), kind=kOutput, calls=%fused_computation.5 | convolution fusion | flops 3831496704 | bytes 15695872 | tf_op jit(solution)/shard_map/bkn,cnx->bckx/dot_general | solution.py:782
  76.2 0.0 copy-done.3
  76.2 0.0 copy-start.1
  76.2 0.0 copy-start.2
  76.2 11.9 %fusion.2 = bf16[8,8,256,256]{3,2,1,0:T(8,128)(2,1)} fusion(bf16[8,8,256,256]{3,2,1,0:T(8,128)(2,1)} %param.17, bf16[8,8,256,384]{3,2,1,0:T(8,128)(2,1)} %convert_bitcast_fusion, bf16[8,256,384,1]{2,1,3,0:T(8,128)(2,1)S(1)} %copy-done.3), kind=kOutput, calls=%fused_computation.4 | convolution fusion | flops 3246391296 | bytes 30932992 | tf_op jit(solution)/shard_map/bcyx,bkx->bcyk/dot_general | solution.py:784
  88.1 0.0 copy-done.1
  88.1 0.0 copy-done.2
  88.1 11.8 %fusion.12.cells = f32[8,304,384]{2,1,0:T(8,128)} fusion(bf16[8,256,384,1]{2,1,0,3:T(8,128)(2,1)S(1)} %copy-done.1, bf16[8,256,304,1]{2,1,0,3:T(8,128)(2,1)S(1)} %copy-done.2, bf16[8,8,256,256]{3,2,1,0:T(8,128)(2,1)} %fusion.2), kind=kOutput, calls=%fused_computation.11 | convolution fusion | flops 6380322816 | bytes 14942208 | tf_op jit(solution)/shard_map/bcyk,bkx->cyx/dot_general | solution.py:788
  99.9 0.0 copy-start
  99.9 11.4 %shard_map.119 = (bf16[3,256,128]{2,1,0:T(8,128)(2,1)S(1)}, bf16[8,48,256]{2,1,0:T(8,128)(2,1)S(1)}, bf16[3,48,128]{2,1,0:T(8,128)(2,1)S(1)}) custom-call(f32[8,304,384]{2,1,0:T(8,128)} %fusion.12.cells), custom_call_target="tpu_custom_call" | custom-call | tf_op jit(solution)/shard_map/pallas_call | solution.py:789
  111.3 0.0 copy-done
  111.3 1.8 %shard_map.120 = f32[8,256,256]{2,1,0:T(8,128)} custom-call(f32[8,304,384]{2,1,0:T(8,128)S(1)} %copy-done, bf16[3,256,128]{2,1,0:T(8,128)(2,1)S(1)} %get-tuple-element.8.left, bf16[8,48,256]{2,1,0:T(8,128)(2,1)S(1)} %get-tuple-element.9.above, bf16[3,48,128]{2,1,0:T(8,128)(2,1)S(1)} %get-tuple-element.10.corner), custom_call_target="tpu_custom_call" | custom-call | tf_op jit(solution)/shard_map/pallas_call | solution.py:811
Async XLA Ops:
  0.0 66.7 %copy-start.4 = (bf16[8,256,304,1]{2,1,3,0:T(8,128)(2,1)S(1)}, bf16[8,256,304,1]{2,1,3,0:T(8,128)(2,1)}, u32[]{:S(2)}) copy-start(bf16[8,256,304,1]{2,1,3,0:T(8,128)(2,1)} %constant.22) | copy-start | bytes 3735556
  66.7 9.5 %copy-start.3 = (bf16[8,256,384,1]{2,1,3,0:T(8,128)(2,1)S(1)}, bf16[8,256,384,1]{2,1,3,0:T(8,128)(2,1)}, u32[]{:S(2)}) copy-start(bf16[8,256,384,1]{2,1,3,0:T(8,128)(2,1)} %constant.23) | copy-start | bytes 4718596
  76.2 11.9 %copy-start.1 = (bf16[8,256,384,1]{2,1,0,3:T(8,128)(2,1)S(1)}, bf16[8,256,384,1]{2,1,0,3:T(8,128)(2,1)}, u32[]{:S(2)}) copy-start(bf16[8,256,384,1]{2,1,0,3:T(8,128)(2,1)} %constant.25) | copy-start | bytes 4718596
  76.2 11.9 %copy-start.2 = (bf16[8,256,304,1]{2,1,0,3:T(8,128)(2,1)S(1)}, bf16[8,256,304,1]{2,1,0,3:T(8,128)(2,1)}, u32[]{:S(2)}) copy-start(bf16[8,256,304,1]{2,1,0,3:T(8,128)(2,1)} %constant.24) | copy-start | bytes 3735556
  99.9 11.4 %copy-start = (f32[8,304,384]{2,1,0:T(8,128)S(1)}, f32[8,304,384]{2,1,0:T(8,128)}, u32[]{:S(2)}) copy-start(f32[8,304,384]{2,1,0:T(8,128)} %fusion.12.cells) | copy-start | bytes 11206660
